TPU v7x, 32 devices: a whole 2x2x4 slice. The times are simulated.
32 devices in a mesh: mp: 4 (over z), dp: 8 (over y, x, core).
Axes of the slice: x: 2, y: 2, z: 4, core: 2. Of those that a mesh axis runs over, the one named last changes fastest.
Arguments:
- volume: bfloat16 [8, 64, 64, 2048], P('dp', 'mp'), may hold values from -6 to 6
- kernel_a: bfloat16 [3, 3, 3, 32, 64], replicated, may hold values from -0.21875 to 0.21875
- kernel_b: bfloat16 [3, 3, 3, 64, 128], P(None, None, None, 'mp'), may hold values from -0.15625 to 0.15625
- cotangent: bfloat16 [8, 16, 16, 16, 128], P('dp', None, None, None, 'mp'), may hold values from -6 to 6
Outputs:
- features: bfloat16 [8, 16, 16, 16, 128], P('dp', None, None, None, 'mp')
- grad_a: float32 [3, 3, 3, 32, 64], replicated
- grad_b: float32 [3, 3, 3, 64, 128], P(None, None, None, 'mp')
All inputs are finite; a program needn't handle non-finite values.
Results may differ from a plain program's by a relative error of at most 0.0049.
Values may be sent and summed in bfloat16 or wider, within the bound.
No kernel may reach another device: no remote copies, remote signals or barrier semaphores. Data moves between devices by JAX's collectives and lax.ppermute only.
A program may use at most 192 MiB of HBM per device.

v0:
```python
import math

import jax
import jax.numpy as jnp
from jax import lax
from jax.sharding import PartitionSpec as P

GRID = 64


def shifted(array, axis, by):
    size = lax.axis_size(axis)
    pairs = [(i, i + by) for i in range(size) if 0 <= i + by < size]
    return lax.ppermute(array, axis, pairs)


def forward_conv(padded, kernel):
    return lax.conv_general_dilated(
        padded,
        kernel,
        (2, 2, 2),
        "VALID",
        dimension_numbers=("NDHWC", "DHWIO", "NDHWC"),
        preferred_element_type=jnp.float32,
    )


def kernel_grad(padded, grads):
    result = lax.conv_general_dilated(
        padded,
        grads,
        (1, 1, 1),
        "VALID",
        rhs_dilation=(2, 2, 2),
        dimension_numbers=("CDHWN", "IDHWO", "NDHWC"),
        preferred_element_type=jnp.float32,
    )
    return jnp.transpose(result, (1, 2, 3, 0, 4))


def input_grad(grads, kernel, first_low):
    flipped = kernel[::-1, ::-1, ::-1]
    return lax.conv_general_dilated(
        grads,
        flipped,
        (1, 1, 1),
        ((first_low, 2), (1, 2), (1, 2)),
        lhs_dilation=(2, 2, 2),
        dimension_numbers=("NDHWC", "DHWOI", "NDHWC"),
        preferred_element_type=jnp.float32,
    )


def pad_sides(field):
    return jnp.pad(field, ((0, 0), (0, 0), (1, 0), (1, 0), (0, 0)))


def pad_low(field):
    return jnp.pad(field, ((0, 0), (1, 0), (1, 0), (1, 0), (0, 0)))


def shards(volume, kernel_a, kernel_b, cotangent):
    samp_local = volume.shape[0]
    planes = volume.shape[1]
    edge = volume.shape[2]
    in_chan = kernel_a.shape[3]
    field = volume.reshape(samp_local, planes, edge, edge, in_chan)
    below = shifted(field[:, planes - 1 :], "mp", 1)
    padded_x = pad_sides(jnp.concatenate([below, field], axis=1))
    pre = forward_conv(padded_x, kernel_a)
    hidden = jnp.where(pre > 0, pre, 0.3 * pre).astype(jnp.bfloat16)
    grouped = lax.all_to_all(hidden, "mp", split_axis=4, concat_axis=1, tiled=True)
    padded_h = pad_low(grouped)
    partial_out = forward_conv(padded_h, kernel_b)
    features = lax.psum_scatter(partial_out, "mp", scatter_dimension=4, tiled=True).astype(
        jnp.bfloat16
    )
    upstream = lax.all_gather(cotangent, "mp", axis=4, tiled=True)
    local_b = kernel_grad(padded_h, upstream)
    back_group = input_grad(upstream, kernel_b, 1).astype(jnp.bfloat16)
    back = lax.all_to_all(back_group, "mp", split_axis=1, concat_axis=4, tiled=True)
    delta = (back.astype(jnp.float32) * jnp.where(pre > 0, 1.0, 0.3)).astype(jnp.bfloat16)
    local_a = kernel_grad(padded_x, delta)
    total_a = lax.psum(local_a, ("mp", "dp"))
    total_b = lax.psum(local_b, "dp")
    samples_all = samp_local * lax.axis_size("dp")
    grad_a = total_a / math.sqrt(samples_all * (GRID // 2) ** 3)
    grad_b = total_b / math.sqrt(samples_all * (GRID // 4) ** 3)
    return (features, grad_a, grad_b)


def solution(mesh):
    return jax.shard_map(
        shards,
        mesh=mesh,
        in_specs=(
            P("dp", "mp", None, None),
            P(),
            P(None, None, None, "mp", None),
            P("dp", None, None, None, "mp"),
        ),
        out_specs=(P("dp", None, None, None, "mp"), P(), P(None, None, None, "mp", None)),
        check_vma=False,
    )
```

profile of v0, /device:TPU:0, one launch (start us, length us, event | category | flops | bytes accessed | tf_op | source)
XLA Modules:
  0.0 911.5 jit_solution(3588795572059447607)
XLA Ops:
  7.2 8.5 copy.123
  15.8 1.1 slice.11
  16.8 1.1 copy.124
  17.9 5.0 collective-permute-start
  22.9 4.1 copy.139
  27.1 61.9 %copy.126 = bf16[1,16,64,64,32]{4,0,3,2,1:T(2,128)(2,1)} copy(bf16[1,16,64,64,32]{2,4,3,1,0:T(8,128)(2,1)} %bitcast.70) | data formatting | bytes 8388608 | tf_op jit(solution)/shard_map/reshape | solution.py:67
  89.0 2.7 copy.125
  91.6 109.1 %pad_maximum_fusion = bf16[1,17,64,64,32]{4,0,3,2,1:T(2,128)(2,1)} fusion(bf16[1,16,64,64,32]{4,0,3,2,1:T(2,128)(2,1)} %copy.126, bf16[1,1,64,64,32]{4,0,3,2,1:T(2,128)(2,1)S(1)} %copy.125), kind=kLoop, calls=%fused_computation.2 | loop fusion | flops 2228224 | bytes 8912896 | tf_op jit(solution)/shard_map/concatenate | solution.py:69
  200.7 62.3 %copy.127 = bf16[1,17,64,64,32]{3,4,2,1,0:T(8,128)(2,1)} copy(bf16[1,17,64,64,32]{4,0,3,2,1:T(2,128)(2,1)} %pad_maximum_fusion) | data formatting | bytes 8912896 | tf_op jit(solution)/shard_map/concatenate | solution.py:69
  263.0 16.6 %copy.158 = bf16[17,64,1,64,32]{1,4,3,0,2:T(8,128)(2,1)} copy(bf16[17,64,1,64,32]{3,4,2,1,0:T(8,128)(2,1)} %bitcast.71) | data formatting | bytes 8912896
  279.6 10.3 %pad.4.clone = bf16[17,64,1,80,32]{1,4,3,0,2:T(8,128)(2,1)} pad(bf16[17,64,1,64,32]{1,4,3,0,2:T(8,128)(2,1)} %copy.158, bf16[]{:T(256)} %constant.17), padding=0_0x0_0x0_0x1_15x0_0 | pad | bytes 10027010 | tf_op jit(solution)/shard_map/concatenate | solution.py:69
  289.9 27.5 %copy.130 = bf16[17,64,1,8,10,32]{5,3,4,1,0,2:T(8,128)(2,1)} copy(bf16[17,64,1,8,10,32]{1,5,4,3,0,2:T(8,128)(2,1)} %bitcast.66) | data formatting | bytes 11141120 | tf_op jit(solution)/shard_map/conv_general_dilated | solution.py:18
  317.4 3.6 slice.12
  321.0 20.3 %compare_select_fusion = (f32[8,32,8,5,64]{4,2,3,1,0:T(8,128)}, bf16[8,32,8,5,64]{4,2,3,1,0:T(8,128)(2,1)S(1)}) fusion(pred[8,5]{0,1:T(8,128)(4,1)S(1)} %copy-done.6, bf16[3,3,3,32,64]{4,3,2,1,0:T(8,128)(2,1)S(1)} %copy-done, bf16[17,64,1,7,2,32]{5,3,4,1,0,2:T(8,128)(2,1)S(1)} %slice.12, bf16[17,64,1,8,10,32]{5,3,4,1,0,2:T(8,128)(2,1)} %copy.130), kind=kOutput, calls=%fused_computation.18 | convolution fusion | flops 1144651776 | bytes 10588200 | tf_op jit(solution)/shard_map/conv_general_dilated | solution.py:18
  341.3 0.5 copy.131
  341.9 0.4 slice_bitcast_fusion.2
  342.2 6.9 copy.132
  349.1 6.4 reshape.71
  355.5 4.2 all-to-all-start
  359.8 3.4 copy.148
  363.2 2.4 slice.18
  365.6 7.0 copy.157
  372.5 10.0 %copy.140 = bf16[1,16,16,16,128]{4,3,2,1,0:T(8,128)(2,1)S(1)} copy(bf16[1,16,16,16,128]{3,2,1,0,4:T(8,128)(2,1)} %all-gather.2.cloned.1.call-done) | data formatting | bytes 2097152 | tf_op jit(solution)/shard_map/all_gather | solution.py:78
  382.5 0.3 copy.160
  382.8 0.3 pad.8.clone
  383.2 0.4 copy.143
  383.6 0.2 slice.16
  383.8 13.2 %fusion.17 = bf16[32,32,8,6,16]{4,2,3,1,0:T(8,128)(2,1)} fusion(bf16[3,3,3,16,128]{4,3,2,1,0:T(8,128)(2,1)S(1)} %copy-done.5, bf16[16,16,1,7,1,128]{5,3,4,1,0,2:T(8,128)(2,1)S(1)} %slice.16, bf16[16,16,1,8,3,128]{5,3,4,1,0,2:T(8,128)(2,1)S(1)} %copy.143), kind=kOutput, calls=%fused_computation.25 | convolution fusion | flops 657752064 | bytes 3715072 | tf_op jit(solution)/shard_map/conv_general_dilated | solution.py:43
  397.0 14.8 %copy.144 = bf16[32,32,8,6,16]{1,4,3,2,0:T(8,128)(2,1)} copy(bf16[32,32,8,6,16]{4,2,3,1,0:T(8,128)(2,1)} %fusion.17) | data formatting | bytes 3145728 | tf_op jit(solution)/shard_map/conv_general_dilated | solution.py:43
  411.9 4.5 select_convert_fusion
  416.4 2.7 fusion.34
  419.1 6.4 reshape.73
  425.5 13.5 %copy.153 = bf16[1,16,16,16,128]{4,0,3,2,1:T(2,128)(2,1)S(1)} copy(bf16[1,16,16,16,128]{3,2,1,0,4:T(8,128)(2,1)} %all-gather.2.cloned.1.call-done) | data formatting | bytes 2097152 | tf_op jit(solution)/shard_map/all_gather | solution.py:78
  439.0 5.1 all-to-all-start.1
  444.1 3.6 reshape.72
  447.7 9.0 copy.133
  456.7 5.4 copy.134
  462.1 7.1 copy.159
  469.2 6.4 pad.6.clone
  475.6 14.6 %copy.137 = bf16[32,32,1,8,6,16]{5,3,4,1,0,2:T(8,128)(2,1)} copy(bf16[32,32,1,8,6,16]{1,5,4,3,0,2:T(8,128)(2,1)} %bitcast.72) | data formatting | bytes 3145728 | tf_op jit(solution)/shard_map/conv_general_dilated | solution.py:18
  490.2 5.8 slice.14
  495.9 31.2 %copy.152 = bf16[1,32,32,32,16]{4,0,3,2,1:T(2,128)(2,1)} copy(bf16[1,32,32,32,16]{3,4,2,1,0:T(8,128)(2,1)} %bitcast.68) | data formatting | bytes 2097152 | tf_op jit(solution)/shard_map/all_to_all | solution.py:72
  527.2 52.7 %fusion.36 = f32[3,3,3,16,128]{4,3,2,1,0:T(8,128)} fusion(bf16[1,32,32,32,16]{4,0,3,2,1:T(2,128)(2,1)} %copy.152, bf16[1,16,16,16,128]{4,0,3,2,1:T(2,128)(2,1)S(1)} %copy.153), kind=kOutput, calls=%fused_computation.46 | convolution fusion | flops 425259008 | bytes 2318336 | tf_op jit(solution)/shard_map/transpose | solution.py:38
  579.9 12.4 %broadcast_select_fusion = f32[16,16,8,3,128]{4,2,3,1,0:T(8,128)S(1)} fusion(pred[8,3]{0,1:T(4,128)(4,1)S(1)} %copy-done.7, bf16[3,3,3,16,128]{4,3,2,1,0:T(8,128)(2,1)S(1)} %copy-done.5, bf16[32,32,1,7,2,16]{5,3,4,1,0,2:T(8,128)(2,1)} %slice.14, bf16[32,32,1,8,6,16]{5,3,4,1,0,2:T(8,128)(2,1)} %copy.137), kind=kOutput, calls=%fused_computation.31 | convolution fusion | flops 658538496 | bytes 5287960 | tf_op jit(solution)/shard_map/conv_general_dilated | solution.py:18
  592.3 2.2 copy.138
  594.5 0.0 all-reduce.3.cloned.1.call-start
  594.5 5.0 reshape.74
  599.5 7.2 copy.146
  606.7 3.2 convert_bitcast_fusion
  610.0 4.4 copy.147
  614.4 10.1 %fusion.12 = bf16[1,8,32,32,64]{3,4,2,1,0:T(8,128)(2,1)} fusion(f32[8,32,1,32,64]{3,4,1,0,2:T(8,128)} %copy.157, f32[1,8,32,32,4,16]{3,5,4,2,1,0:T(8,128)} %copy.147), kind=kLoop, calls=%fused_computation.16 | loop fusion | flops 1048576 | bytes 5242880 | tf_op jit(solution)/shard_map/convert_element_type | solution.py:82
  624.5 11.6 %copy.150 = bf16[1,8,32,32,64]{4,0,3,2,1:T(2,128)(2,1)} copy(bf16[1,8,32,32,64]{3,4,2,1,0:T(8,128)(2,1)} %fusion.12) | data formatting | bytes 2097152 | tf_op jit(solution)/shard_map/convert_element_type | solution.py:82
  636.1 88.0 %fusion.35 = f32[3,3,3,32,64]{4,3,2,1,0:T(8,128)} fusion(bf16[1,17,64,64,32]{4,0,3,2,1:T(2,128)(2,1)} %pad_maximum_fusion, bf16[1,8,32,32,64]{4,0,3,2,1:T(2,128)(2,1)} %copy.150), kind=kOutput, calls=%fused_computation.45 | convolution fusion | flops 887193600 | bytes 5726208 | tf_op jit(solution)/shard_map/transpose | solution.py:38
  724.1 0.0 reduce-scatter.4.cloned.1.call-start
  724.2 1.6 slice_bitcast_fusion.1
  725.7 14.5 %copy.155 = f32[1,16,16,16,128]{2,3,1,0,4:T(8,128)} copy(f32[1,16,16,16,128]{4,2,3,1,0:T(8,128)} %slice_bitcast_fusion.1) | data formatting | bytes 4194304
  740.3 15.3 %reshape.69 = f32[128,4096]{1,0:T(8,128)} reshape(f32[128,1,16,16,16]{4,3,2,1,0:T(8,128)} %bitcast.65) | data formatting | bytes 4194304
  755.6 1.7 broadcast_multiply_fusion.1
  757.3 94.3 %all-reduce.3.cloned.1.call-done = f32[3,3,3,32,64]{4,3,2,1,0:T(8,128)} async-done(((f32[3,3,3,32,64]{4,3,2,1,0:T(8,128)}), f32[3,3,3,32,64]{4,3,2,1,0:T(8,128)}) %all-reduce.3.cloned.1.call-update) | async-done | bytes 221200 | tf_op jit(solution)/shard_map/psum | solution.py:84
  851.5 1.8 broadcast_multiply_fusion
  853.4 45.2 %reduce-scatter.4.cloned.1.call-done = f32[32,4096]{1,0:T(8,128)} async-done(((f32[128,4096]{1,0:T(8,128)}), f32[32,4096]{1,0:T(8,128)}) %reduce-scatter.4.cloned.1.call-update) | async-done | bytes 524304
  898.6 2.6 reshape.70
  901.1 2.1 copy.156
  903.3 1.2 copy.154
  (27 shorter events, 0.2 us)
Async XLA Ops:
  7.2 313.9 %copy-start = (bf16[3,3,3,32,64]{4,3,2,1,0:T(8,128)(2,1)S(1)}, bf16[3,3,3,32,64]{4,3,2,1,0:T(8,128)(2,1)}, u32[]{:S(2)}) copy-start(bf16[3,3,3,32,64]{4,3,2,1,0:T(8,128)(2,1)} %param.5) | copy-start | bytes 331780
  7.2 15.7 %copy-start.3 = (bf16[1,16,16,16,32]{4,3,2,1,0:T(8,128)(2,1)S(1)}, bf16[1,16,16,16,32]{4,3,2,1,0:T(8,128)(2,1)}, u32[]{:S(2)}) copy-start(bf16[1,16,16,16,32]{4,3,2,1,0:T(8,128)(2,1)} %param.7) | copy-start | bytes 786436
  7.2 365.3 %all-gather.2.cloned.1.call-start = ((), (), s32[]{:S(2)}) async-start(), calls=%async_computation.3 | async-start | bytes 10485760 | tf_op jit(solution)/shard_map/all_gather | solution.py:78
  17.9 71.0 %collective-permute-start = (bf16[1,1,64,64,32]{3,4,2,1,0:T(8,128)(2,1)S(1)}, bf16[1,1,64,64,32]{3,4,2,1,0:T(8,128)(2,1)S(1)}, u32[]{:S(2)}, u32[]{:S(2)}) collective-permute-start(bf16[1,1,64,64,32]{3,4,2,1,0:T(8,128)(2,1)S(1)} %copy.124), channel_id=1, source_target_pairs={{0,8},{8,16},{16,24},{1,9},{9,17},{17,25},{2,10},{10,18},{18,26},{... | collective-permute-start | bytes 786440 | tf_op jit(solution)/shard_map/ppermute | solution.py:14
  317.4 3.6 copy-start.6
  355.5 83.5 %all-to-all-start = ((bf16[4,2,65536]{2,1,0:T(2,128)(2,1)}), bf16[4,2,65536]{2,1,0:T(2,128)(2,1)S(1)}, u32[]{:S(2)}, u32[]{:S(2)}) async-start(bf16[4,2,65536]{2,1,0:T(2,128)(2,1)} %reshape.71), calls=%async_computation | async-start | bytes 2097152 | tf_op jit(solution)/shard_map/all_to_all | solution.py:72
  382.5 1.2 copy-start.5
  397.0 14.9 %copy-start.4 = (pred[8,6]{1,0:T(8,128)(4,1)S(1)}, pred[8,6]{1,0:T(8,128)(4,1)}, u32[]{:S(2)}) copy-start(pred[8,6]{1,0:T(8,128)(4,1)} %constant.31) | copy-start | bytes 148
  439.0 155.5 %all-to-all-start.1 = ((bf16[4,2,65536]{2,1,0:T(2,128)(2,1)}), bf16[4,2,65536]{2,1,0:T(2,128)(2,1)}, u32[]{:S(2)}, u32[]{:S(2)}) async-start(bf16[4,2,65536]{2,1,0:T(2,128)(2,1)} %reshape.73), calls=%async_computation.1 | async-start | bytes 2097152 | tf_op jit(solution)/shard_map/all_to_all | solution.py:81
  444.1 311.5 %all-reduce.5.cloned.1.call-start = ((), (), s32[]{:S(2)}) async-start(), calls=%async_computation.5 | async-start | bytes 442368 | tf_op jit(solution)/shard_map/psum | solution.py:85
  527.2 52.7 %copy-start.7 = (pred[8,3]{0,1:T(4,128)(4,1)S(1)}, pred[8,3]{0,1:T(4,128)(4,1)}, u32[]{:S(2)}) copy-start(pred[8,3]{0,1:T(4,128)(4,1)} %constant.29) | copy-start | bytes 76
  594.5 257.1 %all-reduce.3.cloned.1.call-start = ((), (), s32[]{:S(2)}) async-start(), calls=%async_computation.4 | async-start | bytes 884736 | tf_op jit(solution)/shard_map/psum | solution.py:84
  636.1 88.1 %copy-start.2 = (f32[16,16,8,3,128]{4,1,3,2,0:T(8,128)S(1)}, f32[16,16,8,3,128]{4,1,3,2,0:T(8,128)}, u32[]{:S(2)}) copy-start(f32[16,16,8,3,128]{4,1,3,2,0:T(8,128)} %copy.138) | copy-start | bytes 9437188
  724.1 174.5 %reduce-scatter.4.cloned.1.call-start = ((), (), s32[]{:S(2)}) async-start(), calls=%async_computation.6 | async-start | bytes 2621440
  755.5 149.0 %copy-start.1 = (bf16[3,3,3,32,64]{4,3,2,1,0:T(8,128)(2,1)S(1)}, bf16[3,3,3,32,64]{4,3,2,1,0:T(8,128)(2,1)}, u32[]{:S(2)}) copy-start(bf16[3,3,3,32,64]{4,3,2,1,0:T(8,128)(2,1)} %param.5) | copy-start | bytes 331780
Sparse Core Ops, SparseCore 0:
  27.2 149.8 all-gather.1
  594.6 53.5 all-reduce.4
  724.2 127.2 all-reduce.2
  853.7 44.8 reduce-scatter.3
where the time goes:
time: 929 us; the launch traced here: 912 us
  local copies, waits for them, and re-layouts  426 us (46%)
  matrix products  187 us (20%)
  waiting for transfers between devices  140 us (15%)
  other arithmetic  130 us (14%)
  starting transfers between devices  14.4 us (2%)
  between operations  14.4 us (2%)
    transpose x2, matrix products, kernel_grad(): return jnp.transpose(result, (1, 2, 3, 0, 4))  141 us
    concatenate x1, other arithmetic, shards(): padded_x = pad_sides(jnp.concatenate([below, field], axis=1))  109 us
    unnamed x32, local copies, waits for them, and re-layouts  103 us
    psum x1, waiting for transfers between devices, shards(): total_a = lax.psum(local_a, ('mp', 'dp'))  94.3 us
    concatenate x2, local copies, waits for them, and re-layouts, shards(): padded_x = pad_sides(jnp.concatenate([below, field], axis=1))  72.6 us
    reshape x1, local copies, waits for them, and re-layouts, shards(): field = volume.reshape(samp_local, planes, edge, edge, in_chan)  61.9 us
    conv_general_dilated x6, local copies, waits for them, and re-layouts, forward_conv(): lax.conv_general_dilated(padded, kernel, (2, 2, 2), 'VALID', dimension_nu...  55.2 us
    all_to_all x4, local copies, waits for them, and re-layouts, shards(): lax.all_to_all(hidden, 'mp', split_axis=4, concat_axis=1, tiled=True)  52 us
  transfers between devices with their start and end apart: 7, of which 2 were waited for; matrix products, arithmetic and copies ran while one was open for 80% of the time, Pallas kernels for 0%

commit v1 on v0

v1 whole, which is shorter than its diff:
```python
import functools
import math

import jax
import jax.numpy as jnp
from jax import lax
from jax.experimental import pallas as pl
from jax.experimental.pallas import tpu as pltpu
from jax.sharding import PartitionSpec as P

GRID = 64
BF = jnp.bfloat16
F32 = jnp.float32
VMEM = pl.BlockSpec(memory_space=pltpu.VMEM)
TAPS = 27
PAIRS = 5
MIB = 1 << 20


def dot(a, b):
    return lax.dot_general(a, b, (((1,), (0,)), ((), ())), preferred_element_type=F32)


def dot_nt(a, b):
    return lax.dot_general(a, b, (((1,), (1,)), ((), ())), preferred_element_type=F32)


def iota(shape, dim):
    return lax.broadcasted_iota(jnp.int32, shape, dim)


def params(mib=48):
    return pltpu.CompilerParams(vmem_limit_bytes=mib * MIB)


def deinterleave(x):
    row = iota((80, 64), 0)
    col = iota((80, 64), 1)
    pick = (col == 4 * (row % 16) + row // 16 - 1).astype(F32).astype(BF)
    return dot(pick, x).astype(BF)


def store_plane(ref, plane, x):
    y = deinterleave(x)
    for slot in range(5):
        ref[plane, slot, 0:16, :] = jnp.zeros((16, 256), BF)
        for s in range(8):
            ref[plane, slot, 16 + 16 * s : 32 + 16 * s, :] = y[
                16 * slot : 16 * slot + 16, 256 * s : 256 * s + 256
            ]


def build_first(ka_ref, ta_ref):
    left = iota((32, 128), 1) < 64
    zero = jnp.zeros((32, 128), F32)
    for t in range(9):
        wide = []
        for c in range(3):
            k = ka_ref[t // 3, t % 3, c].astype(F32)
            wide.append(jnp.concatenate([k, k], axis=1))
        for half in range(2):
            for w in range(-4, 8):
                row = 384 * t + (32 * w if w >= 0 else 256 + 32 * (w + 4))
                c0 = w - 4 * half + 1
                c1 = c0 - 2
                l = wide[c0] if 0 <= c0 <= 2 else zero
                r = wide[c1] if 0 <= c1 <= 2 else zero
                ta_ref[row : row + 32, 128 * half : 128 * half + 128] = jnp.where(left, l, r).astype(BF)


def first_rows(plane, b):
    main = jnp.concatenate([plane(b, 16, 0, 256), plane(b + 2, 16, 0, 256)], axis=0)
    edge = jnp.concatenate([plane(b, 0, 128, 128), plane(b + 2, 0, 128, 128)], axis=0)
    return [main, edge]


def first_conv(planes, ta_ref):
    total = None
    for a in range(3):
        parts = []
        for b in range(3):
            parts += first_rows(planes[a], b)
        term = dot(jnp.concatenate(parts, axis=1), ta_ref[1152 * a : 1152 * a + 1152, :])
        total = term if total is None else total + term
    return total


def down_shift(x):
    moved = pltpu.roll(x, 1, 0)
    return jnp.where(iota(x.shape, 0) % 16 == 0, 0.0, moved)


def up_shift(x):
    moved = pltpu.roll(x, x.shape[0] - 1, 0)
    return jnp.where(iota(x.shape, 0) % 16 == 15, 0.0, moved)


def store_hidden(put, even, odd):
    put(0, down_shift(odd).astype(BF))
    put(1, even.astype(BF))
    put(2, odd.astype(BF))


def leaky(pre):
    return jnp.where(pre > 0, pre, 0.3 * pre)


def sub(ref, *lead):
    def read(slot, row, lane, width):
        return ref[(*lead, slot, slice(row, row + 128), slice(lane, lane + width))]

    return read


def first_kernel(vol_ref, ka_ref, vd_ref, h_ref, ta_ref, last_ref):
    step = pl.program_id(0)

    @pl.when(step == 0)
    def _():
        build_first(ka_ref, ta_ref)

    for k in range(2):
        store_plane(vd_ref, k, vol_ref[0, k])

    @pl.when(step > 0)
    def _():
        hid = leaky(first_conv([sub(last_ref), sub(vd_ref, 0), sub(vd_ref, 1)], ta_ref))

        def put(slot, x):
            h_ref[0, slot, 0:16, :] = jnp.zeros((16, 256), BF)
            h_ref[0, slot, 16:144, :] = x

        store_hidden(put, hid[0:128], hid[128:256])

    last_ref[...] = vd_ref[1]


def pack_kernel(n, cot_ref, out_ref):
    chan = cot_ref.shape[4]
    lanes = 128 // chan
    rows = 256 // lanes
    per = 16 // n
    row = iota((256, 256), 0)
    col = iota((256, 256), 1)
    source = (row % 16) * 16 + ((row % rows) // 16) * lanes + row // rows
    pick = (col == source).astype(F32).astype(BF)
    for p in range(16):
        y = dot(pick, cot_ref[0, p].reshape(256, chan))
        z = jnp.concatenate([y[rows * l : rows * l + rows] for l in range(lanes)], axis=1).astype(BF)
        t = p // per
        at = (p % per) * rows
        out_ref[t, at : at + rows, :] = z
        if p % per == 0 and t > 0:
            out_ref[t - 1, per * rows : per * rows + rows, :] = z
    out_ref[n - 1, per * rows : per * rows + rows, :] = jnp.zeros((rows, 128), BF)


def lane_order(n, inverse):
    size = n * 128
    chan = 128 // n
    row = iota((size, size), 0)
    col = iota((size, size), 1)
    if inverse:
        row, col = col, row
    target = ((row // chan) % n) * 128 + (row // 128) * chan + row % chan
    return (col == target).astype(F32).astype(BF)


def second_rows(hread, a, count):
    parts = []
    for b in range(3):
        parts.append(jnp.concatenate([hread(2 * p + a, b, 16, 0, 256) for p in range(count)], axis=0))
        parts.append(jnp.concatenate([hread(2 * p + a, b, 0, 128, 128) for p in range(count)], axis=0))
    return jnp.concatenate(parts, axis=1)


def hidden_reader(h_ref, h0_ref, hh_ref):
    def read(index, slot, row, lane, width):
        rows, cols = slice(row, row + 128), slice(lane, lane + width)
        if index == 0:
            return hh_ref[slot, rows, cols]
        if index == 1:
            return h0_ref[slot, rows, cols]
        return h_ref[index - 1, slot, rows, cols]

    return read


def grad_b_kernel(
    n, dp, halo_ref, ka_ref, vd_ref, h_ref, hrecv_ref, cot_ref, vdh_ref, h0_ref, hh_ref, c_ref, out_ref, ta_ref
):
    slab = 16 // n
    chan = 64 // n
    lanes = n
    rows = 256 // lanes
    build_first(ka_ref, ta_ref)
    x = halo_ref[...].reshape(64, 2048)
    y = deinterleave(x)
    for slot in range(5):
        vdh_ref[slot, 0:16, :] = jnp.zeros((16, 256), BF)
        for s in range(8):
            vdh_ref[slot, 16 + 16 * s : 32 + 16 * s, :] = y[16 * slot : 16 * slot + 16, 256 * s : 256 * s + 256]
    hid = leaky(first_conv([sub(vdh_ref), sub(vd_ref, 0), sub(vd_ref, 1)], ta_ref))

    def put_in(ref):
        def put(slot, v):
            ref[slot, 0:16, :] = jnp.zeros((16, 256), BF)
            ref[slot, 16:144, :] = v

        return put

    store_hidden(put_in(h0_ref), hid[0:128], hid[128:256])
    store_hidden(put_in(hh_ref), hrecv_ref[0].astype(F32), hrecv_ref[1].astype(F32))
    wide = jnp.concatenate([cot_ref[t] for t in range(n)], axis=1)
    turned = dot(wide, lane_order(n, False))
    mains = []
    for p in range(slab + 1):
        main = jnp.concatenate(
            [
                turned[
                    p * rows + 16 * (2 * s // lanes) : p * rows + 16 * (2 * s // lanes) + 16,
                    128 * (2 * s % lanes) : 128 * (2 * s % lanes) + 256,
                ]
                for s in range(8)
            ],
            axis=0,
        )
        mains.append(main)
        for slot, v in enumerate((main, up_shift(main))):
            c_ref[p, slot, 0:128, :] = v.astype(BF)
            c_ref[p, slot, 128:144, :] = jnp.zeros((16, 256), BF)
    turn = jnp.concatenate(mains[:slab], axis=0).T.astype(BF)
    read = hidden_reader(h_ref, h0_ref, hh_ref)
    per = 32 // dp
    out_ref[...] = jnp.zeros(out_ref.shape, BF)

    def put_tap(tap, v):
        v = v.astype(BF)
        for z in range(n):
            at = (tap % per) * chan
            out_ref[(tap // per) * n + z, at : at + chan, :] = v[z * chan : z * chan + chan]

    for a in range(3):
        g = dot(turn, second_rows(read, a, slab))
        for b in range(3):
            t = 3 * a + b
            l = 384 * b
            one = (g[0:128, l : l + 128] + g[128:256, l + 128 : l + 256]).T
            two = (g[0:128, l + 256 : l + 384] + g[128:256, l : l + 128]).T
            put_tap(3 * t, two[64:128])
            put_tap(3 * t + 1, one[0:64])
            put_tap(3 * t + 2, one[64:128])


def second_kernel(n, kb_ref, h_ref, h0_ref, hh_ref, c_ref, vd_ref, vdh_ref, feat_ref, out_ref, tb_ref, d_ref):
    slab = 16 // n
    planes = 2 * slab
    chan = 64 // n
    lanes = n
    rows = 256 // lanes
    blank = jnp.zeros((64, 128), BF)
    for t in range(9):
        taps = []
        for c in range(3):
            at = (3 * t + c) * chan
            taps.append(jnp.concatenate([kb_ref[z, at : at + chan, :] for z in range(n)], axis=0))
        for w in range(-2, 4):
            row = 384 * t + (64 * w if w >= 0 else 256 + 64 * (w + 2))
            for r in range(2):
                c = w - 2 * r + 1
                tb_ref[row : row + 64, 128 * r : 128 * r + 128] = taps[c] if 0 <= c <= 2 else blank
    read = hidden_reader(h_ref, h0_ref, hh_ref)
    total = None
    for a in range(3):
        term = dot(second_rows(read, a, slab), tb_ref[1152 * a : 1152 * a + 1152, :])
        total = term if total is None else total + term
    total = total.astype(BF)
    wide = []
    for p in range(slab):
        for m in range(16 // lanes):
            at = 128 * p + 16 * (m * lanes // 2)
            wide.append(
                jnp.concatenate([total[at + 16 * k : at + 16 * k + 16] for k in range(lanes // 2)], axis=1)
            )
    packed = dot(jnp.concatenate(wide, axis=0), lane_order(n, True)).astype(BF)
    for z in range(n):
        feat_ref[z] = packed[:, 128 * z : 128 * z + 128]
    for par in range(2):
        for hp in range(2):
            low, high = None, None
            for a in (1,) if par == 0 else (0, 2):
                for b in (1,) if hp == 0 else (0, 2):
                    t = 3 * a + b
                    up = 1 if a == 0 else 0
                    slot = 1 if b == 0 else 0
                    main = jnp.concatenate([c_ref[p + up, slot, 0:128, :] for p in range(slab)], axis=0)
                    edge = jnp.concatenate([c_ref[p + up, slot, 16:144, 0:128] for p in range(slab)], axis=0)
                    x = dot_nt(main, tb_ref[384 * t : 384 * t + 256, :])
                    e = dot_nt(edge, tb_ref[384 * t + 256 : 384 * t + 384, 0:128])
                    low = x[:, 0:128] if low is None else low + x[:, 0:128]
                    high = x[:, 128:256] + e if high is None else high + x[:, 128:256] + e
            back = jnp.concatenate([low, high], axis=1).astype(BF).astype(F32)
            for p in range(slab):
                u = 2 * p + par
                mask = read(u + 1, 1 + hp, 16, 0, 256).astype(F32) > 0
                v = back[128 * p : 128 * p + 128]
                at = 256 * u + 128 * hp
                d_ref[:, at : at + 128] = jnp.where(mask, v, 0.3 * v).astype(BF).astype(F32).T.astype(BF)
    left = iota((64, 128), 1) < 32
    pieces = []
    for a in range(3):
        for b in range(3):
            mains, edges = [], []
            for u in range(planes):
                src = sub(vdh_ref) if 2 * u + a == 0 else sub(vd_ref, 2 * u + a - 1)
                m, e = first_rows(src, b)
                mains.append(m)
                edges.append(e)
            x = jnp.concatenate([jnp.concatenate(mains, axis=0), jnp.concatenate(edges, axis=0)], axis=1)
            g = dot(d_ref[...], x)
            one = g[0:64, 256:384] + g[128:192, 0:128]
            two = g[0:64, 0:128] + g[128:192, 128:256]
            three = g[64:128, 0:128] + g[192:256, 128:256]
            pieces.append(
                jnp.where(left, pltpu.roll(one, 32, 1), pltpu.roll(two, 32, 1)) + pltpu.roll(three, 96, 1)
            )
    pieces.append(jnp.zeros((64, 128), F32))
    out_ref[...] = jnp.zeros(out_ref.shape, BF)
    for k in range(PAIRS):
        both = jnp.concatenate([pieces[2 * k], pieces[2 * k + 1]], axis=0).T.astype(BF)
        for j in range(6):
            out_ref[6 * k + j] = both[16 * j : 16 * j + 16]


def sum_kernel(scale, in_ref, out_ref):
    total = in_ref[0].astype(F32)
    for k in range(1, in_ref.shape[0]):
        total = total + in_ref[k].astype(F32)
    total = total * scale
    for k in range(out_ref.shape[0]):
        out_ref[k] = total


def unpack_kernel(n, in_ref, out_ref):
    chan = out_ref.shape[4]
    lanes = 128 // chan
    rows = 256 // lanes
    per = 16 // n
    row = iota((256, 256), 0)
    col = iota((256, 256), 1)
    source = (col % 16) * 16 + ((col % rows) // 16) * lanes + col // rows
    pick = (row == source).astype(F32).astype(BF)
    for p in range(16):
        z = in_ref[p // per, (p % per) * rows : (p % per) * rows + rows, :].astype(F32)
        x = jnp.concatenate([z[:, chan * l : chan * l + chan] for l in range(lanes)], axis=0).astype(BF)
        out_ref[0, p] = dot(pick, x).astype(BF).reshape(16, 16, chan)


def last_kernel(in_ref, out_ref):
    for k in range(PAIRS):
        for c in range(3):
            x = jnp.concatenate([in_ref[6 * k + 2 * c], in_ref[6 * k + 2 * c + 1]], axis=0)
            for j in range(2):
                t = 2 * k + j
                if t < 9:
                    out_ref[t // 3, t % 3, c] = x[:, 64 * j : 64 * j + 64]


def call(body, outs, ins, scratch=(), mib=48):
    return pl.pallas_call(
        body,
        out_shape=outs,
        in_specs=[VMEM] * ins,
        out_specs=[VMEM] * len(outs) if isinstance(outs, (list, tuple)) else VMEM,
        scratch_shapes=list(scratch),
        compiler_params=params(mib),
    )


def shards(volume, kernel_a, kernel_b, cotangent):
    n = lax.axis_size("mp")
    dp = lax.axis_size("dp")
    both = ("dp", "mp")
    planes = volume.shape[1]
    hplanes = planes // 2
    slab = hplanes // 2
    chan_b = kernel_b.shape[3]
    chan_o = cotangent.shape[4]
    rows = 256 // (128 // chan_o)
    shape = jax.ShapeDtypeStruct
    up = [(i, i + 1) for i in range(n - 1)]

    halo = lax.ppermute(volume[0, planes - 1], "mp", up)
    packed = call(functools.partial(pack_kernel, n), shape((n, (slab + 1) * rows, 128), BF), 1)(cotangent)
    cot = lax.all_to_all(packed, "mp", 0, 0, tiled=True)
    kb = kernel_b.reshape(1, TAPS * chan_b, 128)
    kb = lax.all_to_all(jnp.broadcast_to(kb, (n, TAPS * chan_b, 128)), "mp", 0, 0, tiled=True)

    vd, hidden = pl.pallas_call(
        first_kernel,
        grid=(hplanes,),
        out_shape=(shape((planes, 5, 144, 256), BF), shape((hplanes, 3, 144, 256), BF)),
        in_specs=[pl.BlockSpec((1, 2, 64, 2048), lambda i: (0, i, 0, 0)), VMEM],
        out_specs=(
            pl.BlockSpec((2, 5, 144, 256), lambda i: (i, 0, 0, 0)),
            pl.BlockSpec((1, 3, 144, 256), lambda i: (i, 0, 0, 0)),
        ),
        scratch_shapes=[pltpu.VMEM((3456, 256), BF), pltpu.VMEM((5, 144, 256), BF)],
        compiler_params=params(),
    )(volume, kernel_a)
    hrecv = lax.ppermute(hidden[hplanes - 1, 1:3, 16:144, :], "mp", up)

    per = 32 // dp
    vdh, h0, hh, c, gb = call(
        functools.partial(grad_b_kernel, n, dp),
        (
            shape((5, 144, 256), BF),
            shape((3, 144, 256), BF),
            shape((3, 144, 256), BF),
            shape((slab + 1, 2, 144, 256), BF),
            shape((dp * n, per * chan_b, 128), BF),
        ),
        6,
        [pltpu.VMEM((3456, 256), BF)],
    )(halo, kernel_a, vd[0:2], hidden, hrecv, cot)
    gb = lax.all_to_all(gb, both, 0, 0, tiled=True)

    feat, ga = call(
        functools.partial(second_kernel, n),
        (shape((n, slab * rows, 128), BF), shape((dp * n, 16, 128), BF)),
        7,
        [pltpu.VMEM((3456, 256), BF), pltpu.VMEM((256, hplanes * 256), BF)],
    )(kb, hidden, h0, hh, c, vd, vdh)
    feat = lax.all_to_all(feat, "mp", 0, 0, tiled=True)
    ga = lax.all_to_all(ga, both, 0, 0, tiled=True)

    samples = volume.shape[0] * dp
    gb = call(
        functools.partial(sum_kernel, 1 / math.sqrt(samples * (GRID // 4) ** 3)),
        shape((dp, per * chan_b, 128), F32),
        1,
    )(gb)
    gb = lax.all_to_all(gb, "dp", 0, 0, tiled=True)
    ga = call(
        functools.partial(sum_kernel, 1 / math.sqrt(samples * (GRID // 2) ** 3)),
        shape((dp * n, 16, 128), F32),
        1,
    )(ga)
    ga = lax.all_to_all(ga, both, 0, 0, tiled=True)

    features = call(functools.partial(unpack_kernel, n), shape((1, 16, 16, 16, chan_o), BF), 1)(feat)
    grad_b = gb.reshape(32, chan_b, 128)[:TAPS].reshape(3, 3, 3, chan_b, 128)
    grad_a = call(last_kernel, shape((3, 3, 3, 32, 64), F32), 1)(ga)
    return (features, grad_a, grad_b)


def solution(mesh):
    return jax.shard_map(
        shards,
        mesh=mesh,
        in_specs=(
            P("dp", "mp", None, None),
            P(),
            P(None, None, None, "mp", None),
            P("dp", None, None, None, "mp"),
        ),
        out_specs=(P("dp", None, None, None, "mp"), P(), P(None, None, None, "mp", None)),
        check_vma=False,
    )
```

time: 929 us -> 133 us (0.14); the launches traced: 912 us -> 133 us
  local copies, waits for them, and re-layouts: 426 us -> 13.1 us
  matrix products: 187 us -> 0 us
  other arithmetic: 130 us -> 0 us
  waiting for transfers between devices: 140 us -> 28.4 us
  blocking collectives: 0 us -> 41.1 us
  Pallas kernels: 0 us -> 28.3 us
  between operations: 14.4 us -> 0.74 us
    transpose x2 -> x0, matrix products: 141 us -> none  [kernel_grad(): return jnp.transpose(result, (1, 2, 3, 0, 4))]
    concatenate x1 -> x0, other arithmetic: 109 us -> none  [shards(): padded_x = pad_sides(jnp.concatenate([below, field], axis=1))]
    unnamed x32 -> x16, local copies, waits for them, and re-layouts: 103 us -> 8.49 us
    psum x2 -> x0, waiting for transfers between devices: 94.3 us -> none  [the longest x1 94.3 us: shards(): total_a = lax.psum(local_a, ('mp', 'dp'))]
    concatenate x2 -> x0, local copies, waits for them, and re-layouts: 72.6 us -> none  [shards(): padded_x = pad_sides(jnp.concatenate([below, field], axis=1))]
    conv_general_dilated x9 -> x0, local copies, waits for them, and re-layouts: 70.6 us -> none  [the longest x6 55.2 us: forward_conv(): lax.conv_general_dilated(padded, kernel, (2, 2, 2), 'VALID', dimension_nu...]
    reshape x1 -> x0, local copies, waits for them, and re-layouts: 61.9 us -> none  [shards(): field = volume.reshape(samp_local, planes, edge, edge, in_chan)]
    all_to_all x5 -> x0, local copies, waits for them, and re-layouts: 59.2 us -> none  [the longest x4 52 us: shards(): lax.all_to_all(hidden, 'mp', split_axis=4, concat_axis=1, tiled=True)]
  transfers between devices with their start and end apart: 7 -> 6, of which waited for: 2 -> 4; matrix products, arithmetic and copies ran while one was open for 80% -> 2% of each run, Pallas kernels for 0% -> 12%
where the time goes in v1:
time: 133 us
  blocking collectives  41.1 us (31%)
  waiting for transfers between devices  28.4 us (21%)
  Pallas kernels  28.3 us (21%)
  starting transfers between devices  21 us (16%)
  local copies, waits for them, and re-layouts  13.1 us (10%)
    all_to_all x1, blocking collectives, shards(): cot = lax.all_to_all(packed, 'mp', 0, 0, tiled=True)  16.4 us
    all_to_all x1, blocking collectives, shards(): ga = lax.all_to_all(ga, both, 0, 0, tiled=True)  13.8 us
    all_to_all x1, waiting for transfers between devices, shards(): gb = lax.all_to_all(gb, both, 0, 0, tiled=True)  13.6 us
    pallas_call x1, Pallas kernels, shards(): call(functools.partial(second_kernel, n), (shape((n, slab * rows, 128), B...  12.2 us
    all_to_all x1, blocking collectives, shards(): feat = lax.all_to_all(feat, 'mp', 0, 0, tiled=True)  10.9 us
    all_to_all x1, waiting for transfers between devices, shards(): ga = lax.all_to_all(ga, both, 0, 0, tiled=True)  9.41 us
    pallas_call x1, Pallas kernels, shards(): pl.pallas_call(first_kernel, grid=(hplanes,), out_shape=(shape((planes, 5...  8.68 us
    unnamed x16, local copies, waits for them, and re-layouts  8.49 us
  transfers between devices with their start and end apart: 6, of which 4 were waited for; matrix products, arithmetic and copies ran while one was open for 2% of the time, Pallas kernels for 12%

profile of v1, /device:TPU:0, one launch (start us, length us, event | category | flops | bytes accessed | tf_op | source)
XLA Modules:
  0.0 132.5 jit_solution(10725983722261302787)
XLA Ops:
  0.6 0.0 copy-start.1
  0.6 1.2 copy-done.1
  1.9 0.8 shard_map.68
  2.6 16.4 %all_to_all.35.cot_ref = bf16[4,320,128]{2,1,0:T(8,128)(2,1)S(1)} all-to-all(bf16[4,320,128]{2,1,0:T(8,128)(2,1)S(1)} %shard_map.68), channel_id=1, replica_groups=mesh['mp'=4,'dp'=8] {'mp'}, dimensions={0} | all-to-all | bytes 655360 | tf_op jit(solution)/shard_map/all_to_all | solution.py:395
  19.0 1.7 %broadcast_in_dim.8 = bf16[4,432,128]{2,1,0:T(8,128)(2,1)} broadcast(bf16[432,128]{1,0:T(8,128)(2,1)} %bitcast.9), dimensions={1,2} | broadcast | bytes 552960 | tf_op jit(solution)/shard_map/broadcast_in_dim | solution.py:397
  20.7 3.5 %all-to-all-start = ((bf16[4,432,128]{2,1,0:T(8,128)(2,1)}), bf16[4,432,128]{2,1,0:T(8,128)(2,1)S(1)}, u32[]{:S(2)}, u32[]{:S(2)}) async-start(bf16[4,432,128]{2,1,0:T(8,128)(2,1)} %broadcast_in_dim.8), calls=%async_computation | async-start | bytes 884736 | tf_op jit(solution)/shard_map/all_to_all | solution.py:397
  24.2 1.0 slice_bitcast_fusion
  25.2 3.9 %collective-permute-start = (bf16[64,2048]{1,0:T(8,128)(2,1)S(1)}, bf16[64,2048]{1,0:T(8,128)(2,1)S(1)}, u32[]{:S(2)}, u32[]{:S(2)}) collective-permute-start(bf16[64,2048]{1,0:T(8,128)(2,1)S(1)} %slice_bitcast_fusion), channel_id=1, source_target_pairs={{0,8},{8,16},{16,24},{1,9},{9,17},{17,25},{2,10},{10,18},{18,26},{... | collective-permute-start | bytes 786440 | tf_op jit(solution)/shard_map/ppermute | solution.py:393
  29.1 0.0 copy-start
  29.1 2.2 %copy-done = bf16[1,16,64,2048]{3,2,1,0:T(8,128)(2,1)S(1)} copy-done((bf16[1,16,64,2048]{3,2,1,0:T(8,128)(2,1)S(1)}, bf16[1,16,64,2048]{3,2,1,0:T(8,128)(2,1)}, u32[]{:S(2)}) %copy-start) | copy-done | bytes 4194328
  31.3 0.0 copy-start.2
  31.3 0.9 copy-done.2
  32.2 8.7 %shard_map.67 = (bf16[16,5,144,256]{3,2,1,0:T(8,128)(2,1)}, bf16[8,3,144,256]{3,2,1,0:T(8,128)(2,1)S(1)}) custom-call(bf16[1,16,64,2048]{3,2,1,0:T(8,128)(2,1)S(1)} %copy-done, bf16[3,3,3,32,64]{4,3,2,1,0:T(8,128)(2,1)S(1)} %copy-done.2), custom_call_target="tpu_custom_call" | custom-call | tf_op jit(solution)/shard_map/pallas_call | solution.py:399
  40.9 3.6 %collective-permute-start.1 = (bf16[2,128,256]{2,1,0:T(8,128)(2,1)S(1)}, bf16[2,128,256]{2,1,0:T(8,128)(2,1)S(1)}, u32[]{:S(2)}, u32[]{:S(2)}) collective-permute-start(bf16[2,128,256]{2,1,0:T(8,128)(2,1)S(1)} %slice_bitcast_fusion.1), channel_id=1, source_target_pairs={{0,8},{8,16},{16,24},{1,9},{9,17},{17,25},{2,10},{10,18},{18,26},{... | collective-permute-start | bytes 393224 | tf_op jit(solution)/shard_map/ppermute | solution.py:411
  44.5 1.2 slice.13.vd_ref
  45.7 1.1 collective-permute-done.1.hrecv_ref
  46.8 0.0 collective-permute-done.halo_ref
  46.8 2.4 %shard_map.69 = (bf16[5,144,256]{2,1,0:T(8,128)(2,1)S(1)}, bf16[3,144,256]{2,1,0:T(8,128)(2,1)S(1)}, bf16[3,144,256]{2,1,0:T(8,128)(2,1)S(1)}, bf16[5,2,144,256]...) custom-call(bf16[64,2048]{1,0:T(8,128)(2,1)S(1)} %collective-permute-done.halo_ref, bf16[3,3,3,32,64]{4,3,2,1,0:T(8,128)(2,1)S(1)} %copy-done.2, ...), custom_call_target="tpu_custom_call" | custom-call | tf_op jit(solution)/shard_map/pallas_call | solution.py:414
  49.3 0.0 copy-start.3
  49.3 0.8 copy-done.3
  50.1 0.0 copy-start.4
  50.1 0.8 copy-done.4
  50.8 0.0 copy-start.6
  50.8 0.7 copy-done.6
  51.5 0.0 all-to-all-done.kb_ref
  51.5 0.0 copy-start.5
  51.5 1.0 copy-done.5
  52.5 0.0 copy-start.7
  52.5 0.9 copy-done.7
  53.4 12.2 %shard_map.70 = (bf16[4,256,128]{2,1,0:T(8,128)(2,1)S(1)}, bf16[32,16,128]{2,1,0:T(8,128)(2,1)S(1)}) custom-call(bf16[4,432,128]{2,1,0:T(8,128)(2,1)S(1)} %all-to-all-done.kb_ref, bf16[8,3,144,256]{3,2,1,0:T(8,128)(2,1)S(1)} %get-tuple-element.12.h_ref, bf16[3,144,256]{2,1,0:T(8,128)(2,1)S(1)} %get-tuple-element.14.h0_ref, ...), custom_call_target="tpu_custom_call" | custom-call | tf_op jit(solution)/shard_map/pallas_call | solution.py:428
  65.6 13.8 %all_to_all.36.in_ref = bf16[32,16,128]{2,1,0:T(8,128)(2,1)S(1)} all-to-all(bf16[32,16,128]{2,1,0:T(8,128)(2,1)S(1)} %get-tuple-element.19), channel_id=1, replica_groups=mesh['mp'=4,'dp'=8] {'dp','mp'}, dimensions={0} | all-to-all | bytes 262144 | tf_op jit(solution)/shard_map/all_to_all | solution.py:435
  79.4 10.9 %all_to_all.37.in_ref = bf16[4,256,128]{2,1,0:T(8,128)(2,1)S(1)} all-to-all(bf16[4,256,128]{2,1,0:T(8,128)(2,1)S(1)} %get-tuple-element.18), channel_id=1, replica_groups=mesh['mp'=4,'dp'=8] {'mp'}, dimensions={0} | all-to-all | bytes 524288 | tf_op jit(solution)/shard_map/all_to_all | solution.py:434
  90.3 2.6 %all-to-all-start.5 = ((bf16[32,64,128]{2,1,0:T(8,128)(2,1)}), bf16[32,64,128]{2,1,0:T(8,128)(2,1)S(1)}, u32[]{:S(2)}, u32[]{:S(2)}) async-start(bf16[32,64,128]{2,1,0:T(8,128)(2,1)} %copy-done.3), calls=%async_computation.5 | async-start | bytes 1048576 | tf_op jit(solution)/shard_map/all_to_all | solution.py:426
  92.9 0.8 shard_map.72
  93.7 13.6 %all-to-all-done.5.in_ref = bf16[32,64,128]{2,1,0:T(8,128)(2,1)S(1)} async-done(((bf16[32,64,128]{2,1,0:T(8,128)(2,1)}), bf16[32,64,128]{2,1,0:T(8,128)(2,1)S(1)}, u32[]{:S(2)}, u32[]{:S(2)}) %all-to-all-start.5) | async-done | bytes 524320 | tf_op jit(solution)/shard_map/all_to_all | solution.py:426
  107.3 4.0 %all-to-all-start.4 = ((f32[32,16,128]{2,1,0:T(8,128)}), f32[32,16,128]{2,1,0:T(8,128)S(1)}, u32[]{:S(2)}, u32[]{:S(2)}) async-start(f32[32,16,128]{2,1,0:T(8,128)} %shard_map.72), calls=%async_computation.4 | async-start | bytes 524288 | tf_op jit(solution)/shard_map/all_to_all | solution.py:449
  111.3 0.8 shard_map.74
  112.1 9.4 %all-to-all-done.4.in_ref = f32[32,16,128]{2,1,0:T(8,128)S(1)} async-done(((f32[32,16,128]{2,1,0:T(8,128)}), f32[32,16,128]{2,1,0:T(8,128)S(1)}, u32[]{:S(2)}, u32[]{:S(2)}) %all-to-all-start.4) | async-done | bytes 262176 | tf_op jit(solution)/shard_map/all_to_all | solution.py:449
  121.5 3.4 %all-to-all-start.6 = ((f32[8,64,128]{2,1,0:T(8,128)}), f32[8,64,128]{2,1,0:T(8,128)S(1)}, u32[]{:S(2)}, u32[]{:S(2)}) async-start(f32[8,64,128]{2,1,0:T(8,128)} %shard_map.74), calls=%async_computation.6 | async-start | bytes 524288 | tf_op jit(solution)/shard_map/all_to_all | solution.py:443
  124.9 1.7 %shard_map.71 = bf16[1,16,16,16,32]{4,3,2,1,0:T(8,128)(2,1)} custom-call(bf16[4,256,128]{2,1,0:T(8,128)(2,1)S(1)} %all_to_all.37.in_ref), custom_call_target="tpu_custom_call" | custom-call | tf_op jit(solution)/shard_map/pallas_call | solution.py:451
  126.7 0.9 shard_map.73
  127.6 4.2 %all-to-all-done.6 = f32[8,64,128]{2,1,0:T(8,128)S(1)} async-done(((f32[8,64,128]{2,1,0:T(8,128)}), f32[8,64,128]{2,1,0:T(8,128)S(1)}, u32[]{:S(2)}, u32[]{:S(2)}) %all-to-all-start.6) | async-done | bytes 262176 | tf_op jit(solution)/shard_map/all_to_all | solution.py:443
  131.8 0.7 slice.16
  (1 shorter events, 0.0 us)
Async XLA Ops:
  0.6 1.2 copy-start.1
  20.7 30.8 %all-to-all-start = ((bf16[4,432,128]{2,1,0:T(8,128)(2,1)}), bf16[4,432,128]{2,1,0:T(8,128)(2,1)S(1)}, u32[]{:S(2)}, u32[]{:S(2)}) async-start(bf16[4,432,128]{2,1,0:T(8,128)(2,1)} %broadcast_in_dim.8), calls=%async_computation | async-start | bytes 884736 | tf_op jit(solution)/shard_map/all_to_all | solution.py:397
  25.2 21.6 %collective-permute-start = (bf16[64,2048]{1,0:T(8,128)(2,1)S(1)}, bf16[64,2048]{1,0:T(8,128)(2,1)S(1)}, u32[]{:S(2)}, u32[]{:S(2)}) collective-permute-start(bf16[64,2048]{1,0:T(8,128)(2,1)S(1)} %slice_bitcast_fusion), channel_id=1, source_target_pairs={{0,8},{8,16},{16,24},{1,9},{9,17},{17,25},{2,10},{10,18},{18,26},{... | collective-permute-start | bytes 786440 | tf_op jit(solution)/shard_map/ppermute | solution.py:393
  29.1 2.2 %copy-start = (bf16[1,16,64,2048]{3,2,1,0:T(8,128)(2,1)S(1)}, bf16[1,16,64,2048]{3,2,1,0:T(8,128)(2,1)}, u32[]{:S(2)}) copy-start(bf16[1,16,64,2048]{3,2,1,0:T(8,128)(2,1)} %vol_ref.1) | copy-start | bytes 12582916
  31.3 0.9 copy-start.2
  40.9 5.9 %collective-permute-start.1 = (bf16[2,128,256]{2,1,0:T(8,128)(2,1)S(1)}, bf16[2,128,256]{2,1,0:T(8,128)(2,1)S(1)}, u32[]{:S(2)}, u32[]{:S(2)}) collective-permute-start(bf16[2,128,256]{2,1,0:T(8,128)(2,1)S(1)} %slice_bitcast_fusion.1), channel_id=1, source_target_pairs={{0,8},{8,16},{16,24},{1,9},{9,17},{17,25},{2,10},{10,18},{18,26},{... | collective-permute-start | bytes 393224 | tf_op jit(solution)/shard_map/ppermute | solution.py:411
  49.3 0.8 copy-start.3
  50.1 0.8 copy-start.4
  50.8 0.7 copy-start.6
  51.5 1.0 copy-start.5
  52.5 0.9 copy-start.7
  90.3 17.0 %all-to-all-start.5 = ((bf16[32,64,128]{2,1,0:T(8,128)(2,1)}), bf16[32,64,128]{2,1,0:T(8,128)(2,1)S(1)}, u32[]{:S(2)}, u32[]{:S(2)}) async-start(bf16[32,64,128]{2,1,0:T(8,128)(2,1)} %copy-done.3), calls=%async_computation.5 | async-start | bytes 1048576 | tf_op jit(solution)/shard_map/all_to_all | solution.py:426
  107.3 14.3 %all-to-all-start.4 = ((f32[32,16,128]{2,1,0:T(8,128)}), f32[32,16,128]{2,1,0:T(8,128)S(1)}, u32[]{:S(2)}, u32[]{:S(2)}) async-start(f32[32,16,128]{2,1,0:T(8,128)} %shard_map.72), calls=%async_computation.4 | async-start | bytes 524288 | tf_op jit(solution)/shard_map/all_to_all | solution.py:449
  121.5 10.3 %all-to-all-start.6 = ((f32[8,64,128]{2,1,0:T(8,128)}), f32[8,64,128]{2,1,0:T(8,128)S(1)}, u32[]{:S(2)}, u32[]{:S(2)}) async-start(f32[8,64,128]{2,1,0:T(8,128)} %shard_map.74), calls=%async_computation.6 | async-start | bytes 524288 | tf_op jit(solution)/shard_map/all_to_all | solution.py:443

commit v2 on v1

v2 whole, which is shorter than its diff:
```python
import functools
import math

import jax
import jax.numpy as jnp
from jax import lax
from jax.experimental import pallas as pl
from jax.experimental.pallas import tpu as pltpu
from jax.sharding import PartitionSpec as P

GRID = 64
BF = jnp.bfloat16
F32 = jnp.float32
VMEM = pl.BlockSpec(memory_space=pltpu.VMEM)
TAPS = 27
HALF = 14
PAIRS = 5
MIB = 1 << 20


def dot(a, b):
    return lax.dot_general(a, b, (((1,), (0,)), ((), ())), preferred_element_type=F32)


def dot_nt(a, b):
    return lax.dot_general(a, b, (((1,), (1,)), ((), ())), preferred_element_type=F32)


def iota(shape, dim):
    return lax.broadcasted_iota(jnp.int32, shape, dim)


def params(mib):
    return pltpu.CompilerParams(vmem_limit_bytes=mib * MIB)


def cost(us):
    return pl.CostEstimate(flops=int(us * 1e9), bytes_accessed=int(us * 3e6), transcendentals=0)


def deinterleave(x, count):
    row = iota((80 * count, 64 * count), 0)
    col = iota((80 * count, 64 * count), 1)
    h = 4 * (row % 16) + row % 80 // 16 - 1
    pick = jnp.logical_and(h >= 0, col == row // 80 * 64 + h).astype(F32).astype(BF)
    return dot(pick, x).astype(BF)


def store_plane(ref, lead, y, row):
    for slot in range(5):
        ref[(*lead, slot, slice(0, 16))] = jnp.zeros((16, 256), BF)
        for s in range(8):
            at = row + 16 * slot
            ref[(*lead, slot, slice(16 + 16 * s, 32 + 16 * s))] = y[at : at + 16, 256 * s : 256 * s + 256]


def build_first(ka_ref, ta_ref, taps=9):
    left = iota((32, 128), 1) < 64
    zero = jnp.zeros((32, 128), F32)
    for t in range(taps):
        wide = []
        for c in range(3):
            k = ka_ref[t // 3, t % 3, c].astype(F32)
            wide.append(jnp.concatenate([k, k], axis=1))
        for half in range(2):
            for w in range(-4, 8):
                row = 384 * t + (32 * w if w >= 0 else 256 + 32 * (w + 4))
                c0 = w - 4 * half + 1
                c1 = c0 - 2
                l = wide[c0] if 0 <= c0 <= 2 else zero
                r = wide[c1] if 0 <= c1 <= 2 else zero
                ta_ref[row : row + 32, 128 * half : 128 * half + 128] = jnp.where(left, l, r).astype(BF)


def first_rows(plane, b):
    main = jnp.concatenate([plane(b, 16, 0, 256), plane(b + 2, 16, 0, 256)], axis=0)
    edge = jnp.concatenate([plane(b, 0, 128, 128), plane(b + 2, 0, 128, 128)], axis=0)
    return [main, edge]


def first_term(planes, a, ta_ref):
    parts = []
    for b in range(3):
        both = [first_rows(plane, b) for plane in planes]
        parts.append(jnp.concatenate([m for m, _ in both], axis=0))
        parts.append(jnp.concatenate([e for _, e in both], axis=0))
    return dot(jnp.concatenate(parts, axis=1), ta_ref[1152 * a : 1152 * a + 1152, :])


def down_shift(x):
    moved = pltpu.roll(x, 1, 0)
    return jnp.where(iota(x.shape, 0) % 16 == 0, 0.0, moved)


def up_shift(x):
    moved = pltpu.roll(x, x.shape[0] - 1, 0)
    return jnp.where(iota(x.shape, 0) % 16 == 15, 0.0, moved)


def store_hidden(put, even, odd):
    put(0, down_shift(odd).astype(BF))
    put(1, even.astype(BF))
    put(2, odd.astype(BF))


def leaky(pre):
    return jnp.where(pre > 0, pre, 0.3 * pre)


def sub(ref, *lead):
    def read(slot, row, lane, width):
        return ref[(*lead, slot, slice(row, row + 128), slice(lane, lane + width))]

    return read


def first_kernel(vol_ref, ka_ref, out_ref, hout_ref, pre_ref, x_ref, vd_ref, h_ref, ta_ref, sems, out_sems, h_sems):
    steps = x_ref.shape[0]

    def fetch(i):
        return pltpu.make_async_copy(vol_ref.at[0, pl.ds(4 * i, 4)], x_ref.at[i], sems.at[i])

    def flush(i):
        return pltpu.make_async_copy(
            vd_ref.at[pl.ds(4 * i + 1, 4)], out_ref.at[pl.ds(4 * i, 4)], out_sems.at[i]
        )

    def flush_hidden(i):
        return pltpu.make_async_copy(h_ref.at[pl.ds(2 * i, 2)], hout_ref.at[pl.ds(2 * i, 2)], h_sems.at[i])

    for i in range(steps):
        fetch(i).start()
    build_first(ka_ref, ta_ref)
    vd_ref[0] = jnp.zeros((5, 144, 256), BF)

    @pl.loop(0, steps)
    def _(i):
        fetch(i).wait()
        y = deinterleave(x_ref[i].reshape(256, 2048), 4)
        for k in range(4):
            store_plane(vd_ref, (4 * i + k + 1,), y, 80 * k)
        flush(i).start()
        total = None
        for a in range(3):
            term = first_term([sub(vd_ref, 4 * i + a), sub(vd_ref, 4 * i + a + 2)], a, ta_ref)
            total = term if total is None else total + term

        @pl.when(i == 0)
        def _():
            pre_ref[...] = total[0:256]

        hid = leaky(total)
        for k in range(2):

            def put(slot, x):
                h_ref[2 * i + k, slot, 0:16, :] = jnp.zeros((16, 256), BF)
                h_ref[2 * i + k, slot, 16:144, :] = x

            store_hidden(put, hid[256 * k : 256 * k + 128], hid[256 * k + 128 : 256 * k + 256])
        flush_hidden(i).start()

    for i in range(steps):
        flush(i).wait()
        flush_hidden(i).wait()


def core_of():
    return lax.axis_index("dp") % 2


def plane_kernel(vol_ref, out_ref, sem):
    copy = pltpu.make_async_copy(vol_ref.at[0, vol_ref.shape[1] - 1], out_ref, sem)
    copy.start()
    copy.wait()


def pack_kernel(n, cot_ref, kb_ref, after_ref, out_ref):
    del after_ref
    chan = cot_ref.shape[4]
    lanes = 128 // chan
    rows = 256 // lanes
    per = 16 // n
    row = iota((256, 256), 0)
    col = iota((256, 256), 1)
    source = (row % 16) * 16 + ((row % rows) // 16) * lanes + row // rows
    pick = (col == source).astype(F32).astype(BF)
    for p in range(16):
        y = dot(pick, cot_ref[0, p].reshape(256, chan))
        z = jnp.concatenate([y[rows * l : rows * l + rows] for l in range(lanes)], axis=1).astype(BF)
        t = p // per
        at = (p % per) * rows
        out_ref[t, at : at + rows, :] = z
        if p % per == 0 and t > 0:
            out_ref[t - 1, per * rows : per * rows + rows, :] = z
    out_ref[n - 1, per * rows : per * rows + rows, :] = jnp.zeros((rows, 128), BF)
    first = 13 * core_of()
    size = kb_ref.shape[1]
    for j in range(HALF):
        v = kb_ref[first + j]
        at = (per + 1) * rows + size * j
        for t in range(n):
            out_ref[t, at : at + size, :] = v


def lane_order(n, inverse):
    size = n * 128
    chan = 128 // n
    row = iota((size, size), 0)
    col = iota((size, size), 1)
    if inverse:
        row, col = col, row
    target = ((row // chan) % n) * 128 + (row // 128) * chan + row % chan
    return (col == target).astype(F32).astype(BF)


def second_rows(hread, a, count):
    planes = [2 * p + a - 1 for p in range(count + 1)][1 if a == 0 else 0 :][:count]
    parts = []
    for b in range(3):
        parts.append(jnp.concatenate([hread(u, b, 16, 0, 256) for u in planes], axis=0))
        parts.append(jnp.concatenate([hread(u, b, 0, 128, 128) for u in planes], axis=0))
    return jnp.concatenate(parts, axis=1)


def hidden_reader(h_ref, h0_ref):
    def read(index, slot, row, lane, width):
        rows, cols = slice(row, row + 128), slice(lane, lane + width)
        return h0_ref[slot, rows, cols] if index == 0 else h_ref[index, slot, rows, cols]

    return read


def put_in(ref):
    def put(slot, v):
        ref[slot, 0:16, :] = jnp.zeros((16, 256), BF)
        ref[slot, 16:144, :] = v

    return put


def put_half(keep_ref, send_ref, item, v):
    mine = core_of() == item % 2

    @pl.when(mine)
    def _():
        keep_ref[item // 2] = v

    @pl.when(jnp.logical_not(mine))
    def _():
        send_ref[item // 2] = v


def clear_from(count, keep_ref, send_ref):
    zero = jnp.zeros(keep_ref.shape[1:], F32)
    for item in range(count, 2 * keep_ref.shape[0]):
        put_half(keep_ref, send_ref, item, zero)


def grad_b_kernel(
    n, halo_ref, ka_ref, pre_ref, hin_ref, cot_ref, vdh_ref, h0_ref, c_ref, keep_ref, send_ref, ta_ref, h_ref, sem
):
    fetch = pltpu.make_async_copy(hin_ref, h_ref, sem)
    fetch.start()
    slab = 16 // n
    lanes = n
    rows = 256 // lanes
    build_first(ka_ref, ta_ref, 3)
    store_plane(vdh_ref, (), deinterleave(halo_ref[...], 1), 0)
    hid = leaky(pre_ref[...] + first_term([sub(vdh_ref)], 0, ta_ref))
    store_hidden(put_in(h0_ref), hid[0:128], hid[128:256])
    wide = jnp.concatenate([cot_ref[t, 0 : (slab + 1) * rows, :] for t in range(n)], axis=1)
    turned = dot(wide, lane_order(n, False))
    turns = []
    for p in range(slab + 1):
        main = jnp.concatenate(
            [
                turned[
                    p * rows + 16 * (2 * s // lanes) : p * rows + 16 * (2 * s // lanes) + 16,
                    128 * (2 * s % lanes) : 128 * (2 * s % lanes) + 256,
                ]
                for s in range(8)
            ],
            axis=0,
        )
        turns.append(main.T.astype(BF))
        for slot, v in enumerate((main, up_shift(main))):
            c_ref[p, slot, 0:128, :] = v.astype(BF)
            c_ref[p, slot, 128:144, :] = jnp.zeros((16, 256), BF)
    read = hidden_reader(h_ref, h0_ref)
    clear_from(TAPS, keep_ref, send_ref)
    fetch.wait()
    for a in range(3):
        first = 1 if a == 0 else 0
        turn = jnp.concatenate(turns[first : first + slab], axis=1)
        g = dot(turn, second_rows(read, a, slab))
        for b in range(3):
            t = 3 * a + b
            l = 384 * b
            one = (g[0:128, l : l + 128] + g[128:256, l + 128 : l + 256]).T
            two = (g[0:128, l + 256 : l + 384] + g[128:256, l : l + 128]).T
            put_half(keep_ref, send_ref, 3 * t, two[64:128])
            put_half(keep_ref, send_ref, 3 * t + 1, one[0:64])
            put_half(keep_ref, send_ref, 3 * t + 2, one[64:128])


def build_second(n, kb_ref, other_ref, tb_ref):
    chan = 64 // n
    start = (16 // n + 1) * (256 // n)
    blank = jnp.zeros((64, 128), BF)
    first = core_of() == 0

    def tap(k):
        j, own_first = (k, True) if k < 13 else (k - 13, False)
        parts = []
        for z in range(n):
            own = kb_ref[z, start + j * chan : start + j * chan + chan, :]
            other = other_ref[z, start + j * chan : start + j * chan + chan, :]
            pair = (own, other) if own_first else (other, own)
            parts.append(jnp.where(first, *pair))
        return jnp.concatenate(parts, axis=0)

    for t in range(9):
        taps = [tap(3 * t + c) for c in range(3)]
        for w in range(-2, 4):
            row = 384 * t + (64 * w if w >= 0 else 256 + 64 * (w + 2))
            for r in range(2):
                c = w - 2 * r + 1
                tb_ref[row : row + 64, 128 * r : 128 * r + 128] = taps[c] if 0 <= c <= 2 else blank


def grad_a_kernel(n, kb_ref, other_ref, h_ref, h0_ref, c_ref, vd_ref, vdh_ref, keep_ref, send_ref, tb_ref, d_ref):
    slab = 16 // n
    planes = 2 * slab
    build_second(n, kb_ref, other_ref, tb_ref)
    read = hidden_reader(h_ref, h0_ref)
    for par in range(2):
        for hp in range(2):
            low, high = None, None
            for a in (1,) if par == 0 else (0, 2):
                for b in (1,) if hp == 0 else (0, 2):
                    t = 3 * a + b
                    up = 1 if a == 0 else 0
                    slot = 1 if b == 0 else 0
                    main = jnp.concatenate([c_ref[p + up, slot, 0:128, :] for p in range(slab)], axis=0)
                    edge = jnp.concatenate([c_ref[p + up, slot, 16:144, 0:128] for p in range(slab)], axis=0)
                    x = dot_nt(main, tb_ref[384 * t : 384 * t + 256, :])
                    e = dot_nt(edge, tb_ref[384 * t + 256 : 384 * t + 384, 0:128])
                    low = x[:, 0:128] if low is None else low + x[:, 0:128]
                    high = x[:, 128:256] + e if high is None else high + x[:, 128:256] + e
            back = jnp.concatenate([low, high], axis=1).astype(BF).astype(F32)
            for p in range(slab):
                u = 2 * p + par
                mask = read(u, 1 + hp, 16, 0, 256).astype(F32) > 0
                v = back[128 * p : 128 * p + 128]
                at = 256 * u + 128 * hp
                d_ref[:, at : at + 128] = jnp.where(mask, v, 0.3 * v).astype(BF).astype(F32).T.astype(BF)
    left = iota((64, 128), 1) < 32
    pieces = []
    for a in range(3):
        for b in range(3):
            mains, edges = [], []
            for u in range(planes):
                src = sub(vdh_ref) if 2 * u + a == 0 else sub(vd_ref, 2 * u + a - 1)
                m, e = first_rows(src, b)
                mains.append(m)
                edges.append(e)
            x = jnp.concatenate([jnp.concatenate(mains, axis=0), jnp.concatenate(edges, axis=0)], axis=1)
            g = dot(d_ref[...], x)
            one = g[0:64, 256:384] + g[128:192, 0:128]
            two = g[0:64, 0:128] + g[128:192, 128:256]
            three = g[64:128, 0:128] + g[192:256, 128:256]
            pieces.append(
                jnp.where(left, pltpu.roll(one, 32, 1), pltpu.roll(two, 32, 1)) + pltpu.roll(three, 96, 1)
            )
    pieces.append(jnp.zeros((64, 128), F32))
    clear_from(6 * PAIRS, keep_ref, send_ref)
    for k in range(PAIRS):
        both = jnp.concatenate([pieces[2 * k], pieces[2 * k + 1]], axis=0).T
        for j in range(6):
            put_half(keep_ref, send_ref, 6 * k + j, both[16 * j : 16 * j + 16])


def features_kernel(n, kb_ref, other_ref, h_ref, h0_ref, *refs):
    outs, (piece_ref, tb_ref) = refs[:n], refs[n:]
    slab = 16 // n
    lanes = n
    build_second(n, kb_ref, other_ref, tb_ref)
    read = hidden_reader(h_ref, h0_ref)
    terms = [dot(second_rows(read, a, slab), tb_ref[1152 * a : 1152 * a + 1152, :]) for a in range(3)]
    local = terms[1] + terms[2]
    total = jnp.concatenate(
        [local[0:128], local[128:] + terms[0][: 128 * slab - 128], terms[0][128 * slab - 128 :]], axis=0
    ).astype(BF)
    wide = []
    for p in range(slab + 1):
        for m in range(16 // lanes):
            at = 128 * p + 16 * (m * lanes // 2)
            wide.append(
                jnp.concatenate([total[at + 16 * k : at + 16 * k + 16] for k in range(lanes // 2)], axis=1)
            )
    packed = dot(jnp.concatenate(wide, axis=0), lane_order(n, True)).astype(BF)
    for z in range(n):
        piece_ref[z] = packed[:, 128 * z : 128 * z + 128]
    me = lax.axis_index("mp")
    for d in range(n):
        outs[d][...] = piece_ref[(me + d) % n]


def pair_kernel(keep_b, got_b, keep_a, got_a, out_ref):
    out_ref[:, 0:64, :] = (keep_b[...] + got_b[...]).astype(BF)
    out_ref[:, 64:80, :] = (keep_a[...] + got_a[...]).astype(BF)


def sum_kernel(n, scale_a, scale_b, in_ref, out_ref):
    chan = 64 // n
    total = in_ref[0].astype(F32)
    for k in range(1, in_ref.shape[0]):
        total = total + in_ref[k].astype(F32)
    tap = total[0:64] * scale_b
    rest = total[64:80] * scale_a
    for g in range(out_ref.shape[0]):
        z = g % n
        out_ref[g, 0:chan, :] = tap[z * chan : z * chan + chan].astype(BF)
        out_ref[g, chan : chan + 16, :] = rest.astype(BF)


def unpack_kernel(n, *refs):
    ins, out_ref = refs[:n], refs[n]
    chan = out_ref.shape[4]
    lanes = 128 // chan
    rows = 256 // lanes
    per = 16 // n
    row = iota((256, 256), 0)
    col = iota((256, 256), 1)
    source = (col % 16) * 16 + ((col % rows) // 16) * lanes + col // rows
    pick = (row == source).astype(F32).astype(BF)
    me = lax.axis_index("mp")
    for d in range(n):
        first = (me + n - d) % n * per
        for p in range(per):
            z = ins[d][p * rows : p * rows + rows, :].astype(F32)
            if p == 0:
                more = ins[(d + 1) % n][per * rows : per * rows + rows, :].astype(F32)
                z = z + jnp.where(first > 0, more, 0.0)
            x = jnp.concatenate([z[:, chan * l : chan * l + chan] for l in range(lanes)], axis=0).astype(BF)
            out_ref[0, first + p] = dot(pick, x).astype(BF).reshape(16, 16, chan)


def last_kernel(mine_ref, other_ref, a_ref, b_ref):
    chan = b_ref.shape[1]
    first = core_of() == 0
    for j in range(15):
        x, y = mine_ref[j].astype(F32), other_ref[j].astype(F32)
        x, y = jnp.where(first, x, y), jnp.where(first, y, x)
        if 2 * j < TAPS:
            b_ref[2 * j] = x[0:chan]
        if 2 * j + 1 < TAPS:
            b_ref[2 * j + 1] = y[0:chan]
        v = jnp.concatenate([x[chan : chan + 16], y[chan : chan + 16]], axis=0)
        for half in range(2):
            t = 2 * (j // 3) + half
            if t < 9:
                a_ref[t // 3, t % 3, j % 3] = v[:, 64 * half : 64 * half + 64]


def call(body, outs, ins, us, scratch=(), mib=16):
    return pl.pallas_call(
        body,
        out_shape=outs,
        grid=(1,),
        in_specs=[VMEM] * ins if isinstance(ins, int) else ins,
        out_specs=[VMEM] * len(outs) if isinstance(outs, (list, tuple)) else VMEM,
        scratch_shapes=list(scratch),
        compiler_params=params(mib),
        cost_estimate=cost(us),
    )


def shards(volume, kernel_a, kernel_b, cotangent):
    n = lax.axis_size("mp")
    dp = lax.axis_size("dp")
    planes = volume.shape[1]
    hplanes = planes // 2
    slab = hplanes // 2
    chan_b = kernel_b.shape[3]
    chan_o = cotangent.shape[4]
    rows = 256 // (128 // chan_o)
    shape = jax.ShapeDtypeStruct
    up = [(i, i + 1) for i in range(n - 1)]
    swap = [(i, i ^ 1) for i in range(dp)]
    groups = [[(2 * k + c) * n + z for k in range(dp // 2) for z in range(n)] for c in range(2)]
    peers = dp * n // 2

    def exchange(x):
        return lax.all_to_all(x, ("dp", "mp"), 0, 0, tiled=True, axis_index_groups=groups)

    volume, cotangent, kernel_b = (
        pltpu.with_memory_space_constraint(x, pltpu.HBM) for x in (volume, cotangent, kernel_b.reshape(TAPS, chan_b, 128))
    )
    sent = (slab + 1) * rows + HALF * chan_b
    halo = pl.pallas_call(
        plane_kernel,
        out_shape=pltpu.VMEM((64, 2048), BF),
        in_specs=[pl.BlockSpec(memory_space=pltpu.HBM)],
        out_specs=VMEM,
        scratch_shapes=[pltpu.SemaphoreType.DMA],
        compiler_params=params(2),
        cost_estimate=cost(1),
    )(volume)
    packed = pl.pallas_call(
        functools.partial(pack_kernel, n),
        grid=(1,),
        out_shape=shape((n, sent, 128), BF),
        in_specs=[
            pl.BlockSpec(cotangent.shape, lambda i: (0, 0, 0, 0, 0)),
            pl.BlockSpec((TAPS, chan_b, 128), lambda i: (0, 0, 0)),
            pl.BlockSpec(memory_space=pl.ANY),
        ],
        out_specs=pl.BlockSpec((n, sent, 128), lambda i: (0, 0, 0)),
        compiler_params=params(8),
        cost_estimate=cost(2),
    )(cotangent, kernel_b, halo)
    halo = lax.ppermute(halo, "mp", up)
    cot = lax.all_to_all(packed, "mp", 0, 0, tiled=True)
    vd, hidden, pre = pl.pallas_call(
        first_kernel,
        out_shape=(
            pltpu.HBM((planes, 5, 144, 256), BF),
            pltpu.HBM((hplanes, 3, 144, 256), BF),
            pltpu.VMEM((256, 256), F32),
        ),
        in_specs=[pl.BlockSpec(memory_space=pltpu.HBM), VMEM],
        out_specs=(pl.BlockSpec(memory_space=pltpu.HBM), pl.BlockSpec(memory_space=pltpu.HBM), VMEM),
        scratch_shapes=[
            pltpu.VMEM((planes // 4, 4, 64, 2048), BF),
            pltpu.VMEM((planes + 1, 5, 144, 256), BF),
            pltpu.VMEM((hplanes, 3, 144, 256), BF),
            pltpu.VMEM((3456, 256), BF),
            pltpu.SemaphoreType.DMA((planes // 4,)),
            pltpu.SemaphoreType.DMA((planes // 4,)),
            pltpu.SemaphoreType.DMA((planes // 4,)),
        ],
        compiler_params=params(24),
        cost_estimate=cost(100),
    )(volume, kernel_a)
    cot, pre, halo = lax.optimization_barrier((cot, pre, halo))
    kb_other = lax.ppermute(cot, "dp", swap)

    vdh, h0, c, keep_b, send_b = call(
        functools.partial(grad_b_kernel, n),
        (
            pltpu.VMEM((5, 144, 256), BF),
            pltpu.VMEM((3, 144, 256), BF),
            pltpu.VMEM((slab + 1, 2, 144, 256), BF),
            pltpu.VMEM((peers, 64, 128), F32),
            pltpu.VMEM((peers, 64, 128), F32),
        ),
        [VMEM, VMEM, VMEM, pl.BlockSpec(memory_space=pltpu.HBM), VMEM],
        3,
        [pltpu.VMEM((1152, 256), BF), pltpu.VMEM((hplanes, 3, 144, 256), BF), pltpu.SemaphoreType.DMA],
        16,
    )(halo, kernel_a, pre, pltpu.with_memory_space_constraint(hidden, pltpu.HBM), cot)
    got_b = lax.ppermute(send_b, "dp", swap)

    keep_a, send_a = call(
        functools.partial(grad_a_kernel, n),
        (shape((peers, 16, 128), F32), shape((peers, 16, 128), F32)),
        7,
        8,
        [pltpu.VMEM((3456, 256), BF), pltpu.VMEM((256, hplanes * 256), BF)],
        24,
    )(cot, kb_other, hidden, h0, c, vd, vdh)
    got_a = lax.ppermute(send_a, "dp", swap)

    sums = call(pair_kernel, shape((peers, 80, 128), BF), 4, 1)(keep_b, got_b, keep_a, got_a)
    sums = exchange(sums)

    pieces = call(
        functools.partial(features_kernel, n),
        [shape(((slab + 1) * rows, 128), BF)] * n,
        4,
        4,
        [
            pltpu.VMEM((n, (slab + 1) * rows, 128), BF),
            pltpu.VMEM((3456, 256), BF),
        ],
    )(cot, kb_other, hidden, h0)
    sums, *pieces = lax.optimization_barrier((sums, *pieces))
    pieces = [pieces[0]] + [
        lax.ppermute(pieces[d], "mp", [(i, (i + d) % n) for i in range(n)]) for d in range(1, n)
    ]

    samples = volume.shape[0] * dp
    scale_a = 1 / math.sqrt(samples * (GRID // 2) ** 3)
    scale_b = 1 / math.sqrt(samples * (GRID // 4) ** 3)
    mine = call(
        functools.partial(sum_kernel, n, scale_a, scale_b), shape((peers, chan_b + 16, 128), BF), 1, 1
    )(sums)
    mine = exchange(mine)
    mine, *pieces = lax.optimization_barrier((mine, *pieces))
    other = lax.ppermute(mine, "dp", swap)

    features = call(functools.partial(unpack_kernel, n), shape((1, 16, 16, 16, chan_o), BF), n, 2)(*pieces)
    grad_a, grad_b = call(
        last_kernel, (shape((3, 3, 3, 32, 64), F32), shape((TAPS, chan_b, 128), F32)), 2, 1
    )(mine, other)
    return (features, grad_a, grad_b.reshape(3, 3, 3, chan_b, 128))


def solution(mesh):
    return jax.shard_map(
        shards,
        mesh=mesh,
        in_specs=(
            P("dp", "mp", None, None),
            P(),
            P(None, None, None, "mp", None),
            P("dp", None, None, None, "mp"),
        ),
        out_specs=(P("dp", None, None, None, "mp"), P(), P(None, None, None, "mp", None)),
        check_vma=False,
    )
```

time: 133 us -> 77.7 us (0.58)
  blocking collectives: 41.1 us -> 0 us
  local copies, waits for them, and re-layouts: 13.1 us -> 0.96 us
  waiting for transfers between devices: 28.4 us -> 22.4 us
  starting transfers between devices: 21 us -> 23.3 us
  Pallas kernels: 28.3 us -> 29.8 us
    all_to_all x3 -> x0, blocking collectives: 41.1 us -> none  [the longest x1 16.4 us: shards(): cot = lax.all_to_all(packed, 'mp', 0, 0, tiled=True)]
    all_to_all x4 -> x3, waiting for transfers between devices: 27.3 us -> 15.3 us  [the longest x2 9.6 us: exchange(): lax.all_to_all(x, ('dp', 'mp'), 0, 0, tiled=True, axis_index_groups=groups)]
    unnamed x16 -> x12, local copies, waits for them, and re-layouts: 8.49 us -> 0.96 us
    ppermute x2 -> x8, waiting for transfers between devices: 1.15 us -> 7.09 us  [the longest x3 5.77 us: shards(): lax.ppermute(pieces[d], 'mp', [(i, (i + d) % n) for i in range(n)])]
    ppermute x2 -> x8, starting transfers between devices: 7.45 us -> 11.3 us  [the longest x3 5.64 us: shards(): lax.ppermute(pieces[d], 'mp', [(i, (i + d) % n) for i in range(n)])]
    slice x2 -> x0, local copies, waits for them, and re-layouts: 1.86 us -> none  [the longest x1 1.16 us: shards(): vd[0:2]]
    broadcast_in_dim x1 -> x0, local copies, waits for them, and re-layouts: 1.72 us -> none  [shards(): jnp.broadcast_to(kb, (n, TAPS * chan_b, 128))]
    pallas_call x7 -> x9, Pallas kernels: 26.5 us -> 28 us  [the longest x1 9.23 us: shards(): pl.pallas_call(first_kernel, out_shape=(pltpu.HBM((planes, 5, 144, 256),...]
  transfers between devices with their start and end apart: 6 -> 11, of which waited for: 4 -> 6; matrix products, arithmetic and copies ran while one was open for 2% -> 0% of each run, Pallas kernels for 12% -> 34%
where the time goes in v2:
time: 77.7 us; the launch traced here: 77.2 us
  Pallas kernels  29.8 us (38%)
  starting transfers between devices  23.3 us (30%)
  waiting for transfers between devices  22.4 us (29%)
  local copies, waits for them, and re-layouts  0.96 us (1%)
    all_to_all x2, waiting for transfers between devices, exchange(): lax.all_to_all(x, ('dp', 'mp'), 0, 0, tiled=True, axis_index_groups=groups)  9.6 us
    pallas_call x1, Pallas kernels, shards(): pl.pallas_call(first_kernel, out_shape=(pltpu.HBM((planes, 5, 144, 256),...  9.23 us
    all_to_all x2, starting transfers between devices, exchange(): lax.all_to_all(x, ('dp', 'mp'), 0, 0, tiled=True, axis_index_groups=groups)  8.24 us
    pallas_call x1, Pallas kernels, shards(): call(functools.partial(grad_a_kernel, n), (shape((peers, 16, 128), F32),...  6.82 us
    ppermute x3, waiting for transfers between devices, shards(): lax.ppermute(pieces[d], 'mp', [(i, (i + d) % n) for i in range(n)])  5.77 us
    all_to_all x1, waiting for transfers between devices, shards(): cot = lax.all_to_all(packed, 'mp', 0, 0, tiled=True)  5.66 us
    ppermute x3, starting transfers between devices, shards(): lax.ppermute(pieces[d], 'mp', [(i, (i + d) % n) for i in range(n)])  5.64 us
    ppermute x1, starting transfers between devices, shards(): halo = lax.ppermute(halo, 'mp', up)  4.94 us
  transfers between devices with their start and end apart: 11, of which 6 were waited for; matrix products, arithmetic and copies ran while one was open for 0% of the time, Pallas kernels for 34%

profile of v2, /device:TPU:0, one launch (start us, length us, event | category | flops | bytes accessed | tf_op | source)
XLA Modules:
  0.0 77.2 jit_solution(6241009275502408979)
XLA Ops:
  0.6 1.0 %shard_map.67.after_ref = bf16[64,2048]{1,0:T(8,128)(2,1)S(1)} custom-call(bf16[1,16,64,2048]{3,2,1,0:T(8,128)(2,1)} %vol_ref.3), custom_call_target="tpu_custom_call" | custom-call | flops 1000000000 | bytes 3000000 | tf_op jit(solution)/shard_map/pallas_call | solution.py:501
  1.6 4.9 %collective-permute-start = (bf16[64,2048]{1,0:T(8,128)(2,1)S(1)}, bf16[64,2048]{1,0:T(8,128)(2,1)S(1)}, u32[]{:S(2)}, u32[]{:S(2)}) collective-permute-start(bf16[64,2048]{1,0:T(8,128)(2,1)S(1)} %shard_map.67.after_ref), channel_id=1, source_target_pairs={{0,8},{8,16},{16,24},{1,9},{9,17},{17,25},{2,10},{10,18},{18,26},{... | collective-permute-start | bytes 786440 | tf_op jit(solution)/shard_map/ppermute | solution.py:523
  6.5 0.0 copy-start
  6.6 2.8 %shard_map.68 = bf16[4,544,128]{2,1,0:T(8,128)(2,1)} custom-call(bf16[1,16,16,16,32]{4,3,2,1,0:T(8,128)(2,1)} %cot_ref.1, bf16[27,16,128]{2,1,0:T(8,128)(2,1)} %bitcast.2, bf16[64,2048]{1,0:T(8,128)(2,1)S(1)} %shard_map.67.after_ref), custom_call_target="tpu_custom_call" | custom-call | flops 2000000000 | bytes 6000000 | tf_op jit(solution)/shard_map/pallas_call | solution.py:510
  9.4 3.8 %all-to-all-start = ((bf16[4,544,128]{2,1,0:T(8,128)(2,1)}), bf16[4,544,128]{2,1,0:T(8,128)(2,1)S(1)}, u32[]{:S(2)}, u32[]{:S(2)}) async-start(bf16[4,544,128]{2,1,0:T(8,128)(2,1)} %shard_map.68), calls=%async_computation | async-start | bytes 1114112 | tf_op jit(solution)/shard_map/all_to_all | solution.py:524
  13.3 0.0 copy-done
  13.3 9.2 %shard_map.69 = (bf16[16,5,144,256]{3,2,1,0:T(8,128)(2,1)}, bf16[8,3,144,256]{3,2,1,0:T(8,128)(2,1)}, f32[256,256]{1,0:T(8,128)S(1)}) custom-call(bf16[1,16,64,2048]{3,2,1,0:T(8,128)(2,1)} %vol_ref.3, bf16[3,3,3,32,64]{4,3,2,1,0:T(8,128)(2,1)S(1)} %copy-done), custom_call_target="tpu_custom_call" | custom-call | flops 99999997952 | bytes 300000000 | tf_op jit(solution)/shard_map/pallas_call | solution.py:525
  22.5 0.0 collective-permute-done.halo_ref
  22.5 5.7 %all-to-all-done.cot_ref.kb_ref = bf16[4,544,128]{2,1,0:T(8,128)(2,1)S(1)} async-done(((bf16[4,544,128]{2,1,0:T(8,128)(2,1)}), bf16[4,544,128]{2,1,0:T(8,128)(2,1)S(1)}, u32[]{:S(2)}, u32[]{:S(2)}) %all-to-all-start) | async-done | bytes 557088 | tf_op jit(solution)/shard_map/all_to_all | solution.py:524
  28.2 0.0 collective-permute-start.2
  28.2 0.0 copy-start.1
  28.2 0.0 copy-start.3
  28.2 3.9 %shard_map.70 = (bf16[5,144,256]{2,1,0:T(8,128)(2,1)S(1)}, bf16[3,144,256]{2,1,0:T(8,128)(2,1)S(1)}, bf16[5,2,144,256]{3,2,1,0:T(8,128)(2,1)S(1)}, f32[16,64,128]{2,1,0:T(8,128)S(1)}, f32[16,64,128]{2,1,0:T(8,128)S(1)}) custom-call(bf16[64,2048]{1,0:T(8,128)(2,1)S(1)} %collective-permute-done.halo_ref, bf16[3,3,3,32,64]{4,3,2,1,0:T(8,128)(2,1)S(1)} %copy-done, ...), custom_call_target="tpu_custom_call" | custom-call | flops 3000000000 | bytes 9000000 | tf_op jit(solution)/shard_map/pallas_call | solution.py:549
  32.0 0.0 copy-start.4
  32.1 0.6 collective-permute-start.1
  32.6 0.0 collective-permute-done.2.other_ref
  32.6 0.0 copy-done.1
  32.6 0.0 copy-done.3
  32.6 6.8 %shard_map.71 = (f32[16,16,128]{2,1,0:T(8,128)S(1)}, f32[16,16,128]{2,1,0:T(8,128)S(1)}) custom-call(bf16[4,544,128]{2,1,0:T(8,128)(2,1)S(1)} %all-to-all-done.cot_ref.kb_ref, bf16[4,544,128]{2,1,0:T(8,128)(2,1)S(1)} %collective-permute-done.2.other_ref, bf16[8,3,144,256]{3,2,1,0:T(8,128)(2,1)S(1)} %copy-done.1, ...), custom_call_target="tpu_custom_call" | custom-call | flops 8000000000 | bytes 24000000 | tf_op jit(solution)/shard_map/pallas_call | solution.py:565
  39.5 0.0 copy-done.4
  39.5 0.0 copy-start.2
  39.5 0.1 collective-permute-start.3
  39.6 0.0 collective-permute-done.1.got_b
  39.6 1.3 %collective-permute-done.3.got_a = f32[16,16,128]{2,1,0:T(8,128)S(1)} collective-permute-done((f32[16,16,128]{2,1,0:T(8,128)S(1)}, f32[16,16,128]{2,1,0:T(8,128)S(1)}, u32[]{:S(2)}, u32[]{:S(2)}) %collective-permute-start.3) | collective-permute-done | bytes 131104 | tf_op jit(solution)/shard_map/ppermute | solution.py:573
  40.9 0.8 %shard_map.72 = bf16[16,80,128]{2,1,0:T(8,128)(2,1)} custom-call(f32[16,64,128]{2,1,0:T(8,128)S(1)} %get-tuple-element.37.keep_b, f32[16,64,128]{2,1,0:T(8,128)S(1)} %collective-permute-done.1.got_b, f32[16,16,128]{2,1,0:T(8,128)S(1)} %get-tuple-element.43.keep_a, f32[16,16,128]{2,1,0:T(8,128)S(1)} %collective-permute-done.3.got_a), custom_call_target="tpu_custom_call" | custom-call | flops 1000000000 | bytes 3000000 | tf_op jit(solution)/shard_map/pallas_call | solution.py:575
  41.7 4.7 %all-to-all-start.1 = ((bf16[16,80,128]{2,1,0:T(8,128)(2,1)}), bf16[16,80,128]{2,1,0:T(8,128)(2,1)S(1)}, u32[]{:S(2)}, u32[]{:S(2)}) async-start(bf16[16,80,128]{2,1,0:T(8,128)(2,1)} %shard_map.72), calls=%async_computation.1 | async-start | bytes 655360 | tf_op jit(solution)/shard_map/all_to_all | solution.py:495
  46.4 0.0 copy-done.2
  46.4 0.0 copy-start.5
  46.5 0.9 %copy-done.5 = bf16[3,144,256]{2,1,0:T(8,128)(2,1)S(1)} copy-done((bf16[3,144,256]{2,1,0:T(8,128)(2,1)S(1)}, bf16[3,144,256]{2,1,0:T(8,128)(2,1)}, u32[]{:S(2)}) %copy-start.5) | copy-done | bytes 221208
  47.4 1.9 %shard_map.73 = (bf16[320,128]{1,0:T(8,128)(2,1)S(1)}, bf16[320,128]{1,0:T(8,128)(2,1)S(1)}, bf16[320,128]{1,0:T(8,128)(2,1)S(1)}, bf16[320,128]{1,0:T(8,128)(2,1)S(1)}) custom-call(bf16[4,544,128]{2,1,0:T(8,128)(2,1)S(1)} %all-to-all-done.cot_ref.kb_ref, bf16[4,544,128]{2,1,0:T(8,128)(2,1)S(1)} %collective-permute-done.2.other_ref, ...), custom_call_target="tpu_custom_call" | custom-call | flops 4000000000 | bytes 12000000 | tf_op jit(solution)/shard_map/pallas_call | solution.py:578
  49.3 9.4 %all-to-all-done.1.in_ref = bf16[16,80,128]{2,1,0:T(8,128)(2,1)S(1)} async-done(((bf16[16,80,128]{2,1,0:T(8,128)(2,1)}), bf16[16,80,128]{2,1,0:T(8,128)(2,1)S(1)}, u32[]{:S(2)}, u32[]{:S(2)}) %all-to-all-start.1) | async-done | bytes 327712 | tf_op jit(solution)/shard_map/all_to_all | solution.py:495
  58.7 0.7 shard_map.74
  59.4 3.5 %all-to-all-start.2 = ((bf16[16,32,128]{2,1,0:T(8,128)(2,1)}), bf16[16,32,128]{2,1,0:T(8,128)(2,1)S(1)}, u32[]{:S(2)}, u32[]{:S(2)}) async-start(bf16[16,32,128]{2,1,0:T(8,128)(2,1)} %shard_map.74), calls=%async_computation.2 | async-start | bytes 262144 | tf_op jit(solution)/shard_map/all_to_all | solution.py:495
  62.9 1.8 %collective-permute-start.4 = (bf16[320,128]{1,0:T(8,128)(2,1)S(1)}, bf16[320,128]{1,0:T(8,128)(2,1)S(1)}, u32[]{:S(2)}, u32[]{:S(2)}) collective-permute-start(bf16[320,128]{1,0:T(8,128)(2,1)S(1)} %get-tuple-element.51), channel_id=1, source_target_pairs={{0,8},{8,16},{16,24},{24,0},{1,9},{9,17},{17,25},{25,1},{2,10},{10... | collective-permute-start | bytes 245768 | tf_op jit(solution)/shard_map/ppermute | solution.py:590
  64.8 2.4 %collective-permute-start.5 = (bf16[320,128]{1,0:T(8,128)(2,1)S(1)}, bf16[320,128]{1,0:T(8,128)(2,1)S(1)}, u32[]{:S(2)}, u32[]{:S(2)}) collective-permute-start(bf16[320,128]{1,0:T(8,128)(2,1)S(1)} %get-tuple-element.52), channel_id=1, source_target_pairs={{0,16},{8,24},{16,0},{24,8},{1,17},{9,25},{17,1},{25,9},{2,18},{10... | collective-permute-start | bytes 245768 | tf_op jit(solution)/shard_map/ppermute | solution.py:590
  67.1 1.5 %collective-permute-start.6 = (bf16[320,128]{1,0:T(8,128)(2,1)S(1)}, bf16[320,128]{1,0:T(8,128)(2,1)S(1)}, u32[]{:S(2)}, u32[]{:S(2)}) collective-permute-start(bf16[320,128]{1,0:T(8,128)(2,1)S(1)} %get-tuple-element.53), channel_id=1, source_target_pairs={{0,24},{8,0},{16,8},{24,16},{1,25},{9,1},{17,9},{25,17},{2,26},{10... | collective-permute-start | bytes 245768 | tf_op jit(solution)/shard_map/ppermute | solution.py:590
  68.6 3.2 %collective-permute-done.4.refs_1_ = bf16[320,128]{1,0:T(8,128)(2,1)S(1)} collective-permute-done((bf16[320,128]{1,0:T(8,128)(2,1)S(1)}, bf16[320,128]{1,0:T(8,128)(2,1)S(1)}, u32[]{:S(2)}, u32[]{:S(2)}) %collective-permute-start.4) | collective-permute-done | bytes 81952 | tf_op jit(solution)/shard_map/ppermute | solution.py:590
  71.8 2.6 %collective-permute-done.5.refs_2_ = bf16[320,128]{1,0:T(8,128)(2,1)S(1)} collective-permute-done((bf16[320,128]{1,0:T(8,128)(2,1)S(1)}, bf16[320,128]{1,0:T(8,128)(2,1)S(1)}, u32[]{:S(2)}, u32[]{:S(2)}) %collective-permute-start.5) | collective-permute-done | bytes 81952 | tf_op jit(solution)/shard_map/ppermute | solution.py:590
  74.3 0.0 collective-permute-done.6.refs_3_
  74.4 0.2 all-to-all-done.2.mine_ref
  74.6 0.0 collective-permute-start.7
  74.6 1.8 %shard_map.75 = bf16[1,16,16,16,32]{4,3,2,1,0:T(8,128)(2,1)} custom-call(bf16[320,128]{1,0:T(8,128)(2,1)S(1)} %get-tuple-element.54.refs_0_, bf16[320,128]{1,0:T(8,128)(2,1)S(1)} %collective-permute-done.4.refs_1_, bf16[320,128]{1,0:T(8,128)(2,1)S(1)} %collective-permute-done.5.refs_2_, bf16[320,128]{1,0:T(8,128)(2,1)S(1)} %collective-permute-done.6.refs_3_), custom_call_target="tpu_custom_call" | custom-call | flops 2000000000 | bytes 6000000 | tf_op jit(solution)/shard_map/pallas_call | solution.py:603
  76.3 0.0 collective-permute-done.7.other_ref
  76.3 0.9 %shard_map.76 = (f32[3,3,3,32,64]{4,3,2,1,0:T(8,128)}, f32[27,16,128]{2,1,0:T(8,128)}) custom-call(bf16[16,32,128]{2,1,0:T(8,128)(2,1)S(1)} %all-to-all-done.2.mine_ref, bf16[16,32,128]{2,1,0:T(8,128)(2,1)S(1)} %collective-permute-done.7.other_ref), custom_call_target="tpu_custom_call" | custom-call | flops 1000000000 | bytes 3000000 | tf_op jit(solution)/shard_map/pallas_call | solution.py:604
Async XLA Ops:
  1.6 20.9 %collective-permute-start = (bf16[64,2048]{1,0:T(8,128)(2,1)S(1)}, bf16[64,2048]{1,0:T(8,128)(2,1)S(1)}, u32[]{:S(2)}, u32[]{:S(2)}) collective-permute-start(bf16[64,2048]{1,0:T(8,128)(2,1)S(1)} %shard_map.67.after_ref), channel_id=1, source_target_pairs={{0,8},{8,16},{16,24},{1,9},{9,17},{17,25},{2,10},{10,18},{18,26},{... | collective-permute-start | bytes 786440 | tf_op jit(solution)/shard_map/ppermute | solution.py:523
  6.5 6.7 %copy-start = (bf16[3,3,3,32,64]{4,3,2,1,0:T(8,128)(2,1)S(1)}, bf16[3,3,3,32,64]{4,3,2,1,0:T(8,128)(2,1)}, u32[]{:S(2)}) copy-start(bf16[3,3,3,32,64]{4,3,2,1,0:T(8,128)(2,1)} %ka_ref.3) | copy-start | bytes 331780
  9.4 18.8 %all-to-all-start = ((bf16[4,544,128]{2,1,0:T(8,128)(2,1)}), bf16[4,544,128]{2,1,0:T(8,128)(2,1)S(1)}, u32[]{:S(2)}, u32[]{:S(2)}) async-start(bf16[4,544,128]{2,1,0:T(8,128)(2,1)} %shard_map.68), calls=%async_computation | async-start | bytes 1114112 | tf_op jit(solution)/shard_map/all_to_all | solution.py:524
  28.2 4.5 %collective-permute-start.2 = (bf16[4,544,128]{2,1,0:T(8,128)(2,1)S(1)}, bf16[4,544,128]{2,1,0:T(8,128)(2,1)S(1)}, u32[]{:S(2)}, u32[]{:S(2)}) collective-permute-start(bf16[4,544,128]{2,1,0:T(8,128)(2,1)S(1)} %all-to-all-done.cot_ref.kb_ref), channel_id=1, source_target_pairs={{0,1},{1,0},{2,3},{3,2},{4,5},{5,4},{6,7},{7,6},{8,9},{9,8},{10,11... | collective-permute-start | bytes 1671176 | tf_op jit(solution)/shard_map/ppermute | solution.py:547
  28.2 4.5 %copy-start.1 = (bf16[8,3,144,256]{3,2,1,0:T(8,128)(2,1)S(1)}, bf16[8,3,144,256]{3,2,1,0:T(8,128)(2,1)}, u32[]{:S(2)}) copy-start(bf16[8,3,144,256]{3,2,1,0:T(8,128)(2,1)} %get-tuple-element.35.hin_ref.h_ref) | copy-start | bytes 5308420
  28.2 4.5 %copy-start.3 = (bf16[16,5,144,256]{3,2,1,0:T(8,128)(2,1)S(1)}, bf16[16,5,144,256]{3,2,1,0:T(8,128)(2,1)}, u32[]{:S(2)}) copy-start(bf16[16,5,144,256]{3,2,1,0:T(8,128)(2,1)} %get-tuple-element.41.vd_ref) | copy-start | bytes 17694724
  32.0 7.4 %copy-start.4 = (bf16[3,144,256]{2,1,0:T(8,128)(2,1)}, bf16[3,144,256]{2,1,0:T(8,128)(2,1)S(1)}, u32[]{:S(2)}) copy-start(bf16[3,144,256]{2,1,0:T(8,128)(2,1)S(1)} %get-tuple-element.39.h0_ref) | copy-start | bytes 663556
  32.1 7.5 %collective-permute-start.1 = (f32[16,64,128]{2,1,0:T(8,128)S(1)}, f32[16,64,128]{2,1,0:T(8,128)S(1)}, u32[]{:S(2)}, u32[]{:S(2)}) collective-permute-start(f32[16,64,128]{2,1,0:T(8,128)S(1)} %get-tuple-element.38), channel_id=1, source_target_pairs={{0,1},{1,0},{2,3},{3,2},{4,5},{5,4},{6,7},{7,6},{8,9},{9,8},{10,11... | collective-permute-start | bytes 1572872 | tf_op jit(solution)/shard_map/ppermute | solution.py:563
  39.5 6.9 %copy-start.2 = (bf16[8,3,144,256]{3,2,1,0:T(8,128)(2,1)S(1)}, bf16[8,3,144,256]{3,2,1,0:T(8,128)(2,1)}, u32[]{:S(2)}) copy-start(bf16[8,3,144,256]{3,2,1,0:T(8,128)(2,1)} %get-tuple-element.35.hin_ref.h_ref) | copy-start | bytes 5308420
  39.5 1.4 %collective-permute-start.3 = (f32[16,16,128]{2,1,0:T(8,128)S(1)}, f32[16,16,128]{2,1,0:T(8,128)S(1)}, u32[]{:S(2)}, u32[]{:S(2)}) collective-permute-start(f32[16,16,128]{2,1,0:T(8,128)S(1)} %get-tuple-element.44), channel_id=1, source_target_pairs={{0,1},{1,0},{2,3},{3,2},{4,5},{5,4},{6,7},{7,6},{8,9},{9,8},{10,11... | collective-permute-start | bytes 393224 | tf_op jit(solution)/shard_map/ppermute | solution.py:573
  41.7 17.0 %all-to-all-start.1 = ((bf16[16,80,128]{2,1,0:T(8,128)(2,1)}), bf16[16,80,128]{2,1,0:T(8,128)(2,1)S(1)}, u32[]{:S(2)}, u32[]{:S(2)}) async-start(bf16[16,80,128]{2,1,0:T(8,128)(2,1)} %shard_map.72), calls=%async_computation.1 | async-start | bytes 655360 | tf_op jit(solution)/shard_map/all_to_all | solution.py:495
  46.4 0.9 %copy-start.5 = (bf16[3,144,256]{2,1,0:T(8,128)(2,1)S(1)}, bf16[3,144,256]{2,1,0:T(8,128)(2,1)}, u32[]{:S(2)}) copy-start(bf16[3,144,256]{2,1,0:T(8,128)(2,1)} %copy-done.4) | copy-start | bytes 663556
  59.4 15.1 %all-to-all-start.2 = ((bf16[16,32,128]{2,1,0:T(8,128)(2,1)}), bf16[16,32,128]{2,1,0:T(8,128)(2,1)S(1)}, u32[]{:S(2)}, u32[]{:S(2)}) async-start(bf16[16,32,128]{2,1,0:T(8,128)(2,1)} %shard_map.74), calls=%async_computation.2 | async-start | bytes 262144 | tf_op jit(solution)/shard_map/all_to_all | solution.py:495
  62.9 8.8 %collective-permute-start.4 = (bf16[320,128]{1,0:T(8,128)(2,1)S(1)}, bf16[320,128]{1,0:T(8,128)(2,1)S(1)}, u32[]{:S(2)}, u32[]{:S(2)}) collective-permute-start(bf16[320,128]{1,0:T(8,128)(2,1)S(1)} %get-tuple-element.51), channel_id=1, source_target_pairs={{0,8},{8,16},{16,24},{24,0},{1,9},{9,17},{17,25},{25,1},{2,10},{10... | collective-permute-start | bytes 245768 | tf_op jit(solution)/shard_map/ppermute | solution.py:590
  64.8 9.6 %collective-permute-start.5 = (bf16[320,128]{1,0:T(8,128)(2,1)S(1)}, bf16[320,128]{1,0:T(8,128)(2,1)S(1)}, u32[]{:S(2)}, u32[]{:S(2)}) collective-permute-start(bf16[320,128]{1,0:T(8,128)(2,1)S(1)} %get-tuple-element.52), channel_id=1, source_target_pairs={{0,16},{8,24},{16,0},{24,8},{1,17},{9,25},{17,1},{25,9},{2,18},{10... | collective-permute-start | bytes 245768 | tf_op jit(solution)/shard_map/ppermute | solution.py:590
  67.1 7.2 %collective-permute-start.6 = (bf16[320,128]{1,0:T(8,128)(2,1)S(1)}, bf16[320,128]{1,0:T(8,128)(2,1)S(1)}, u32[]{:S(2)}, u32[]{:S(2)}) collective-permute-start(bf16[320,128]{1,0:T(8,128)(2,1)S(1)} %get-tuple-element.53), channel_id=1, source_target_pairs={{0,24},{8,0},{16,8},{24,16},{1,25},{9,1},{17,9},{25,17},{2,26},{10... | collective-permute-start | bytes 245768 | tf_op jit(solution)/shard_map/ppermute | solution.py:590
  74.6 1.8 %collective-permute-start.7 = (bf16[16,32,128]{2,1,0:T(8,128)(2,1)S(1)}, bf16[16,32,128]{2,1,0:T(8,128)(2,1)S(1)}, u32[]{:S(2)}, u32[]{:S(2)}) collective-permute-start(bf16[16,32,128]{2,1,0:T(8,128)(2,1)S(1)} %all-to-all-done.2.mine_ref), channel_id=1, source_target_pairs={{0,1},{1,0},{2,3},{3,2},{4,5},{5,4},{6,7},{7,6},{8,9},{9,8},{10,11... | collective-permute-start | bytes 393224 | tf_op jit(solution)/shard_map/ppermute | solution.py:601

commit v3 on v2

--- a/solution.py
+++ b/solution.py
@@ -20,10 +20,6 @@
 
 def dot(a, b):
     return lax.dot_general(a, b, (((1,), (0,)), ((), ())), preferred_element_type=F32)
-
-
-def dot_nt(a, b):
-    return lax.dot_general(a, b, (((1,), (1,)), ((), ())), preferred_element_type=F32)
 
 
 def iota(shape, dim):
@@ -92,6 +88,11 @@
     return jnp.where(iota(x.shape, 0) % 16 == 0, 0.0, moved)
 
 
+def next_group(x):
+    moved = pltpu.roll(x, 112, 1)
+    return jnp.where(iota(x.shape, 1) >= 112, 0.0, moved)
+
+
 def up_shift(x):
     moved = pltpu.roll(x, x.shape[0] - 1, 0)
     return jnp.where(iota(x.shape, 0) % 16 == 15, 0.0, moved)
@@ -114,7 +115,7 @@
     return read
 
 
-def first_kernel(vol_ref, ka_ref, out_ref, hout_ref, pre_ref, x_ref, vd_ref, h_ref, ta_ref, sems, out_sems, h_sems):
+def first_kernel(vol_ref, ka_ref, out_ref, h_ref, pre_ref, x_ref, vd_ref, ta_ref, sems, out_sems):
     steps = x_ref.shape[0]
 
     def fetch(i):
@@ -124,9 +125,6 @@
         return pltpu.make_async_copy(
             vd_ref.at[pl.ds(4 * i + 1, 4)], out_ref.at[pl.ds(4 * i, 4)], out_sems.at[i]
         )
-
-    def flush_hidden(i):
-        return pltpu.make_async_copy(h_ref.at[pl.ds(2 * i, 2)], hout_ref.at[pl.ds(2 * i, 2)], h_sems.at[i])
 
     for i in range(steps):
         fetch(i).start()
@@ -157,11 +155,17 @@
                 h_ref[2 * i + k, slot, 16:144, :] = x
 
             store_hidden(put, hid[256 * k : 256 * k + 128], hid[256 * k + 128 : 256 * k + 256])
-        flush_hidden(i).start()
 
     for i in range(steps):
         flush(i).wait()
-        flush_hidden(i).wait()
+
+
+def order(n):
+    return sorted(range(n), key=lambda z: abs(2 * z - (n - 1)))
+
+
+def place(n, z):
+    return order(n).index(z)
 
 
 def core_of():
@@ -189,10 +193,10 @@
         z = jnp.concatenate([y[rows * l : rows * l + rows] for l in range(lanes)], axis=1).astype(BF)
         t = p // per
         at = (p % per) * rows
-        out_ref[t, at : at + rows, :] = z
+        out_ref[place(n, t), at : at + rows, :] = z
         if p % per == 0 and t > 0:
-            out_ref[t - 1, per * rows : per * rows + rows, :] = z
-    out_ref[n - 1, per * rows : per * rows + rows, :] = jnp.zeros((rows, 128), BF)
+            out_ref[place(n, t - 1), per * rows : per * rows + rows, :] = z
+    out_ref[place(n, n - 1), per * rows : per * rows + rows, :] = jnp.zeros((rows, 128), BF)
     first = 13 * core_of()
     size = kb_ref.shape[1]
     for j in range(HALF):
@@ -213,8 +217,12 @@
     return (col == target).astype(F32).astype(BF)
 
 
+def slab_planes(a, count):
+    return [2 * p + a - 1 for p in range(count + 1)][1 if a == 0 else 0 :][:count]
+
+
 def second_rows(hread, a, count):
-    planes = [2 * p + a - 1 for p in range(count + 1)][1 if a == 0 else 0 :][:count]
+    planes = slab_planes(a, count)
     parts = []
     for b in range(3):
         parts.append(jnp.concatenate([hread(u, b, 16, 0, 256) for u in planes], axis=0))
@@ -238,37 +246,33 @@
     return put
 
 
-def put_half(keep_ref, send_ref, item, v):
-    mine = core_of() == item % 2
-
-    @pl.when(mine)
-    def _():
-        keep_ref[item // 2] = v
-
-    @pl.when(jnp.logical_not(mine))
-    def _():
-        send_ref[item // 2] = v
-
-
-def clear_from(count, keep_ref, send_ref):
+def put_half(both_ref, item, v):
+    both_ref[(item + core_of()) % 2, item // 2] = v
+
+
+def split_halves(count, both_ref, keep_ref, send_ref):
     zero = jnp.zeros(keep_ref.shape[1:], F32)
     for item in range(count, 2 * keep_ref.shape[0]):
-        put_half(keep_ref, send_ref, item, zero)
-
-
-def grad_b_kernel(
-    n, halo_ref, ka_ref, pre_ref, hin_ref, cot_ref, vdh_ref, h0_ref, c_ref, keep_ref, send_ref, ta_ref, h_ref, sem
-):
-    fetch = pltpu.make_async_copy(hin_ref, h_ref, sem)
-    fetch.start()
+        put_half(both_ref, item, zero)
+    keep_ref[...] = both_ref[0]
+    send_ref[...] = both_ref[1]
+
+
+def halo_kernel(halo_ref, ka_ref, pre_ref, vd_out, h0_ref, vdh_ref, ta_ref, sem):
+    build_first(ka_ref, ta_ref, 3)
+    store_plane(vdh_ref, (), deinterleave(halo_ref[...], 1), 0)
+    flush = pltpu.make_async_copy(vdh_ref, vd_out, sem)
+    flush.start()
+    hid = leaky(pre_ref[...] + first_term([sub(vdh_ref)], 0, ta_ref))
+    store_hidden(put_in(h0_ref), hid[0:128], hid[128:256])
+    flush.wait()
+
+
+def grad_b_kernel(n, h_ref, h0_ref, cot_ref, c_ref, both_ref):
     slab = 16 // n
     lanes = n
     rows = 256 // lanes
-    build_first(ka_ref, ta_ref, 3)
-    store_plane(vdh_ref, (), deinterleave(halo_ref[...], 1), 0)
-    hid = leaky(pre_ref[...] + first_term([sub(vdh_ref)], 0, ta_ref))
-    store_hidden(put_in(h0_ref), hid[0:128], hid[128:256])
-    wide = jnp.concatenate([cot_ref[t, 0 : (slab + 1) * rows, :] for t in range(n)], axis=1)
+    wide = jnp.concatenate([cot_ref[place(n, t), 0 : (slab + 1) * rows, :] for t in range(n)], axis=1)
     turned = dot(wide, lane_order(n, False))
     turns = []
     for p in range(slab + 1):
@@ -282,43 +286,54 @@
             ],
             axis=0,
         )
-        turns.append(main.T.astype(BF))
+        turn = main.T
+        one = jnp.concatenate([turn[0:128], turn[128:256]], axis=1)
+        two = jnp.concatenate([turn[128:256], next_group(turn[0:128])], axis=1)
+        turns.append(jnp.concatenate([one, two], axis=0).astype(BF))
         for slot, v in enumerate((main, up_shift(main))):
             c_ref[p, slot, 0:128, :] = v.astype(BF)
             c_ref[p, slot, 128:144, :] = jnp.zeros((16, 256), BF)
     read = hidden_reader(h_ref, h0_ref)
-    clear_from(TAPS, keep_ref, send_ref)
-    fetch.wait()
     for a in range(3):
         first = 1 if a == 0 else 0
         turn = jnp.concatenate(turns[first : first + slab], axis=1)
-        g = dot(turn, second_rows(read, a, slab))
+        columns = []
+        for b in range(3):
+            tiles = [read(u, b, 16, 128 * k, 128) for u in slab_planes(a, slab) for k in range(2)]
+            columns.append(jnp.concatenate(tiles, axis=0))
+        g = dot(turn, jnp.concatenate(columns, axis=1))
         for b in range(3):
             t = 3 * a + b
-            l = 384 * b
-            one = (g[0:128, l : l + 128] + g[128:256, l + 128 : l + 256]).T
-            two = (g[0:128, l + 256 : l + 384] + g[128:256, l : l + 128]).T
-            put_half(keep_ref, send_ref, 3 * t, two[64:128])
-            put_half(keep_ref, send_ref, 3 * t + 1, one[0:64])
-            put_half(keep_ref, send_ref, 3 * t + 2, one[64:128])
-
-
-def build_second(n, kb_ref, other_ref, tb_ref):
+            one = g[0:128, 128 * b : 128 * b + 128].T
+            two = g[128:256, 128 * b : 128 * b + 128].T
+            both_ref[3 * t % 2, 3 * t // 2] = two[64:128]
+            both_ref[(3 * t + 1) % 2, (3 * t + 1) // 2] = one[0:64]
+            both_ref[(3 * t + 2) % 2, (3 * t + 2) // 2] = one[64:128]
+    for item in range(TAPS, 2 * both_ref.shape[1]):
+        both_ref[item % 2, item // 2] = jnp.zeros(both_ref.shape[2:], F32)
+
+
+def second_taps(n, kb_ref, other_ref):
     chan = 64 // n
     start = (16 // n + 1) * (256 // n)
-    blank = jnp.zeros((64, 128), BF)
     first = core_of() == 0
 
     def tap(k):
         j, own_first = (k, True) if k < 13 else (k - 13, False)
         parts = []
         for z in range(n):
-            own = kb_ref[z, start + j * chan : start + j * chan + chan, :]
-            other = other_ref[z, start + j * chan : start + j * chan + chan, :]
+            own = kb_ref[place(n, z), start + j * chan : start + j * chan + chan, :]
+            other = other_ref[place(n, z), start + j * chan : start + j * chan + chan, :]
             pair = (own, other) if own_first else (other, own)
             parts.append(jnp.where(first, *pair))
         return jnp.concatenate(parts, axis=0)
 
+    return tap
+
+
+def build_second(n, kb_ref, other_ref, tb_ref):
+    tap = second_taps(n, kb_ref, other_ref)
+    blank = jnp.zeros((64, 128), BF)
     for t in range(9):
         taps = [tap(3 * t + c) for c in range(3)]
         for w in range(-2, 4):
@@ -328,56 +343,74 @@
                 tb_ref[row : row + 64, 128 * r : 128 * r + 128] = taps[c] if 0 <= c <= 2 else blank
 
 
-def grad_a_kernel(n, kb_ref, other_ref, h_ref, h0_ref, c_ref, vd_ref, vdh_ref, keep_ref, send_ref, tb_ref, d_ref):
+REACH = (((4,), (3, 5)), ((1, 7), (0, 2, 6, 8)))
+
+
+def build_transposed(n, kb_ref, other_ref, tb_ref):
+    tap = second_taps(n, kb_ref, other_ref)
+    blank = jnp.zeros((128, 128), BF)
+    for at, t in enumerate(REACH[0][0] + REACH[0][1] + REACH[1][0] + REACH[1][1]):
+        taps = [tap(3 * t + c).astype(F32) for c in range(3)]
+        both = jnp.concatenate([taps[1], taps[2]], axis=0).T.astype(BF)
+        low = jnp.concatenate([jnp.zeros((64, 128), F32), taps[0]], axis=0).T.astype(BF)
+        for r, (left, right) in enumerate(((both, blank), (low, both), (blank, low))):
+            row = 384 * at + 128 * r
+            tb_ref[row : row + 128, 0:128] = left
+            tb_ref[row : row + 128, 128:256] = right
+
+
+def grad_a_kernel(n, kb_ref, other_ref, h_ref, h0_ref, c_ref, vd_ref, vdh_ref, keep_ref, send_ref, tb_ref, d_ref, both_ref):
     slab = 16 // n
     planes = 2 * slab
-    build_second(n, kb_ref, other_ref, tb_ref)
+    build_transposed(n, kb_ref, other_ref, tb_ref)
     read = hidden_reader(h_ref, h0_ref)
+    row = 0
     for par in range(2):
         for hp in range(2):
-            low, high = None, None
-            for a in (1,) if par == 0 else (0, 2):
-                for b in (1,) if hp == 0 else (0, 2):
-                    t = 3 * a + b
-                    up = 1 if a == 0 else 0
-                    slot = 1 if b == 0 else 0
-                    main = jnp.concatenate([c_ref[p + up, slot, 0:128, :] for p in range(slab)], axis=0)
-                    edge = jnp.concatenate([c_ref[p + up, slot, 16:144, 0:128] for p in range(slab)], axis=0)
-                    x = dot_nt(main, tb_ref[384 * t : 384 * t + 256, :])
-                    e = dot_nt(edge, tb_ref[384 * t + 256 : 384 * t + 384, 0:128])
-                    low = x[:, 0:128] if low is None else low + x[:, 0:128]
-                    high = x[:, 128:256] + e if high is None else high + x[:, 128:256] + e
-            back = jnp.concatenate([low, high], axis=1).astype(BF).astype(F32)
+            parts = []
+            for t in REACH[par][hp]:
+                up = 1 if t < 3 else 0
+                slot = 1 if t % 3 == 0 else 0
+                parts.append(jnp.concatenate([c_ref[p + up, slot, 0:128, :] for p in range(slab)], axis=0))
+                parts.append(jnp.concatenate([c_ref[p + up, slot, 16:144, 0:128] for p in range(slab)], axis=0))
+            size = 192 * len(parts)
+            back = dot(jnp.concatenate(parts, axis=1), tb_ref[row : row + size, :])
+            row += size
+            back = back.astype(BF).astype(F32)
             for p in range(slab):
                 u = 2 * p + par
                 mask = read(u, 1 + hp, 16, 0, 256).astype(F32) > 0
                 v = back[128 * p : 128 * p + 128]
-                at = 256 * u + 128 * hp
-                d_ref[:, at : at + 128] = jnp.where(mask, v, 0.3 * v).astype(BF).astype(F32).T.astype(BF)
+                v = jnp.where(mask, v, 0.3 * v).T
+                at = 512 * u + 256 * hp
+                d_ref[0:128, at : at + 128] = v[0:128].astype(BF)
+                d_ref[128:192, at : at + 128] = v[128:192].astype(BF)
+                d_ref[0:128, at + 128 : at + 256] = v[128:256].astype(BF)
+                d_ref[128:192, at + 128 : at + 256] = next_group(v[0:64]).astype(BF)
     left = iota((64, 128), 1) < 32
     pieces = []
-    for a in range(3):
-        for b in range(3):
-            mains, edges = [], []
+    for first in range(0, 9, 2):
+        columns = []
+        for t in range(first, min(first + 2, 9)):
+            a, b = t // 3, t % 3
+            tiles = []
             for u in range(planes):
                 src = sub(vdh_ref) if 2 * u + a == 0 else sub(vd_ref, 2 * u + a - 1)
-                m, e = first_rows(src, b)
-                mains.append(m)
-                edges.append(e)
-            x = jnp.concatenate([jnp.concatenate(mains, axis=0), jnp.concatenate(edges, axis=0)], axis=1)
-            g = dot(d_ref[...], x)
-            one = g[0:64, 256:384] + g[128:192, 0:128]
-            two = g[0:64, 0:128] + g[128:192, 128:256]
-            three = g[64:128, 0:128] + g[192:256, 128:256]
+                tiles += [src(2 * hp + b, 16, 128 * k, 128) for hp in range(2) for k in range(2)]
+            columns.append(jnp.concatenate(tiles, axis=0))
+        both = dot(d_ref[...], jnp.concatenate(columns, axis=1))
+        for j in range(len(columns)):
+            g = both[:, 128 * j : 128 * j + 128]
             pieces.append(
-                jnp.where(left, pltpu.roll(one, 32, 1), pltpu.roll(two, 32, 1)) + pltpu.roll(three, 96, 1)
+                jnp.where(left, pltpu.roll(g[128:192], 32, 1), pltpu.roll(g[0:64], 32, 1))
+                + pltpu.roll(g[64:128], 96, 1)
             )
     pieces.append(jnp.zeros((64, 128), F32))
-    clear_from(6 * PAIRS, keep_ref, send_ref)
     for k in range(PAIRS):
         both = jnp.concatenate([pieces[2 * k], pieces[2 * k + 1]], axis=0).T
         for j in range(6):
-            put_half(keep_ref, send_ref, 6 * k + j, both[16 * j : 16 * j + 16])
+            put_half(both_ref, 6 * k + j, both[16 * j : 16 * j + 16])
+    split_halves(6 * PAIRS, both_ref, keep_ref, send_ref)
 
 
 def features_kernel(n, kb_ref, other_ref, h_ref, h0_ref, *refs):
@@ -406,8 +439,9 @@
         outs[d][...] = piece_ref[(me + d) % n]
 
 
-def pair_kernel(keep_b, got_b, keep_a, got_a, out_ref):
-    out_ref[:, 0:64, :] = (keep_b[...] + got_b[...]).astype(BF)
+def pair_kernel(mine_b, got_b, keep_a, got_a, out_ref):
+    core = core_of()
+    out_ref[:, 0:64, :] = (mine_b[core] + got_b[core]).astype(BF)
     out_ref[:, 64:80, :] = (keep_a[...] + got_a[...]).astype(BF)
 
 
@@ -419,7 +453,7 @@
     tap = total[0:64] * scale_b
     rest = total[64:80] * scale_a
     for g in range(out_ref.shape[0]):
-        z = g % n
+        z = order(n)[g % n]
         out_ref[g, 0:chan, :] = tap[z * chan : z * chan + chan].astype(BF)
         out_ref[g, chan : chan + 16, :] = rest.astype(BF)
 
@@ -488,7 +522,7 @@
     shape = jax.ShapeDtypeStruct
     up = [(i, i + 1) for i in range(n - 1)]
     swap = [(i, i ^ 1) for i in range(dp)]
-    groups = [[(2 * k + c) * n + z for k in range(dp // 2) for z in range(n)] for c in range(2)]
+    groups = [[(2 * k + c) * n + z for k in range(dp // 2) for z in order(n)] for c in range(2)]
     peers = dp * n // 2
 
     def exchange(x):
@@ -521,58 +555,62 @@
         cost_estimate=cost(2),
     )(cotangent, kernel_b, halo)
     halo = lax.ppermute(halo, "mp", up)
-    cot = lax.all_to_all(packed, "mp", 0, 0, tiled=True)
+    cot = lax.all_to_all(packed, "mp", 0, 0, tiled=True, axis_index_groups=[order(n)])
     vd, hidden, pre = pl.pallas_call(
         first_kernel,
         out_shape=(
             pltpu.HBM((planes, 5, 144, 256), BF),
-            pltpu.HBM((hplanes, 3, 144, 256), BF),
+            pltpu.VMEM((hplanes, 3, 144, 256), BF),
             pltpu.VMEM((256, 256), F32),
         ),
         in_specs=[pl.BlockSpec(memory_space=pltpu.HBM), VMEM],
-        out_specs=(pl.BlockSpec(memory_space=pltpu.HBM), pl.BlockSpec(memory_space=pltpu.HBM), VMEM),
+        out_specs=(pl.BlockSpec(memory_space=pltpu.HBM), VMEM, VMEM),
         scratch_shapes=[
             pltpu.VMEM((planes // 4, 4, 64, 2048), BF),
             pltpu.VMEM((planes + 1, 5, 144, 256), BF),
-            pltpu.VMEM((hplanes, 3, 144, 256), BF),
             pltpu.VMEM((3456, 256), BF),
-            pltpu.SemaphoreType.DMA((planes // 4,)),
             pltpu.SemaphoreType.DMA((planes // 4,)),
             pltpu.SemaphoreType.DMA((planes // 4,)),
         ],
         compiler_params=params(24),
         cost_estimate=cost(100),
     )(volume, kernel_a)
-    cot, pre, halo = lax.optimization_barrier((cot, pre, halo))
+    hbm = pl.BlockSpec(memory_space=pltpu.HBM)
+    vdh, h0 = pl.pallas_call(
+        halo_kernel,
+        out_shape=(pltpu.HBM((5, 144, 256), BF), pltpu.VMEM((3, 144, 256), BF)),
+        in_specs=[VMEM, VMEM, VMEM],
+        out_specs=(hbm, VMEM),
+        scratch_shapes=[
+            pltpu.VMEM((5, 144, 256), BF),
+            pltpu.VMEM((1152, 256), BF),
+            pltpu.SemaphoreType.DMA,
+        ],
+        compiler_params=params(16),
+        cost_estimate=cost(10),
+    )(halo, kernel_a, pre)
+    cot, h0 = lax.optimization_barrier((cot, h0))
     kb_other = lax.ppermute(cot, "dp", swap)
 
-    vdh, h0, c, keep_b, send_b = call(
+    c, mine_b = call(
         functools.partial(grad_b_kernel, n),
-        (
-            pltpu.VMEM((5, 144, 256), BF),
-            pltpu.VMEM((3, 144, 256), BF),
-            pltpu.VMEM((slab + 1, 2, 144, 256), BF),
-            pltpu.VMEM((peers, 64, 128), F32),
-            pltpu.VMEM((peers, 64, 128), F32),
-        ),
-        [VMEM, VMEM, VMEM, pl.BlockSpec(memory_space=pltpu.HBM), VMEM],
+        (pltpu.VMEM((slab + 1, 2, 144, 256), BF), pltpu.VMEM((2, peers, 64, 128), F32)),
         3,
-        [pltpu.VMEM((1152, 256), BF), pltpu.VMEM((hplanes, 3, 144, 256), BF), pltpu.SemaphoreType.DMA],
-        16,
-    )(halo, kernel_a, pre, pltpu.with_memory_space_constraint(hidden, pltpu.HBM), cot)
-    got_b = lax.ppermute(send_b, "dp", swap)
+        3,
+    )(hidden, h0, cot)
+    got_b = lax.ppermute(mine_b, "dp", swap)
 
     keep_a, send_a = call(
         functools.partial(grad_a_kernel, n),
         (shape((peers, 16, 128), F32), shape((peers, 16, 128), F32)),
         7,
         8,
-        [pltpu.VMEM((3456, 256), BF), pltpu.VMEM((256, hplanes * 256), BF)],
+        [pltpu.VMEM((3456, 256), BF), pltpu.VMEM((192, hplanes * 512), BF), pltpu.VMEM((2, peers, 16, 128), F32)],
         24,
     )(cot, kb_other, hidden, h0, c, vd, vdh)
     got_a = lax.ppermute(send_a, "dp", swap)
 
-    sums = call(pair_kernel, shape((peers, 80, 128), BF), 4, 1)(keep_b, got_b, keep_a, got_a)
+    sums = call(pair_kernel, pltpu.VMEM((peers, 80, 128), BF), 4, 1)(mine_b, got_b, keep_a, got_a)
     sums = exchange(sums)
 
     pieces = call(
@@ -585,16 +623,24 @@
             pltpu.VMEM((3456, 256), BF),
         ],
     )(cot, kb_other, hidden, h0)
+    pieces = list(pieces)
+    early = (1,)
+
+    def send(d):
+        pieces[d] = lax.ppermute(pieces[d], "mp", [(i, (i + d) % n) for i in range(n)])
+
+    for d in early:
+        send(d)
     sums, *pieces = lax.optimization_barrier((sums, *pieces))
-    pieces = [pieces[0]] + [
-        lax.ppermute(pieces[d], "mp", [(i, (i + d) % n) for i in range(n)]) for d in range(1, n)
-    ]
+    for d in range(1, n):
+        if d not in early:
+            send(d)
 
     samples = volume.shape[0] * dp
     scale_a = 1 / math.sqrt(samples * (GRID // 2) ** 3)
     scale_b = 1 / math.sqrt(samples * (GRID // 4) ** 3)
     mine = call(
-        functools.partial(sum_kernel, n, scale_a, scale_b), shape((peers, chan_b + 16, 128), BF), 1, 1
+        functools.partial(sum_kernel, n, scale_a, scale_b), pltpu.VMEM((peers, chan_b + 16, 128), BF), 1, 1
     )(sums)
     mine = exchange(mine)
     mine, *pieces = lax.optimization_barrier((mine, *pieces))

time: 77.7 us -> 70.9 us (0.912)
  waiting for transfers between devices: 22.4 us -> 17.5 us
  Pallas kernels: 29.8 us -> 26.1 us
  starting transfers between devices: 23.3 us -> 24.9 us
    all_to_all x2, waiting for transfers between devices: 9.6 us -> 1.54 us  [exchange(): lax.all_to_all(x, ('dp', 'mp'), 0, 0, tiled=True, axis_index_groups=groups)]
    ppermute x4, waiting for transfers between devices: 5.77 us -> 12.7 us  [the longest x3 12.7 us: send(): lax.ppermute(pieces[d], 'mp', [(i, (i + d) % n) for i in range(n)])]
    all_to_all x1, waiting for transfers between devices: 5.66 us -> 2.25 us  [shards(): lax.all_to_all(packed, 'mp', 0, 0, tiled=True, axis_index_groups=[order(n)])]
    ppermute x4, starting transfers between devices: 6.21 us -> 3.26 us  [the longest x3 2.68 us: send(): lax.ppermute(pieces[d], 'mp', [(i, (i + d) % n) for i in range(n)])]
    all_to_all x2, starting transfers between devices: 8.24 us -> 11.1 us  [exchange(): lax.all_to_all(x, ('dp', 'mp'), 0, 0, tiled=True, axis_index_groups=groups)]
    pallas_call x1, Pallas kernels: 6.82 us -> 4.87 us  [shards(): call(functools.partial(grad_a_kernel, n), (shape((peers, 16, 128), F32),...]
    all_to_all x1, starting transfers between devices: 3.85 us -> 5.01 us  [shards(): lax.all_to_all(packed, 'mp', 0, 0, tiled=True, axis_index_groups=[order(n)])]
    pallas_call x3 -> x4, Pallas kernels: 5.35 us -> 4.36 us  [the longest x1 1.81 us: shards(): call(functools.partial(grad_b_kernel, n), (pltpu.VMEM((slab + 1, 2, 144,...]
  transfers between devices with their start and end apart: 11 -> 11, of which waited for: 6 -> 5; matrix products, arithmetic and copies ran while one was open for 0% -> 0% of each run, Pallas kernels for 34% -> 32%
where the time goes in v3:
time: 70.9 us; the launch traced here: 70.4 us
  Pallas kernels  26.1 us (37%)
  starting transfers between devices  24.9 us (35%)
  waiting for transfers between devices  17.5 us (25%)
  local copies, waits for them, and re-layouts  1.25 us (2%)
  between operations  0.73 us (1%)
    ppermute x3, waiting for transfers between devices, send(): lax.ppermute(pieces[d], 'mp', [(i, (i + d) % n) for i in range(n)])  12.7 us
    all_to_all x2, starting transfers between devices, exchange(): lax.all_to_all(x, ('dp', 'mp'), 0, 0, tiled=True, axis_index_groups=groups)  11.1 us
    pallas_call x1, Pallas kernels, shards(): pl.pallas_call(first_kernel, out_shape=(pltpu.HBM((planes, 5, 144, 256),...  8.45 us
    all_to_all x1, starting transfers between devices, shards(): lax.all_to_all(packed, 'mp', 0, 0, tiled=True, axis_index_groups=[order(n)])  5.01 us
    ppermute x1, starting transfers between devices, shards(): halo = lax.ppermute(halo, 'mp', up)  4.94 us
    pallas_call x1, Pallas kernels, shards(): call(functools.partial(grad_a_kernel, n), (shape((peers, 16, 128), F32),...  4.87 us
    pallas_call x1, Pallas kernels, shards(): pl.pallas_call(functools.partial(pack_kernel, n), grid=(1,), out_shape=sh...  2.85 us
    ppermute x3, starting transfers between devices, send(): lax.ppermute(pieces[d], 'mp', [(i, (i + d) % n) for i in range(n)])  2.68 us
  transfers between devices with their start and end apart: 11, of which 5 were waited for; matrix products, arithmetic and copies ran while one was open for 0% of the time, Pallas kernels for 32%

profile of v3, /device:TPU:0, one launch (start us, length us, event | category | flops | bytes accessed | tf_op | source)
XLA Modules:
  0.0 70.4 jit_solution(2493094759559436568)
XLA Ops:
  0.6 1.0 %shard_map.68.after_ref = bf16[64,2048]{1,0:T(8,128)(2,1)S(1)} custom-call(bf16[1,16,64,2048]{3,2,1,0:T(8,128)(2,1)} %vol_ref.3), custom_call_target="tpu_custom_call" | custom-call | flops 1000000000 | bytes 3000000 | tf_op jit(solution)/shard_map/pallas_call | solution.py:535
  1.6 4.9 %collective-permute-start = (bf16[64,2048]{1,0:T(8,128)(2,1)S(1)}, bf16[64,2048]{1,0:T(8,128)(2,1)S(1)}, u32[]{:S(2)}, u32[]{:S(2)}) collective-permute-start(bf16[64,2048]{1,0:T(8,128)(2,1)S(1)} %shard_map.68.after_ref), channel_id=1, source_target_pairs={{0,8},{8,16},{16,24},{1,9},{9,17},{17,25},{2,10},{10,18},{18,26},{... | collective-permute-start | bytes 786440 | tf_op jit(solution)/shard_map/ppermute | solution.py:557
  6.5 0.0 copy-start
  6.6 2.8 %shard_map.69 = bf16[4,544,128]{2,1,0:T(8,128)(2,1)} custom-call(bf16[1,16,16,16,32]{4,3,2,1,0:T(8,128)(2,1)} %cot_ref.1, bf16[27,16,128]{2,1,0:T(8,128)(2,1)} %bitcast.2, bf16[64,2048]{1,0:T(8,128)(2,1)S(1)} %shard_map.68.after_ref), custom_call_target="tpu_custom_call" | custom-call | flops 2000000000 | bytes 6000000 | tf_op jit(solution)/shard_map/pallas_call | solution.py:544
  9.4 5.0 %all-to-all-start = ((bf16[4,544,128]{2,1,0:T(8,128)(2,1)}), bf16[4,544,128]{2,1,0:T(8,128)(2,1)S(1)}, u32[]{:S(2)}, u32[]{:S(2)}) async-start(bf16[4,544,128]{2,1,0:T(8,128)(2,1)} %shard_map.69), calls=%async_computation | async-start | bytes 1114112 | tf_op jit(solution)/shard_map/all_to_all | solution.py:558
  14.4 0.0 copy-done
  14.4 8.5 %shard_map.67 = (bf16[16,5,144,256]{3,2,1,0:T(8,128)(2,1)}, bf16[8,3,144,256]{3,2,1,0:T(8,128)(2,1)S(1)}, f32[256,256]{1,0:T(8,128)S(1)}) custom-call(bf16[1,16,64,2048]{3,2,1,0:T(8,128)(2,1)} %vol_ref.3, bf16[3,3,3,32,64]{4,3,2,1,0:T(8,128)(2,1)S(1)} %copy-done), custom_call_target="tpu_custom_call" | custom-call | flops 99999997952 | bytes 300000000 | tf_op jit(solution)/shard_map/pallas_call | solution.py:559
  22.9 0.0 collective-permute-done.halo_ref
  22.9 1.1 %shard_map.70 = (bf16[5,144,256]{2,1,0:T(8,128)(2,1)}, bf16[3,144,256]{2,1,0:T(8,128)(2,1)S(1)}) custom-call(bf16[64,2048]{1,0:T(8,128)(2,1)S(1)} %collective-permute-done.halo_ref, bf16[3,3,3,32,64]{4,3,2,1,0:T(8,128)(2,1)S(1)} %copy-done, f32[256,256]{1,0:T(8,128)S(1)} %get-tuple-element.31.pre_ref), custom_call_target="tpu_custom_call" | custom-call | flops 10000000000 | bytes 30000000 | tf_op jit(solution)/shard_map/pallas_call | solution.py:579
  24.0 0.0 copy-start.2
  24.0 2.2 %all-to-all-done.cot_ref.kb_ref = bf16[4,544,128]{2,1,0:T(8,128)(2,1)S(1)} async-done(((bf16[4,544,128]{2,1,0:T(8,128)(2,1)}), bf16[4,544,128]{2,1,0:T(8,128)(2,1)S(1)}, u32[]{:S(2)}, u32[]{:S(2)}) %all-to-all-start) | async-done | bytes 557088 | tf_op jit(solution)/shard_map/all_to_all | solution.py:558
  26.2 0.0 collective-permute-start.2
  26.2 0.0 copy-start.1
  26.2 0.0 copy-start.4
  26.2 1.8 %shard_map.71 = (bf16[5,2,144,256]{3,2,1,0:T(8,128)(2,1)S(1)}, f32[2,16,64,128]{3,2,1,0:T(8,128)S(1)}) custom-call(bf16[8,3,144,256]{3,2,1,0:T(8,128)(2,1)S(1)} %get-tuple-element.30.h_ref, bf16[3,144,256]{2,1,0:T(8,128)(2,1)S(1)} %get-tuple-element.33.h0_ref, bf16[4,544,128]{2,1,0:T(8,128)(2,1)S(1)} %all-to-all-done.cot_ref.kb_ref), custom_call_target="tpu_custom_call" | custom-call | flops 3000000000 | bytes 9000000 | tf_op jit(solution)/shard_map/pallas_call | solution.py:595
  28.0 0.6 collective-permute-start.1
  28.6 0.0 collective-permute-done.2.other_ref
  28.6 0.0 copy-done.2
  28.6 0.3 copy-done.1
  28.9 0.0 copy-done.4
  28.9 4.9 %shard_map.72 = (f32[16,16,128]{2,1,0:T(8,128)S(1)}, f32[16,16,128]{2,1,0:T(8,128)S(1)}) custom-call(bf16[4,544,128]{2,1,0:T(8,128)(2,1)S(1)} %all-to-all-done.cot_ref.kb_ref, bf16[4,544,128]{2,1,0:T(8,128)(2,1)S(1)} %collective-permute-done.2.other_ref, bf16[8,3,144,256]{3,2,1,0:T(8,128)(2,1)S(1)} %get-tuple-element.30.h_ref, ...), custom_call_target="tpu_custom_call" | custom-call | flops 8000000000 | bytes 24000000 | tf_op jit(solution)/shard_map/pallas_call | solution.py:603
  33.8 0.6 collective-permute-start.3
  34.4 1.0 %collective-permute-done.3.got_a = f32[16,16,128]{2,1,0:T(8,128)S(1)} collective-permute-done((f32[16,16,128]{2,1,0:T(8,128)S(1)}, f32[16,16,128]{2,1,0:T(8,128)S(1)}, u32[]{:S(2)}, u32[]{:S(2)}) %collective-permute-start.3) | collective-permute-done | bytes 131104 | tf_op jit(solution)/shard_map/ppermute | solution.py:611
  35.4 0.0 collective-permute-done.1.got_b
  35.4 0.8 %shard_map.73 = bf16[16,80,128]{2,1,0:T(8,128)(2,1)} custom-call(f32[2,16,64,128]{3,2,1,0:T(8,128)S(1)} %get-tuple-element.35.mine_b, f32[2,16,64,128]{3,2,1,0:T(8,128)S(1)} %collective-permute-done.1.got_b, f32[16,16,128]{2,1,0:T(8,128)S(1)} %get-tuple-element.39.keep_a, f32[16,16,128]{2,1,0:T(8,128)S(1)} %collective-permute-done.3.got_a), custom_call_target="tpu_custom_call" | custom-call | flops 1000000000 | bytes 3000000 | tf_op jit(solution)/shard_map/pallas_call | solution.py:613
  36.1 6.9 %all-to-all-start.1 = ((bf16[16,80,128]{2,1,0:T(8,128)(2,1)}), bf16[16,80,128]{2,1,0:T(8,128)(2,1)S(1)}, u32[]{:S(2)}, u32[]{:S(2)}) async-start(bf16[16,80,128]{2,1,0:T(8,128)(2,1)} %shard_map.73), calls=%async_computation.1 | async-start | bytes 655360 | tf_op jit(solution)/shard_map/all_to_all | solution.py:529
  43.0 0.0 copy-start.3
  43.0 0.9 %copy-done.3 = bf16[3,144,256]{2,1,0:T(8,128)(2,1)S(1)} copy-done((bf16[3,144,256]{2,1,0:T(8,128)(2,1)S(1)}, bf16[3,144,256]{2,1,0:T(8,128)(2,1)}, u32[]{:S(2)}) %copy-start.3) | copy-done | bytes 221208
  44.0 1.9 %shard_map.74 = (bf16[320,128]{1,0:T(8,128)(2,1)S(1)}, bf16[320,128]{1,0:T(8,128)(2,1)S(1)}, bf16[320,128]{1,0:T(8,128)(2,1)S(1)}, bf16[320,128]{1,0:T(8,128)(2,1)S(1)}) custom-call(bf16[4,544,128]{2,1,0:T(8,128)(2,1)S(1)} %all-to-all-done.cot_ref.kb_ref, bf16[4,544,128]{2,1,0:T(8,128)(2,1)S(1)} %collective-permute-done.2.other_ref, ...), custom_call_target="tpu_custom_call" | custom-call | flops 4000000000 | bytes 12000000 | tf_op jit(solution)/shard_map/pallas_call | solution.py:616
  45.9 0.2 collective-permute-start.4
  46.1 7.2 %collective-permute-done.4.refs_1_ = bf16[320,128]{1,0:T(8,128)(2,1)S(1)} collective-permute-done((bf16[320,128]{1,0:T(8,128)(2,1)S(1)}, bf16[320,128]{1,0:T(8,128)(2,1)S(1)}, u32[]{:S(2)}, u32[]{:S(2)}) %collective-permute-start.4) | collective-permute-done | bytes 81952 | tf_op jit(solution)/shard_map/ppermute | solution.py:630
  53.3 1.5 %all-to-all-done.1.in_ref = bf16[16,80,128]{2,1,0:T(8,128)(2,1)S(1)} async-done(((bf16[16,80,128]{2,1,0:T(8,128)(2,1)}), bf16[16,80,128]{2,1,0:T(8,128)(2,1)S(1)}, u32[]{:S(2)}, u32[]{:S(2)}) %all-to-all-start.1) | async-done | bytes 327712 | tf_op jit(solution)/shard_map/all_to_all | solution.py:529
  54.8 0.7 %shard_map.75 = bf16[16,32,128]{2,1,0:T(8,128)(2,1)} custom-call(bf16[16,80,128]{2,1,0:T(8,128)(2,1)S(1)} %all-to-all-done.1.in_ref), custom_call_target="tpu_custom_call" | custom-call | flops 1000000000 | bytes 3000000 | tf_op jit(solution)/shard_map/pallas_call | solution.py:642
  55.5 4.2 %all-to-all-start.2 = ((bf16[16,32,128]{2,1,0:T(8,128)(2,1)}), bf16[16,32,128]{2,1,0:T(8,128)(2,1)S(1)}, u32[]{:S(2)}, u32[]{:S(2)}) async-start(bf16[16,32,128]{2,1,0:T(8,128)(2,1)} %shard_map.75), calls=%async_computation.2 | async-start | bytes 262144 | tf_op jit(solution)/shard_map/all_to_all | solution.py:529
  59.7 1.5 %collective-permute-start.5 = (bf16[320,128]{1,0:T(8,128)(2,1)S(1)}, bf16[320,128]{1,0:T(8,128)(2,1)S(1)}, u32[]{:S(2)}, u32[]{:S(2)}) collective-permute-start(bf16[320,128]{1,0:T(8,128)(2,1)S(1)} %get-tuple-element.48), channel_id=1, source_target_pairs={{0,16},{8,24},{16,0},{24,8},{1,17},{9,25},{17,1},{25,9},{2,18},{10... | collective-permute-start | bytes 245768 | tf_op jit(solution)/shard_map/ppermute | solution.py:630
  61.2 1.1 %collective-permute-start.6 = (bf16[320,128]{1,0:T(8,128)(2,1)S(1)}, bf16[320,128]{1,0:T(8,128)(2,1)S(1)}, u32[]{:S(2)}, u32[]{:S(2)}) collective-permute-start(bf16[320,128]{1,0:T(8,128)(2,1)S(1)} %get-tuple-element.49), channel_id=1, source_target_pairs={{0,24},{8,0},{16,8},{24,16},{1,25},{9,1},{17,9},{25,17},{2,26},{10... | collective-permute-start | bytes 245768 | tf_op jit(solution)/shard_map/ppermute | solution.py:630
  62.2 5.5 %collective-permute-done.5.refs_2_ = bf16[320,128]{1,0:T(8,128)(2,1)S(1)} collective-permute-done((bf16[320,128]{1,0:T(8,128)(2,1)S(1)}, bf16[320,128]{1,0:T(8,128)(2,1)S(1)}, u32[]{:S(2)}, u32[]{:S(2)}) %collective-permute-start.5) | collective-permute-done | bytes 81952 | tf_op jit(solution)/shard_map/ppermute | solution.py:630
  67.7 0.0 collective-permute-done.6.refs_3_
  67.7 0.0 all-to-all-done.2.mine_ref
  67.7 0.0 collective-permute-start.7
  67.8 1.8 %shard_map.76 = bf16[1,16,16,16,32]{4,3,2,1,0:T(8,128)(2,1)} custom-call(bf16[320,128]{1,0:T(8,128)(2,1)S(1)} %get-tuple-element.50.refs_0_, bf16[320,128]{1,0:T(8,128)(2,1)S(1)} %collective-permute-done.4.refs_1_, bf16[320,128]{1,0:T(8,128)(2,1)S(1)} %collective-permute-done.5.refs_2_, bf16[320,128]{1,0:T(8,128)(2,1)S(1)} %collective-permute-done.6.refs_3_), custom_call_target="tpu_custom_call" | custom-call | flops 2000000000 | bytes 6000000 | tf_op jit(solution)/shard_map/pallas_call | solution.py:649
  69.5 0.0 collective-permute-done.7.other_ref
  69.5 0.9 %shard_map.77 = (f32[3,3,3,32,64]{4,3,2,1,0:T(8,128)}, f32[27,16,128]{2,1,0:T(8,128)}) custom-call(bf16[16,32,128]{2,1,0:T(8,128)(2,1)S(1)} %all-to-all-done.2.mine_ref, bf16[16,32,128]{2,1,0:T(8,128)(2,1)S(1)} %collective-permute-done.7.other_ref), custom_call_target="tpu_custom_call" | custom-call | flops 1000000000 | bytes 3000000 | tf_op jit(solution)/shard_map/pallas_call | solution.py:650
Async XLA Ops:
  1.6 21.3 %collective-permute-start = (bf16[64,2048]{1,0:T(8,128)(2,1)S(1)}, bf16[64,2048]{1,0:T(8,128)(2,1)S(1)}, u32[]{:S(2)}, u32[]{:S(2)}) collective-permute-start(bf16[64,2048]{1,0:T(8,128)(2,1)S(1)} %shard_map.68.after_ref), channel_id=1, source_target_pairs={{0,8},{8,16},{16,24},{1,9},{9,17},{17,25},{2,10},{10,18},{18,26},{... | collective-permute-start | bytes 786440 | tf_op jit(solution)/shard_map/ppermute | solution.py:557
  6.5 7.9 %copy-start = (bf16[3,3,3,32,64]{4,3,2,1,0:T(8,128)(2,1)S(1)}, bf16[3,3,3,32,64]{4,3,2,1,0:T(8,128)(2,1)}, u32[]{:S(2)}) copy-start(bf16[3,3,3,32,64]{4,3,2,1,0:T(8,128)(2,1)} %ka_ref.3) | copy-start | bytes 331780
  9.4 16.8 %all-to-all-start = ((bf16[4,544,128]{2,1,0:T(8,128)(2,1)}), bf16[4,544,128]{2,1,0:T(8,128)(2,1)S(1)}, u32[]{:S(2)}, u32[]{:S(2)}) async-start(bf16[4,544,128]{2,1,0:T(8,128)(2,1)} %shard_map.69), calls=%async_computation | async-start | bytes 1114112 | tf_op jit(solution)/shard_map/all_to_all | solution.py:558
  24.0 4.7 %copy-start.2 = (bf16[3,144,256]{2,1,0:T(8,128)(2,1)}, bf16[3,144,256]{2,1,0:T(8,128)(2,1)S(1)}, u32[]{:S(2)}) copy-start(bf16[3,144,256]{2,1,0:T(8,128)(2,1)S(1)} %get-tuple-element.33.h0_ref) | copy-start | bytes 663556
  26.2 2.4 %collective-permute-start.2 = (bf16[4,544,128]{2,1,0:T(8,128)(2,1)S(1)}, bf16[4,544,128]{2,1,0:T(8,128)(2,1)S(1)}, u32[]{:S(2)}, u32[]{:S(2)}) collective-permute-start(bf16[4,544,128]{2,1,0:T(8,128)(2,1)S(1)} %all-to-all-done.cot_ref.kb_ref), channel_id=1, source_target_pairs={{0,1},{1,0},{2,3},{3,2},{4,5},{5,4},{6,7},{7,6},{8,9},{9,8},{10,11... | collective-permute-start | bytes 1671176 | tf_op jit(solution)/shard_map/ppermute | solution.py:593
  26.2 2.7 %copy-start.1 = (bf16[16,5,144,256]{3,2,1,0:T(8,128)(2,1)S(1)}, bf16[16,5,144,256]{3,2,1,0:T(8,128)(2,1)}, u32[]{:S(2)}) copy-start(bf16[16,5,144,256]{3,2,1,0:T(8,128)(2,1)} %get-tuple-element.37.vd_ref) | copy-start | bytes 17694724
  26.2 2.7 %copy-start.4 = (bf16[5,144,256]{2,1,0:T(8,128)(2,1)S(1)}, bf16[5,144,256]{2,1,0:T(8,128)(2,1)}, u32[]{:S(2)}) copy-start(bf16[5,144,256]{2,1,0:T(8,128)(2,1)} %get-tuple-element.38.vdh_ref) | copy-start | bytes 1105924
  28.0 7.3 %collective-permute-start.1 = (f32[2,16,64,128]{3,2,1,0:T(8,128)S(1)}, f32[2,16,64,128]{3,2,1,0:T(8,128)S(1)}, u32[]{:S(2)}, u32[]{:S(2)}) collective-permute-start(f32[2,16,64,128]{3,2,1,0:T(8,128)S(1)} %get-tuple-element.35.mine_b), channel_id=1, source_target_pairs={{0,1},{1,0},{2,3},{3,2},{4,5},{5,4},{6,7},{7,6},{8,9},{9,8},{10,11... | collective-permute-start | bytes 3145736 | tf_op jit(solution)/shard_map/ppermute | solution.py:601
  33.8 1.6 %collective-permute-start.3 = (f32[16,16,128]{2,1,0:T(8,128)S(1)}, f32[16,16,128]{2,1,0:T(8,128)S(1)}, u32[]{:S(2)}, u32[]{:S(2)}) collective-permute-start(f32[16,16,128]{2,1,0:T(8,128)S(1)} %get-tuple-element.40), channel_id=1, source_target_pairs={{0,1},{1,0},{2,3},{3,2},{4,5},{5,4},{6,7},{7,6},{8,9},{9,8},{10,11... | collective-permute-start | bytes 393224 | tf_op jit(solution)/shard_map/ppermute | solution.py:611
  36.1 18.6 %all-to-all-start.1 = ((bf16[16,80,128]{2,1,0:T(8,128)(2,1)}), bf16[16,80,128]{2,1,0:T(8,128)(2,1)S(1)}, u32[]{:S(2)}, u32[]{:S(2)}) async-start(bf16[16,80,128]{2,1,0:T(8,128)(2,1)} %shard_map.73), calls=%async_computation.1 | async-start | bytes 655360 | tf_op jit(solution)/shard_map/all_to_all | solution.py:529
  43.0 0.9 %copy-start.3 = (bf16[3,144,256]{2,1,0:T(8,128)(2,1)S(1)}, bf16[3,144,256]{2,1,0:T(8,128)(2,1)}, u32[]{:S(2)}) copy-start(bf16[3,144,256]{2,1,0:T(8,128)(2,1)} %copy-done.2) | copy-start | bytes 663556
  45.9 7.4 %collective-permute-start.4 = (bf16[320,128]{1,0:T(8,128)(2,1)S(1)}, bf16[320,128]{1,0:T(8,128)(2,1)S(1)}, u32[]{:S(2)}, u32[]{:S(2)}) collective-permute-start(bf16[320,128]{1,0:T(8,128)(2,1)S(1)} %get-tuple-element.42), channel_id=1, source_target_pairs={{0,8},{8,16},{16,24},{24,0},{1,9},{9,17},{17,25},{25,1},{2,10},{10... | collective-permute-start | bytes 245768 | tf_op jit(solution)/shard_map/ppermute | solution.py:630
  55.5 12.2 %all-to-all-start.2 = ((bf16[16,32,128]{2,1,0:T(8,128)(2,1)}), bf16[16,32,128]{2,1,0:T(8,128)(2,1)S(1)}, u32[]{:S(2)}, u32[]{:S(2)}) async-start(bf16[16,32,128]{2,1,0:T(8,128)(2,1)} %shard_map.75), calls=%async_computation.2 | async-start | bytes 262144 | tf_op jit(solution)/shard_map/all_to_all | solution.py:529
  59.7 8.0 %collective-permute-start.5 = (bf16[320,128]{1,0:T(8,128)(2,1)S(1)}, bf16[320,128]{1,0:T(8,128)(2,1)S(1)}, u32[]{:S(2)}, u32[]{:S(2)}) collective-permute-start(bf16[320,128]{1,0:T(8,128)(2,1)S(1)} %get-tuple-element.48), channel_id=1, source_target_pairs={{0,16},{8,24},{16,0},{24,8},{1,17},{9,25},{17,1},{25,9},{2,18},{10... | collective-permute-start | bytes 245768 | tf_op jit(solution)/shard_map/ppermute | solution.py:630
  61.2 6.6 %collective-permute-start.6 = (bf16[320,128]{1,0:T(8,128)(2,1)S(1)}, bf16[320,128]{1,0:T(8,128)(2,1)S(1)}, u32[]{:S(2)}, u32[]{:S(2)}) collective-permute-start(bf16[320,128]{1,0:T(8,128)(2,1)S(1)} %get-tuple-element.49), channel_id=1, source_target_pairs={{0,24},{8,0},{16,8},{24,16},{1,25},{9,1},{17,9},{25,17},{2,26},{10... | collective-permute-start | bytes 245768 | tf_op jit(solution)/shard_map/ppermute | solution.py:630
  67.7 1.8 %collective-permute-start.7 = (bf16[16,32,128]{2,1,0:T(8,128)(2,1)S(1)}, bf16[16,32,128]{2,1,0:T(8,128)(2,1)S(1)}, u32[]{:S(2)}, u32[]{:S(2)}) collective-permute-start(bf16[16,32,128]{2,1,0:T(8,128)(2,1)S(1)} %all-to-all-done.2.mine_ref), channel_id=1, source_target_pairs={{0,1},{1,0},{2,3},{3,2},{4,5},{5,4},{6,7},{7,6},{8,9},{9,8},{10,11... | collective-permute-start | bytes 393224 | tf_op jit(solution)/shard_map/ppermute | solution.py:647

commit v4 on v3

--- a/solution.py
+++ b/solution.py
@@ -160,14 +160,6 @@
         flush(i).wait()
 
 
-def order(n):
-    return sorted(range(n), key=lambda z: abs(2 * z - (n - 1)))
-
-
-def place(n, z):
-    return order(n).index(z)
-
-
 def core_of():
     return lax.axis_index("dp") % 2
 
@@ -178,8 +170,9 @@
     copy.wait()
 
 
-def pack_kernel(n, cot_ref, kb_ref, after_ref, out_ref):
+def pack_kernel(n, cot_ref, kb_ref, after_ref, *refs):
     del after_ref
+    outs, full_ref = refs[:n], refs[n]
     chan = cot_ref.shape[4]
     lanes = 128 // chan
     rows = 256 // lanes
@@ -193,17 +186,27 @@
         z = jnp.concatenate([y[rows * l : rows * l + rows] for l in range(lanes)], axis=1).astype(BF)
         t = p // per
         at = (p % per) * rows
-        out_ref[place(n, t), at : at + rows, :] = z
+        full_ref[t, at : at + rows, :] = z
         if p % per == 0 and t > 0:
-            out_ref[place(n, t - 1), per * rows : per * rows + rows, :] = z
-    out_ref[place(n, n - 1), per * rows : per * rows + rows, :] = jnp.zeros((rows, 128), BF)
+            full_ref[t - 1, per * rows : per * rows + rows, :] = z
+    full_ref[n - 1, per * rows : per * rows + rows, :] = jnp.zeros((rows, 128), BF)
+    me = lax.axis_index("mp")
     first = 13 * core_of()
     size = kb_ref.shape[1]
-    for j in range(HALF):
-        v = kb_ref[first + j]
-        at = (per + 1) * rows + size * j
-        for t in range(n):
-            out_ref[t, at : at + size, :] = v
+    head = (per + 1) * rows
+    for d in range(n):
+        outs[d][0:head, :] = full_ref[(me + d) % n]
+        for j in range(HALF):
+            outs[d][head + size * j : head + size * j + size, :] = kb_ref[first + j]
+
+
+def gather_kernel(n, *refs):
+    pieces, (cot_ref, kb_ref) = refs[:n], refs[n:]
+    head, tail = cot_ref.shape[1], kb_ref.shape[1]
+    me = lax.axis_index("mp")
+    for d in range(n):
+        cot_ref[(me + n - d) % n] = pieces[d][0:head, :]
+        kb_ref[(me + n - d) % n] = pieces[d][head : head + tail, :]
 
 
 def lane_order(n, inverse):
@@ -272,7 +275,7 @@
     slab = 16 // n
     lanes = n
     rows = 256 // lanes
-    wide = jnp.concatenate([cot_ref[place(n, t), 0 : (slab + 1) * rows, :] for t in range(n)], axis=1)
+    wide = jnp.concatenate([cot_ref[t] for t in range(n)], axis=1)
     turned = dot(wide, lane_order(n, False))
     turns = []
     for p in range(slab + 1):
@@ -315,15 +318,14 @@
 
 def second_taps(n, kb_ref, other_ref):
     chan = 64 // n
-    start = (16 // n + 1) * (256 // n)
     first = core_of() == 0
 
     def tap(k):
         j, own_first = (k, True) if k < 13 else (k - 13, False)
         parts = []
         for z in range(n):
-            own = kb_ref[place(n, z), start + j * chan : start + j * chan + chan, :]
-            other = other_ref[place(n, z), start + j * chan : start + j * chan + chan, :]
+            own = kb_ref[z, j * chan : j * chan + chan, :]
+            other = other_ref[z, j * chan : j * chan + chan, :]
             pair = (own, other) if own_first else (other, own)
             parts.append(jnp.where(first, *pair))
         return jnp.concatenate(parts, axis=0)
@@ -439,23 +441,51 @@
         outs[d][...] = piece_ref[(me + d) % n]
 
 
-def pair_kernel(mine_b, got_b, keep_a, got_a, out_ref):
+def per_column(columns):
+    return -(-14 // columns), -(-15 // columns)
+
+
+def pair_kernel(columns, mine_b, got_b, keep_a, got_a, *outs):
+    taps, chunks = per_column(columns)
     core = core_of()
-    out_ref[:, 0:64, :] = (mine_b[core] + got_b[core]).astype(BF)
-    out_ref[:, 64:80, :] = (keep_a[...] + got_a[...]).astype(BF)
-
-
-def sum_kernel(n, scale_a, scale_b, in_ref, out_ref):
+    k = lax.axis_index("dp") // 2
+    for m in range(columns):
+        to = jnp.bitwise_xor(k, m)
+        for s in range(taps):
+            j = to * taps + s
+            outs[m][64 * s : 64 * s + 64, :] = (mine_b[core, j] + got_b[core, j]).astype(BF)
+        for s in range(chunks):
+            j = to * chunks + s
+            at = 64 * taps + 16 * s
+            outs[m][at : at + 16, :] = (keep_a[j] + got_a[j]).astype(BF)
+
+
+def column_sum_kernel(n, columns, *refs):
+    ins, outs, piece_ref = refs[:columns], refs[columns : columns + n], refs[columns + n]
+    taps, chunks = per_column(columns)
     chan = 64 // n
-    total = in_ref[0].astype(F32)
-    for k in range(1, in_ref.shape[0]):
-        total = total + in_ref[k].astype(F32)
-    tap = total[0:64] * scale_b
-    rest = total[64:80] * scale_a
-    for g in range(out_ref.shape[0]):
-        z = order(n)[g % n]
-        out_ref[g, 0:chan, :] = tap[z * chan : z * chan + chan].astype(BF)
-        out_ref[g, chan : chan + 16, :] = rest.astype(BF)
+    total = ins[0][...].astype(F32)
+    for m in range(1, columns):
+        total = total + ins[m][...].astype(F32)
+    total = total.astype(BF)
+    for z in range(n):
+        for s in range(taps):
+            at = 64 * s + chan * z
+            piece_ref[z, chan * s : chan * s + chan, :] = total[at : at + chan]
+        piece_ref[z, chan * taps :, :] = total[64 * taps :]
+    me = lax.axis_index("mp")
+    for d in range(n):
+        outs[d][...] = piece_ref[(me + d) % n]
+
+
+def slab_sum_kernel(n, columns, scale_a, scale_b, *refs):
+    ins, out_ref = refs[:n], refs[n]
+    split = 64 // n * per_column(columns)[0]
+    total = ins[0][...].astype(F32)
+    for d in range(1, n):
+        total = total + ins[d][...].astype(F32)
+    out_ref[0:split, :] = (total[0:split] * scale_b).astype(BF)
+    out_ref[split:, :] = (total[split:] * scale_a).astype(BF)
 
 
 def unpack_kernel(n, *refs):
@@ -480,17 +510,23 @@
             out_ref[0, first + p] = dot(pick, x).astype(BF).reshape(16, 16, chan)
 
 
-def last_kernel(mine_ref, other_ref, a_ref, b_ref):
+def last_kernel(columns, *refs):
+    mine, other, (a_ref, b_ref, chunk_ref, tap_ref) = refs[:columns], refs[columns : 2 * columns], refs[2 * columns :]
+    taps, chunks = per_column(columns)
     chan = b_ref.shape[1]
-    first = core_of() == 0
+    core = core_of()
+    k = lax.axis_index("dp") // 2
+    for m in range(columns):
+        owner = jnp.bitwise_xor(k, m)
+        for piece, c in ((mine[m], core), (other[m], 1 - core)):
+            for s in range(taps):
+                tap_ref[2 * (owner * taps + s) + c] = piece[chan * s : chan * s + chan, :].astype(F32)
+            for s in range(chunks):
+                at = chan * taps + 16 * s
+                chunk_ref[2 * (owner * chunks + s) + c] = piece[at : at + 16, :].astype(F32)
+    b_ref[...] = tap_ref[0:TAPS]
     for j in range(15):
-        x, y = mine_ref[j].astype(F32), other_ref[j].astype(F32)
-        x, y = jnp.where(first, x, y), jnp.where(first, y, x)
-        if 2 * j < TAPS:
-            b_ref[2 * j] = x[0:chan]
-        if 2 * j + 1 < TAPS:
-            b_ref[2 * j + 1] = y[0:chan]
-        v = jnp.concatenate([x[chan : chan + 16], y[chan : chan + 16]], axis=0)
+        v = jnp.concatenate([chunk_ref[2 * j], chunk_ref[2 * j + 1]], axis=0)
         for half in range(2):
             t = 2 * (j // 3) + half
             if t < 9:
@@ -522,11 +558,14 @@
     shape = jax.ShapeDtypeStruct
     up = [(i, i + 1) for i in range(n - 1)]
     swap = [(i, i ^ 1) for i in range(dp)]
-    groups = [[(2 * k + c) * n + z for k in range(dp // 2) for z in order(n)] for c in range(2)]
-    peers = dp * n // 2
-
-    def exchange(x):
-        return lax.all_to_all(x, ("dp", "mp"), 0, 0, tiled=True, axis_index_groups=groups)
+    columns = dp // 2
+    taps, chunks = per_column(columns)
+
+    def along_mp(x, d):
+        return lax.ppermute(x, "mp", [(i, (i + d) % n) for i in range(n)])
+
+    def along_dp(x, m):
+        return lax.ppermute(x, "dp", [(i, i ^ (2 * m)) for i in range(dp)])
 
     volume, cotangent, kernel_b = (
         pltpu.with_memory_space_constraint(x, pltpu.HBM) for x in (volume, cotangent, kernel_b.reshape(TAPS, chan_b, 128))
@@ -541,21 +580,26 @@
         compiler_params=params(2),
         cost_estimate=cost(1),
     )(volume)
-    packed = pl.pallas_call(
-        functools.partial(pack_kernel, n),
-        grid=(1,),
-        out_shape=shape((n, sent, 128), BF),
-        in_specs=[
-            pl.BlockSpec(cotangent.shape, lambda i: (0, 0, 0, 0, 0)),
-            pl.BlockSpec((TAPS, chan_b, 128), lambda i: (0, 0, 0)),
-            pl.BlockSpec(memory_space=pl.ANY),
-        ],
-        out_specs=pl.BlockSpec((n, sent, 128), lambda i: (0, 0, 0)),
-        compiler_params=params(8),
-        cost_estimate=cost(2),
-    )(cotangent, kernel_b, halo)
+    parts = list(
+        pl.pallas_call(
+            functools.partial(pack_kernel, n),
+            grid=(1,),
+            out_shape=[pltpu.VMEM((sent, 128), BF)] * n,
+            in_specs=[
+                pl.BlockSpec(cotangent.shape, lambda i: (0, 0, 0, 0, 0)),
+                pl.BlockSpec((TAPS, chan_b, 128), lambda i: (0, 0, 0)),
+                pl.BlockSpec(memory_space=pl.ANY),
+            ],
+            out_specs=[VMEM] * n,
+            scratch_shapes=[pltpu.VMEM((n, (slab + 1) * rows, 128), BF)],
+            compiler_params=params(8),
+            cost_estimate=cost(2),
+        )(cotangent, kernel_b, halo)
+    )
     halo = lax.ppermute(halo, "mp", up)
-    cot = lax.all_to_all(packed, "mp", 0, 0, tiled=True, axis_index_groups=[order(n)])
+    for d in range(1, n):
+        parts[d] = lax.ppermute(parts[d], "mp", [(i, (i + d) % n) for i in range(n)])
+
     vd, hidden, pre = pl.pallas_call(
         first_kernel,
         out_shape=(
@@ -589,12 +633,18 @@
         compiler_params=params(16),
         cost_estimate=cost(10),
     )(halo, kernel_a, pre)
-    cot, h0 = lax.optimization_barrier((cot, h0))
-    kb_other = lax.ppermute(cot, "dp", swap)
+    h0, *parts = lax.optimization_barrier((h0, *parts))
+    cot, kb = call(
+        functools.partial(gather_kernel, n),
+        (pltpu.VMEM((n, (slab + 1) * rows, 128), BF), pltpu.VMEM((n, HALF * chan_b, 128), BF)),
+        n,
+        1,
+    )(*parts)
+    kb_other = lax.ppermute(kb, "dp", swap)
 
     c, mine_b = call(
         functools.partial(grad_b_kernel, n),
-        (pltpu.VMEM((slab + 1, 2, 144, 256), BF), pltpu.VMEM((2, peers, 64, 128), F32)),
+        (pltpu.VMEM((slab + 1, 2, 144, 256), BF), pltpu.VMEM((2, columns * taps, 64, 128), F32)),
         3,
         3,
     )(hidden, h0, cot)
@@ -602,54 +652,73 @@
 
     keep_a, send_a = call(
         functools.partial(grad_a_kernel, n),
-        (shape((peers, 16, 128), F32), shape((peers, 16, 128), F32)),
+        (pltpu.VMEM((columns * chunks, 16, 128), F32), pltpu.VMEM((columns * chunks, 16, 128), F32)),
         7,
         8,
-        [pltpu.VMEM((3456, 256), BF), pltpu.VMEM((192, hplanes * 512), BF), pltpu.VMEM((2, peers, 16, 128), F32)],
+        [pltpu.VMEM((3456, 256), BF), pltpu.VMEM((192, hplanes * 512), BF), pltpu.VMEM((2, columns * chunks, 16, 128), F32)],
         24,
-    )(cot, kb_other, hidden, h0, c, vd, vdh)
+    )(kb, kb_other, hidden, h0, c, vd, vdh)
     got_a = lax.ppermute(send_a, "dp", swap)
 
-    sums = call(pair_kernel, pltpu.VMEM((peers, 80, 128), BF), 4, 1)(mine_b, got_b, keep_a, got_a)
-    sums = exchange(sums)
-
-    pieces = call(
-        functools.partial(features_kernel, n),
-        [shape(((slab + 1) * rows, 128), BF)] * n,
-        4,
-        4,
-        [
-            pltpu.VMEM((n, (slab + 1) * rows, 128), BF),
-            pltpu.VMEM((3456, 256), BF),
-        ],
-    )(cot, kb_other, hidden, h0)
-    pieces = list(pieces)
-    early = (1,)
-
-    def send(d):
-        pieces[d] = lax.ppermute(pieces[d], "mp", [(i, (i + d) % n) for i in range(n)])
-
-    for d in early:
-        send(d)
-    sums, *pieces = lax.optimization_barrier((sums, *pieces))
+    size = 64 * taps + 16 * chunks
+    sums = list(
+        call(functools.partial(pair_kernel, columns), [pltpu.VMEM((size, 128), BF)] * columns, 4, 1)(
+            mine_b, got_b, keep_a, got_a
+        )
+    )
+    for m in range(1, columns):
+        sums[m] = along_dp(sums[m], m)
+    pieces = list(
+        call(
+            functools.partial(features_kernel, n),
+            [pltpu.VMEM(((slab + 1) * rows, 128), BF)] * n,
+            4,
+            4,
+            [
+                pltpu.VMEM((n, (slab + 1) * rows, 128), BF),
+                pltpu.VMEM((3456, 256), BF),
+            ],
+        )(kb, kb_other, hidden, h0)
+    )
     for d in range(1, n):
-        if d not in early:
-            send(d)
+        pieces[d] = along_mp(pieces[d], d)
+
+    size = chan_b * taps + 16 * chunks
+    sums = list(
+        call(
+            functools.partial(column_sum_kernel, n, columns),
+            [pltpu.VMEM((size, 128), BF)] * n,
+            columns,
+            1,
+            [pltpu.VMEM((n, size, 128), BF)],
+        )(*sums)
+    )
+    for d in range(1, n):
+        sums[d] = along_mp(sums[d], d)
+    both = lax.optimization_barrier((*sums, *pieces))
+    sums, pieces = both[:n], both[n:]
 
     samples = volume.shape[0] * dp
     scale_a = 1 / math.sqrt(samples * (GRID // 2) ** 3)
     scale_b = 1 / math.sqrt(samples * (GRID // 4) ** 3)
-    mine = call(
-        functools.partial(sum_kernel, n, scale_a, scale_b), pltpu.VMEM((peers, chan_b + 16, 128), BF), 1, 1
-    )(sums)
-    mine = exchange(mine)
-    mine, *pieces = lax.optimization_barrier((mine, *pieces))
-    other = lax.ppermute(mine, "dp", swap)
-
+    total = call(
+        functools.partial(slab_sum_kernel, n, columns, scale_a, scale_b), pltpu.VMEM((size, 128), BF), n, 1
+    )(*sums)
+    mine = [total] + [along_dp(total, m) for m in range(1, columns)]
     features = call(functools.partial(unpack_kernel, n), shape((1, 16, 16, 16, chan_o), BF), n, 2)(*pieces)
+    both = lax.optimization_barrier((features, *mine))
+    features, mine = both[0], both[1:]
+    other = [lax.ppermute(x, "dp", swap) for x in mine]
     grad_a, grad_b = call(
-        last_kernel, (shape((3, 3, 3, 32, 64), F32), shape((TAPS, chan_b, 128), F32)), 2, 1
-    )(mine, other)
+        functools.partial(last_kernel, columns),
+        (shape((3, 3, 3, 32, 64), F32), shape((TAPS, chan_b, 128), F32)),
+        2 * columns,
+        1,
+        [
+            pltpu.VMEM((2 * columns * chunks, 16, 128), F32),
+            pltpu.VMEM((2 * columns * taps, chan_b, 128), F32),
+        ],
+    )(*mine, *other)
     return (features, grad_a, grad_b.reshape(3, 3, 3, chan_b, 128))
 
 

time: 70.9 us -> 62.6 us (0.88)
  waiting for transfers between devices: 17.5 us -> 7.95 us
  starting transfers between devices: 24.9 us -> 29.4 us
  Pallas kernels: 26.1 us -> 24 us
  local copies, waits for them, and re-layouts: 1.25 us -> 0.24 us
    ppermute x5 -> x20, starting transfers between devices: 2.69 us -> 23.6 us  [the longest x6 9.8 us: along_mp(): return lax.ppermute(x, 'mp', [(i, (i + d) % n) for i in range(n)])]
    all_to_all x3 -> x0, starting transfers between devices: 16.1 us -> none  [the longest x2 11.1 us: exchange(): lax.all_to_all(x, ('dp', 'mp'), 0, 0, tiled=True, axis_index_groups=groups)]
    ppermute x5 -> x20, waiting for transfers between devices: 12.7 us -> 6.75 us  [the longest x6 4.26 us: along_mp(): return lax.ppermute(x, 'mp', [(i, (i + d) % n) for i in range(n)])]
    all_to_all x3 -> x0, waiting for transfers between devices: 3.79 us -> none  [the longest x1 2.25 us: shards(): lax.all_to_all(packed, 'mp', 0, 0, tiled=True, axis_index_groups=[order(n)])]
    pallas_call x6 -> x8, Pallas kernels: 12 us -> 9.96 us  [the longest x1 4.87 us: shards(): call(functools.partial(grad_a_kernel, n), (pltpu.VMEM((columns * chunks,...]
    unnamed x10 -> x8, local copies, waits for them, and re-layouts: 1.25 us -> 0.24 us
  transfers between devices with their start and end apart: 11 -> 23, of which waited for: 5 -> 10; matrix products, arithmetic and copies ran while one was open for 0% -> 0% of each run, Pallas kernels for 32% -> 35%
where the time goes in v4:
time: 62.6 us; the launch traced here: 62.4 us
  starting transfers between devices  29.4 us (47%)
  Pallas kernels  24 us (38%)
  waiting for transfers between devices  7.95 us (13%)
  between operations  0.82 us (1%)
    ppermute x6, starting transfers between devices, along_mp(): return lax.ppermute(x, 'mp', [(i, (i + d) % n) for i in range(n)])  9.8 us
    pallas_call x1, Pallas kernels, shards(): pl.pallas_call(first_kernel, out_shape=(pltpu.HBM((planes, 5, 144, 256),...  8.46 us
    ppermute x6, starting transfers between devices, along_dp(): return lax.ppermute(x, 'dp', [(i, i ^ 2 * m) for i in range(dp)])  7.11 us
    ppermute x3, starting transfers between devices, shards(): lax.ppermute(parts[d], 'mp', [(i, (i + d) % n) for i in range(n)])  5.55 us
    ppermute x1, starting transfers between devices, shards(): halo = lax.ppermute(halo, 'mp', up)  5.08 us
    pallas_call x1, Pallas kernels, shards(): call(functools.partial(grad_a_kernel, n), (pltpu.VMEM((columns * chunks,...  4.87 us
    ppermute x6, waiting for transfers between devices, along_mp(): return lax.ppermute(x, 'mp', [(i, (i + d) % n) for i in range(n)])  4.26 us
    pallas_call x1, Pallas kernels, shards(): pl.pallas_call(functools.partial(pack_kernel, n), grid=(1,), out_shape=[p...  2.05 us
  transfers between devices with their start and end apart: 23, of which 10 were waited for; matrix products, arithmetic and copies ran while one was open for 0% of the time, Pallas kernels for 35%

profile of v4, /device:TPU:0, one launch (start us, length us, event | category | flops | bytes accessed | tf_op | source)
XLA Modules:
  0.0 62.4 jit_solution(11658365394872343020)
XLA Ops:
  0.6 1.0 %shard_map.68.after_ref = bf16[64,2048]{1,0:T(8,128)(2,1)S(1)} custom-call(bf16[1,16,64,2048]{3,2,1,0:T(8,128)(2,1)} %vol_ref.3), custom_call_target="tpu_custom_call" | custom-call | flops 1000000000 | bytes 3000000 | tf_op jit(solution)/shard_map/pallas_call | solution.py:574
  1.6 0.0 copy-start
  1.6 5.1 %collective-permute-start = (bf16[64,2048]{1,0:T(8,128)(2,1)S(1)}, bf16[64,2048]{1,0:T(8,128)(2,1)S(1)}, u32[]{:S(2)}, u32[]{:S(2)}) collective-permute-start(bf16[64,2048]{1,0:T(8,128)(2,1)S(1)} %shard_map.68.after_ref), channel_id=1, source_target_pairs={{0,8},{8,16},{16,24},{1,9},{9,17},{17,25},{2,10},{10,18},{18,26},{... | collective-permute-start | bytes 786440 | tf_op jit(solution)/shard_map/ppermute | solution.py:599
  6.7 2.0 %shard_map.70 = (bf16[544,128]{1,0:T(8,128)(2,1)S(1)}, bf16[544,128]{1,0:T(8,128)(2,1)S(1)}, bf16[544,128]{1,0:T(8,128)(2,1)S(1)}, bf16[544,128]{1,0:T(8,128)(2,1)S(1)}) custom-call(bf16[1,16,16,16,32]{4,3,2,1,0:T(8,128)(2,1)} %cot_ref.1, bf16[27,16,128]{2,1,0:T(8,128)(2,1)} %bitcast.4, bf16[64,2048]{1,0:T(8,128)(2,1)S(1)} %shard_map.68.after_ref), custom_call_target="tpu_custom_call" | custom-call | flops 2000000000 | bytes 6000000 | tf_op jit(solution)/shard_map/pallas_call | solution.py:584
  8.7 1.6 %collective-permute-start.1 = (bf16[544,128]{1,0:T(8,128)(2,1)S(1)}, bf16[544,128]{1,0:T(8,128)(2,1)S(1)}, u32[]{:S(2)}, u32[]{:S(2)}) collective-permute-start(bf16[544,128]{1,0:T(8,128)(2,1)S(1)} %get-tuple-element.54), channel_id=1, source_target_pairs={{0,8},{8,16},{16,24},{24,0},{1,9},{9,17},{17,25},{25,1},{2,10},{10... | collective-permute-start | bytes 417800 | tf_op jit(solution)/shard_map/ppermute | solution.py:601
  10.4 1.1 %collective-permute-start.2 = (bf16[544,128]{1,0:T(8,128)(2,1)S(1)}, bf16[544,128]{1,0:T(8,128)(2,1)S(1)}, u32[]{:S(2)}, u32[]{:S(2)}) collective-permute-start(bf16[544,128]{1,0:T(8,128)(2,1)S(1)} %get-tuple-element.55), channel_id=1, source_target_pairs={{0,16},{8,24},{16,0},{24,8},{1,17},{9,25},{17,1},{25,9},{2,18},{10... | collective-permute-start | bytes 417800 | tf_op jit(solution)/shard_map/ppermute | solution.py:601
  11.5 2.8 %collective-permute-start.3 = (bf16[544,128]{1,0:T(8,128)(2,1)S(1)}, bf16[544,128]{1,0:T(8,128)(2,1)S(1)}, u32[]{:S(2)}, u32[]{:S(2)}) collective-permute-start(bf16[544,128]{1,0:T(8,128)(2,1)S(1)} %get-tuple-element.56), channel_id=1, source_target_pairs={{0,24},{8,0},{16,8},{24,16},{1,25},{9,1},{17,9},{25,17},{2,26},{10... | collective-permute-start | bytes 417800 | tf_op jit(solution)/shard_map/ppermute | solution.py:601
  14.3 8.5 %shard_map.67 = (bf16[16,5,144,256]{3,2,1,0:T(8,128)(2,1)}, bf16[8,3,144,256]{3,2,1,0:T(8,128)(2,1)S(1)}, f32[256,256]{1,0:T(8,128)S(1)}) custom-call(bf16[1,16,64,2048]{3,2,1,0:T(8,128)(2,1)} %vol_ref.3, bf16[3,3,3,32,64]{4,3,2,1,0:T(8,128)(2,1)S(1)} %copy-done), custom_call_target="tpu_custom_call" | custom-call | flops 99999997952 | bytes 300000000 | tf_op jit(solution)/shard_map/pallas_call | solution.py:603
  22.8 0.0 collective-permute-done.halo_ref
  22.8 1.1 %shard_map.69 = (bf16[5,144,256]{2,1,0:T(8,128)(2,1)}, bf16[3,144,256]{2,1,0:T(8,128)(2,1)S(1)}) custom-call(bf16[64,2048]{1,0:T(8,128)(2,1)S(1)} %collective-permute-done.halo_ref, bf16[3,3,3,32,64]{4,3,2,1,0:T(8,128)(2,1)S(1)} %copy-done, f32[256,256]{1,0:T(8,128)S(1)} %get-tuple-element.51.pre_ref), custom_call_target="tpu_custom_call" | custom-call | flops 10000000000 | bytes 30000000 | tf_op jit(solution)/shard_map/pallas_call | solution.py:623
  23.8 0.0 collective-permute-done.1.refs_1_
  23.9 0.0 collective-permute-done.2.refs_2_
  23.9 0.0 collective-permute-done.3.refs_3_
  23.9 0.0 slice-start
  23.9 0.1 shard_map.71
  23.9 0.1 collective-permute-start.5
  24.0 0.0 slice-start.1
  24.0 0.0 copy-start.1
  24.0 1.8 %shard_map.72 = (bf16[5,2,144,256]{3,2,1,0:T(8,128)(2,1)S(1)}, f32[2,16,64,128]{3,2,1,0:T(8,128)S(1)}) custom-call(bf16[8,3,144,256]{3,2,1,0:T(8,128)(2,1)S(1)} %get-tuple-element.50.h_ref, bf16[3,144,256]{2,1,0:T(8,128)(2,1)S(1)} %get-tuple-element.57.h0_ref, bf16[4,320,128]{2,1,0:T(8,128)(2,1)S(1)} %get-tuple-element.62.cot_ref), custom_call_target="tpu_custom_call" | custom-call | flops 3000000000 | bytes 9000000 | tf_op jit(solution)/shard_map/pallas_call | solution.py:645
  25.9 0.5 collective-permute-start.4
  26.4 0.0 collective-permute-done.5.other_ref
  26.4 0.2 slice-done.1
  26.6 0.0 copy-done.1
  26.6 4.9 %shard_map.73 = (f32[16,16,128]{2,1,0:T(8,128)S(1)}, f32[16,16,128]{2,1,0:T(8,128)S(1)}) custom-call(bf16[4,224,128]{2,1,0:T(8,128)(2,1)S(1)} %get-tuple-element.64.kb_ref, bf16[4,224,128]{2,1,0:T(8,128)(2,1)S(1)} %collective-permute-done.5.other_ref, bf16[8,3,144,256]{3,2,1,0:T(8,128)(2,1)S(1)} %get-tuple-element.50.h_ref, ...), custom_call_target="tpu_custom_call" | custom-call | flops 8000000000 | bytes 24000000 | tf_op jit(solution)/shard_map/pallas_call | solution.py:653
  31.5 0.2 collective-permute-start.6
  31.7 1.2 %collective-permute-done.6.got_a = f32[16,16,128]{2,1,0:T(8,128)S(1)} collective-permute-done((f32[16,16,128]{2,1,0:T(8,128)S(1)}, f32[16,16,128]{2,1,0:T(8,128)S(1)}, u32[]{:S(2)}, u32[]{:S(2)}) %collective-permute-start.6) | collective-permute-done | bytes 131104 | tf_op jit(solution)/shard_map/ppermute | solution.py:661
  32.9 0.0 collective-permute-done.4.got_b
  32.9 0.1 shard_map.74
  33.0 1.5 %collective-permute-start.7 = (bf16[320,128]{1,0:T(8,128)(2,1)S(1)}, bf16[320,128]{1,0:T(8,128)(2,1)S(1)}, u32[]{:S(2)}, u32[]{:S(2)}) collective-permute-start(bf16[320,128]{1,0:T(8,128)(2,1)S(1)} %get-tuple-element.71), channel_id=1, source_target_pairs={{0,2},{1,3},{2,0},{3,1},{4,6},{5,7},{6,4},{7,5},{8,10},{9,11},{10,... | collective-permute-start | bytes 245768 | tf_op jit(solution)/shard_map/ppermute | solution.py:568
  34.5 1.5 %collective-permute-start.8 = (bf16[320,128]{1,0:T(8,128)(2,1)S(1)}, bf16[320,128]{1,0:T(8,128)(2,1)S(1)}, u32[]{:S(2)}, u32[]{:S(2)}) collective-permute-start(bf16[320,128]{1,0:T(8,128)(2,1)S(1)} %get-tuple-element.72), channel_id=1, source_target_pairs={{0,4},{1,5},{2,6},{3,7},{4,0},{5,1},{6,2},{7,3},{8,12},{9,13},{10,... | collective-permute-start | bytes 245768 | tf_op jit(solution)/shard_map/ppermute | solution.py:568
  36.1 0.5 collective-permute-start.9
  36.5 1.9 %shard_map.76 = (bf16[320,128]{1,0:T(8,128)(2,1)S(1)}, bf16[320,128]{1,0:T(8,128)(2,1)S(1)}, bf16[320,128]{1,0:T(8,128)(2,1)S(1)}, bf16[320,128]{1,0:T(8,128)(2,1)S(1)}) custom-call(bf16[4,224,128]{2,1,0:T(8,128)(2,1)S(1)} %get-tuple-element.64.kb_ref, bf16[4,224,128]{2,1,0:T(8,128)(2,1)S(1)} %collective-permute-done.5.other_ref, ...), custom_call_target="tpu_custom_call" | custom-call | flops 4000000000 | bytes 12000000 | tf_op jit(solution)/shard_map/pallas_call | solution.py:672
  38.5 1.9 %collective-permute-start.13 = (bf16[320,128]{1,0:T(8,128)(2,1)S(1)}, bf16[320,128]{1,0:T(8,128)(2,1)S(1)}, u32[]{:S(2)}, u32[]{:S(2)}) collective-permute-start(bf16[320,128]{1,0:T(8,128)(2,1)S(1)} %get-tuple-element.79), channel_id=1, source_target_pairs={{0,8},{8,16},{16,24},{24,0},{1,9},{9,17},{17,25},{25,1},{2,10},{10... | collective-permute-start | bytes 245768 | tf_op jit(solution)/shard_map/ppermute | solution.py:565
  40.4 3.4 %collective-permute-start.14 = (bf16[320,128]{1,0:T(8,128)(2,1)S(1)}, bf16[320,128]{1,0:T(8,128)(2,1)S(1)}, u32[]{:S(2)}, u32[]{:S(2)}) collective-permute-start(bf16[320,128]{1,0:T(8,128)(2,1)S(1)} %get-tuple-element.80), channel_id=1, source_target_pairs={{0,16},{8,24},{16,0},{24,8},{1,17},{9,25},{17,1},{25,9},{2,18},{10... | collective-permute-start | bytes 245768 | tf_op jit(solution)/shard_map/ppermute | solution.py:565
  43.8 0.0 collective-permute-done.7.refs_1_
  43.8 0.0 collective-permute-start.15
  43.8 0.0 collective-permute-done.8.refs_2_
  43.8 0.0 collective-permute-done.9.refs_3_
  43.8 0.1 shard_map.75
  43.9 2.1 %collective-permute-start.10 = (bf16[128,128]{1,0:T(8,128)(2,1)S(1)}, bf16[128,128]{1,0:T(8,128)(2,1)S(1)}, u32[]{:S(2)}, u32[]{:S(2)}) collective-permute-start(bf16[128,128]{1,0:T(8,128)(2,1)S(1)} %get-tuple-element.75), channel_id=1, source_target_pairs={{0,8},{8,16},{16,24},{24,0},{1,9},{9,17},{17,25},{25,1},{2,10},{10... | collective-permute-start | bytes 98312 | tf_op jit(solution)/shard_map/ppermute | solution.py:565
  45.9 0.8 %collective-permute-start.11 = (bf16[128,128]{1,0:T(8,128)(2,1)S(1)}, bf16[128,128]{1,0:T(8,128)(2,1)S(1)}, u32[]{:S(2)}, u32[]{:S(2)}) collective-permute-start(bf16[128,128]{1,0:T(8,128)(2,1)S(1)} %get-tuple-element.76), channel_id=1, source_target_pairs={{0,16},{8,24},{16,0},{24,8},{1,17},{9,25},{17,1},{25,9},{2,18},{10... | collective-permute-start | bytes 98312 | tf_op jit(solution)/shard_map/ppermute | solution.py:565
  46.8 0.0 collective-permute-done.13.refs_1_
  46.8 1.6 %collective-permute-start.12 = (bf16[128,128]{1,0:T(8,128)(2,1)S(1)}, bf16[128,128]{1,0:T(8,128)(2,1)S(1)}, u32[]{:S(2)}, u32[]{:S(2)}) collective-permute-start(bf16[128,128]{1,0:T(8,128)(2,1)S(1)} %get-tuple-element.77), channel_id=1, source_target_pairs={{0,24},{8,0},{16,8},{24,16},{1,25},{9,1},{17,9},{25,17},{2,26},{10... | collective-permute-start | bytes 98312 | tf_op jit(solution)/shard_map/ppermute | solution.py:565
  48.4 1.1 %collective-permute-done.14.refs_2_ = bf16[320,128]{1,0:T(8,128)(2,1)S(1)} collective-permute-done((bf16[320,128]{1,0:T(8,128)(2,1)S(1)}, bf16[320,128]{1,0:T(8,128)(2,1)S(1)}, u32[]{:S(2)}, u32[]{:S(2)}) %collective-permute-start.14) | collective-permute-done | bytes 81952 | tf_op jit(solution)/shard_map/ppermute | solution.py:565
  49.5 0.9 %collective-permute-done.15.refs_3_ = bf16[320,128]{1,0:T(8,128)(2,1)S(1)} collective-permute-done((bf16[320,128]{1,0:T(8,128)(2,1)S(1)}, bf16[320,128]{1,0:T(8,128)(2,1)S(1)}, u32[]{:S(2)}, u32[]{:S(2)}) %collective-permute-start.15) | collective-permute-done | bytes 81952 | tf_op jit(solution)/shard_map/ppermute | solution.py:565
  50.3 0.0 collective-permute-done.10.refs_1_
  50.3 2.3 %collective-permute-done.11.refs_2_ = bf16[128,128]{1,0:T(8,128)(2,1)S(1)} collective-permute-done((bf16[128,128]{1,0:T(8,128)(2,1)S(1)}, bf16[128,128]{1,0:T(8,128)(2,1)S(1)}, u32[]{:S(2)}, u32[]{:S(2)}) %collective-permute-start.11) | collective-permute-done | bytes 32800 | tf_op jit(solution)/shard_map/ppermute | solution.py:565
  52.6 0.0 collective-permute-done.12.refs_3_
  52.7 2.5 %collective-permute-start.18 = (bf16[128,128]{1,0:T(8,128)(2,1)S(1)}, bf16[128,128]{1,0:T(8,128)(2,1)S(1)}, u32[]{:S(2)}, u32[]{:S(2)}) collective-permute-start(bf16[128,128]{1,0:T(8,128)(2,1)S(1)} %shard_map.78.refs_0_), channel_id=1, source_target_pairs={{0,6},{1,7},{2,4},{3,5},{4,2},{5,3},{6,0},{7,1},{8,14},{9,15},{10,... | collective-permute-start | bytes 98312 | tf_op jit(solution)/shard_map/ppermute | solution.py:568
  55.2 0.5 collective-permute-start.17
  55.7 0.5 collective-permute-start.16
  56.2 1.8 %shard_map.77 = bf16[1,16,16,16,32]{4,3,2,1,0:T(8,128)(2,1)} custom-call(bf16[320,128]{1,0:T(8,128)(2,1)S(1)} %get-tuple-element.82.refs_0_, bf16[320,128]{1,0:T(8,128)(2,1)S(1)} %collective-permute-done.13.refs_1_, bf16[320,128]{1,0:T(8,128)(2,1)S(1)} %collective-permute-done.14.refs_2_, bf16[320,128]{1,0:T(8,128)(2,1)S(1)} %collective-permute-done.15.refs_3_), custom_call_target="tpu_custom_call" | custom-call | flops 2000000000 | bytes 6000000 | tf_op jit(solution)/shard_map/pallas_call | solution.py:708
  58.0 0.0 collective-permute-done.18.refs_3_
  58.0 1.1 %collective-permute-done.17.refs_2_ = bf16[128,128]{1,0:T(8,128)(2,1)S(1)} collective-permute-done((bf16[128,128]{1,0:T(8,128)(2,1)S(1)}, bf16[128,128]{1,0:T(8,128)(2,1)S(1)}, u32[]{:S(2)}, u32[]{:S(2)}) %collective-permute-start.17) | collective-permute-done | bytes 32800 | tf_op jit(solution)/shard_map/ppermute | solution.py:568
  59.1 0.5 collective-permute-done.16.refs_1_
  59.6 0.0 collective-permute-start.19
  59.6 0.5 collective-permute-start.20
  60.1 0.0 collective-permute-start.21
  60.1 0.5 collective-permute-start.22
  60.6 0.2 collective-permute-done.19.refs_4_
  60.8 0.2 collective-permute-done.20.refs_5_
  61.0 0.3 collective-permute-done.21.refs_6_
  61.3 0.2 collective-permute-done.22.refs_7_
  61.5 0.9 %shard_map.79 = (f32[3,3,3,32,64]{4,3,2,1,0:T(8,128)}, f32[27,16,128]{2,1,0:T(8,128)}) custom-call(bf16[128,128]{1,0:T(8,128)(2,1)S(1)} %shard_map.78.refs_0_, bf16[128,128]{1,0:T(8,128)(2,1)S(1)} %collective-permute-done.16.refs_1_, bf16[128,128]{1,0:T(8,128)(2,1)S(1)} %collective-permute-done.17.refs_2_, ...), custom_call_target="tpu_custom_call" | custom-call | flops 1000000000 | bytes 3000000 | tf_op jit(solution)/shard_map/pallas_call | solution.py:712
  (4 shorter events, 0.0 us)
Async XLA Ops:
  1.6 12.7 %copy-start = (bf16[3,3,3,32,64]{4,3,2,1,0:T(8,128)(2,1)S(1)}, bf16[3,3,3,32,64]{4,3,2,1,0:T(8,128)(2,1)}, u32[]{:S(2)}) copy-start(bf16[3,3,3,32,64]{4,3,2,1,0:T(8,128)(2,1)} %ka_ref.3) | copy-start | bytes 331780
  1.6 21.2 %collective-permute-start = (bf16[64,2048]{1,0:T(8,128)(2,1)S(1)}, bf16[64,2048]{1,0:T(8,128)(2,1)S(1)}, u32[]{:S(2)}, u32[]{:S(2)}) collective-permute-start(bf16[64,2048]{1,0:T(8,128)(2,1)S(1)} %shard_map.68.after_ref), channel_id=1, source_target_pairs={{0,8},{8,16},{16,24},{1,9},{9,17},{17,25},{2,10},{10,18},{18,26},{... | collective-permute-start | bytes 786440 | tf_op jit(solution)/shard_map/ppermute | solution.py:599
  8.7 15.1 %collective-permute-start.1 = (bf16[544,128]{1,0:T(8,128)(2,1)S(1)}, bf16[544,128]{1,0:T(8,128)(2,1)S(1)}, u32[]{:S(2)}, u32[]{:S(2)}) collective-permute-start(bf16[544,128]{1,0:T(8,128)(2,1)S(1)} %get-tuple-element.54), channel_id=1, source_target_pairs={{0,8},{8,16},{16,24},{24,0},{1,9},{9,17},{17,25},{25,1},{2,10},{10... | collective-permute-start | bytes 417800 | tf_op jit(solution)/shard_map/ppermute | solution.py:601
  10.4 13.5 %collective-permute-start.2 = (bf16[544,128]{1,0:T(8,128)(2,1)S(1)}, bf16[544,128]{1,0:T(8,128)(2,1)S(1)}, u32[]{:S(2)}, u32[]{:S(2)}) collective-permute-start(bf16[544,128]{1,0:T(8,128)(2,1)S(1)} %get-tuple-element.55), channel_id=1, source_target_pairs={{0,16},{8,24},{16,0},{24,8},{1,17},{9,25},{17,1},{25,9},{2,18},{10... | collective-permute-start | bytes 417800 | tf_op jit(solution)/shard_map/ppermute | solution.py:601
  11.5 12.4 %collective-permute-start.3 = (bf16[544,128]{1,0:T(8,128)(2,1)S(1)}, bf16[544,128]{1,0:T(8,128)(2,1)S(1)}, u32[]{:S(2)}, u32[]{:S(2)}) collective-permute-start(bf16[544,128]{1,0:T(8,128)(2,1)S(1)} %get-tuple-element.56), channel_id=1, source_target_pairs={{0,24},{8,0},{16,8},{24,16},{1,25},{9,1},{17,9},{25,17},{2,26},{10... | collective-permute-start | bytes 417800 | tf_op jit(solution)/shard_map/ppermute | solution.py:601
  23.9 2.5 %slice-start = ((s8[5898240]{0:T(1024)(128)(4,1)}), s8[1703936]{0:T(1024)(128)(4,1)S(1)}, s32[]{:S(2)}) async-start(s8[5898240]{0:T(1024)(128)(4,1)} %bitcast.2), calls=%async_computation | async-start | bytes 3407872
  23.9 2.5 %collective-permute-start.5 = (bf16[4,224,128]{2,1,0:T(8,128)(2,1)S(1)}, bf16[4,224,128]{2,1,0:T(8,128)(2,1)S(1)}, u32[]{:S(2)}, u32[]{:S(2)}) collective-permute-start(bf16[4,224,128]{2,1,0:T(8,128)(2,1)S(1)} %get-tuple-element.64.kb_ref), channel_id=1, source_target_pairs={{0,1},{1,0},{2,3},{3,2},{4,5},{5,4},{6,7},{7,6},{8,9},{9,8},{10,11... | collective-permute-start | bytes 688136 | tf_op jit(solution)/shard_map/ppermute | solution.py:643
  24.0 2.6 %slice-start.1 = ((s8[5898240]{0:T(1024)(128)(4,1)}), s8[4194304]{0:T(1024)(128)(4,1)S(1)}, s32[]{:S(2)}) async-start(s8[5898240]{0:T(1024)(128)(4,1)} %bitcast.2), calls=%async_computation.1 | async-start | bytes 8388608
  24.0 2.6 %copy-start.1 = (bf16[5,144,256]{2,1,0:T(8,128)(2,1)S(1)}, bf16[5,144,256]{2,1,0:T(8,128)(2,1)}, u32[]{:S(2)}) copy-start(bf16[5,144,256]{2,1,0:T(8,128)(2,1)} %get-tuple-element.67.vdh_ref) | copy-start | bytes 1105924
  25.9 7.1 %collective-permute-start.4 = (f32[2,16,64,128]{3,2,1,0:T(8,128)S(1)}, f32[2,16,64,128]{3,2,1,0:T(8,128)S(1)}, u32[]{:S(2)}, u32[]{:S(2)}) collective-permute-start(f32[2,16,64,128]{3,2,1,0:T(8,128)S(1)} %get-tuple-element.63.mine_b), channel_id=1, source_target_pairs={{0,1},{1,0},{2,3},{3,2},{4,5},{5,4},{6,7},{7,6},{8,9},{9,8},{10,11... | collective-permute-start | bytes 3145736 | tf_op jit(solution)/shard_map/ppermute | solution.py:651
  31.5 1.4 %collective-permute-start.6 = (f32[16,16,128]{2,1,0:T(8,128)S(1)}, f32[16,16,128]{2,1,0:T(8,128)S(1)}, u32[]{:S(2)}, u32[]{:S(2)}) collective-permute-start(f32[16,16,128]{2,1,0:T(8,128)S(1)} %get-tuple-element.69), channel_id=1, source_target_pairs={{0,1},{1,0},{2,3},{3,2},{4,5},{5,4},{6,7},{7,6},{8,9},{9,8},{10,11... | collective-permute-start | bytes 393224 | tf_op jit(solution)/shard_map/ppermute | solution.py:661
  33.0 10.8 %collective-permute-start.7 = (bf16[320,128]{1,0:T(8,128)(2,1)S(1)}, bf16[320,128]{1,0:T(8,128)(2,1)S(1)}, u32[]{:S(2)}, u32[]{:S(2)}) collective-permute-start(bf16[320,128]{1,0:T(8,128)(2,1)S(1)} %get-tuple-element.71), channel_id=1, source_target_pairs={{0,2},{1,3},{2,0},{3,1},{4,6},{5,7},{6,4},{7,5},{8,10},{9,11},{10,... | collective-permute-start | bytes 245768 | tf_op jit(solution)/shard_map/ppermute | solution.py:568
  34.5 9.2 %collective-permute-start.8 = (bf16[320,128]{1,0:T(8,128)(2,1)S(1)}, bf16[320,128]{1,0:T(8,128)(2,1)S(1)}, u32[]{:S(2)}, u32[]{:S(2)}) collective-permute-start(bf16[320,128]{1,0:T(8,128)(2,1)S(1)} %get-tuple-element.72), channel_id=1, source_target_pairs={{0,4},{1,5},{2,6},{3,7},{4,0},{5,1},{6,2},{7,3},{8,12},{9,13},{10,... | collective-permute-start | bytes 245768 | tf_op jit(solution)/shard_map/ppermute | solution.py:568
  36.1 7.7 %collective-permute-start.9 = (bf16[320,128]{1,0:T(8,128)(2,1)S(1)}, bf16[320,128]{1,0:T(8,128)(2,1)S(1)}, u32[]{:S(2)}, u32[]{:S(2)}) collective-permute-start(bf16[320,128]{1,0:T(8,128)(2,1)S(1)} %get-tuple-element.73), channel_id=1, source_target_pairs={{0,6},{1,7},{2,4},{3,5},{4,2},{5,3},{6,0},{7,1},{8,14},{9,15},{10,... | collective-permute-start | bytes 245768 | tf_op jit(solution)/shard_map/ppermute | solution.py:568
  38.5 8.3 %collective-permute-start.13 = (bf16[320,128]{1,0:T(8,128)(2,1)S(1)}, bf16[320,128]{1,0:T(8,128)(2,1)S(1)}, u32[]{:S(2)}, u32[]{:S(2)}) collective-permute-start(bf16[320,128]{1,0:T(8,128)(2,1)S(1)} %get-tuple-element.79), channel_id=1, source_target_pairs={{0,8},{8,16},{16,24},{24,0},{1,9},{9,17},{17,25},{25,1},{2,10},{10... | collective-permute-start | bytes 245768 | tf_op jit(solution)/shard_map/ppermute | solution.py:565
  40.4 9.1 %collective-permute-start.14 = (bf16[320,128]{1,0:T(8,128)(2,1)S(1)}, bf16[320,128]{1,0:T(8,128)(2,1)S(1)}, u32[]{:S(2)}, u32[]{:S(2)}) collective-permute-start(bf16[320,128]{1,0:T(8,128)(2,1)S(1)} %get-tuple-element.80), channel_id=1, source_target_pairs={{0,16},{8,24},{16,0},{24,8},{1,17},{9,25},{17,1},{25,9},{2,18},{10... | collective-permute-start | bytes 245768 | tf_op jit(solution)/shard_map/ppermute | solution.py:565
  43.8 6.6 %collective-permute-start.15 = (bf16[320,128]{1,0:T(8,128)(2,1)S(1)}, bf16[320,128]{1,0:T(8,128)(2,1)S(1)}, u32[]{:S(2)}, u32[]{:S(2)}) collective-permute-start(bf16[320,128]{1,0:T(8,128)(2,1)S(1)} %get-tuple-element.81), channel_id=1, source_target_pairs={{0,24},{8,0},{16,8},{24,16},{1,25},{9,1},{17,9},{25,17},{2,26},{10... | collective-permute-start | bytes 245768 | tf_op jit(solution)/shard_map/ppermute | solution.py:565
  43.9 6.5 %collective-permute-start.10 = (bf16[128,128]{1,0:T(8,128)(2,1)S(1)}, bf16[128,128]{1,0:T(8,128)(2,1)S(1)}, u32[]{:S(2)}, u32[]{:S(2)}) collective-permute-start(bf16[128,128]{1,0:T(8,128)(2,1)S(1)} %get-tuple-element.75), channel_id=1, source_target_pairs={{0,8},{8,16},{16,24},{24,0},{1,9},{9,17},{17,25},{25,1},{2,10},{10... | collective-permute-start | bytes 98312 | tf_op jit(solution)/shard_map/ppermute | solution.py:565
  45.9 6.7 %collective-permute-start.11 = (bf16[128,128]{1,0:T(8,128)(2,1)S(1)}, bf16[128,128]{1,0:T(8,128)(2,1)S(1)}, u32[]{:S(2)}, u32[]{:S(2)}) collective-permute-start(bf16[128,128]{1,0:T(8,128)(2,1)S(1)} %get-tuple-element.76), channel_id=1, source_target_pairs={{0,16},{8,24},{16,0},{24,8},{1,17},{9,25},{17,1},{25,9},{2,18},{10... | collective-permute-start | bytes 98312 | tf_op jit(solution)/shard_map/ppermute | solution.py:565
  46.8 5.9 %collective-permute-start.12 = (bf16[128,128]{1,0:T(8,128)(2,1)S(1)}, bf16[128,128]{1,0:T(8,128)(2,1)S(1)}, u32[]{:S(2)}, u32[]{:S(2)}) collective-permute-start(bf16[128,128]{1,0:T(8,128)(2,1)S(1)} %get-tuple-element.77), channel_id=1, source_target_pairs={{0,24},{8,0},{16,8},{24,16},{1,25},{9,1},{17,9},{25,17},{2,26},{10... | collective-permute-start | bytes 98312 | tf_op jit(solution)/shard_map/ppermute | solution.py:565
  52.7 5.3 %collective-permute-start.18 = (bf16[128,128]{1,0:T(8,128)(2,1)S(1)}, bf16[128,128]{1,0:T(8,128)(2,1)S(1)}, u32[]{:S(2)}, u32[]{:S(2)}) collective-permute-start(bf16[128,128]{1,0:T(8,128)(2,1)S(1)} %shard_map.78.refs_0_), channel_id=1, source_target_pairs={{0,6},{1,7},{2,4},{3,5},{4,2},{5,3},{6,0},{7,1},{8,14},{9,15},{10,... | collective-permute-start | bytes 98312 | tf_op jit(solution)/shard_map/ppermute | solution.py:568
  55.2 3.9 %collective-permute-start.17 = (bf16[128,128]{1,0:T(8,128)(2,1)S(1)}, bf16[128,128]{1,0:T(8,128)(2,1)S(1)}, u32[]{:S(2)}, u32[]{:S(2)}) collective-permute-start(bf16[128,128]{1,0:T(8,128)(2,1)S(1)} %shard_map.78.refs_0_), channel_id=1, source_target_pairs={{0,4},{1,5},{2,6},{3,7},{4,0},{5,1},{6,2},{7,3},{8,12},{9,13},{10,... | collective-permute-start | bytes 98312 | tf_op jit(solution)/shard_map/ppermute | solution.py:568
  55.7 3.9 %collective-permute-start.16 = (bf16[128,128]{1,0:T(8,128)(2,1)S(1)}, bf16[128,128]{1,0:T(8,128)(2,1)S(1)}, u32[]{:S(2)}, u32[]{:S(2)}) collective-permute-start(bf16[128,128]{1,0:T(8,128)(2,1)S(1)} %shard_map.78.refs_0_), channel_id=1, source_target_pairs={{0,2},{1,3},{2,0},{3,1},{4,6},{5,7},{6,4},{7,5},{8,10},{9,11},{10,... | collective-permute-start | bytes 98312 | tf_op jit(solution)/shard_map/ppermute | solution.py:568
  59.6 1.2 %collective-permute-start.19 = (bf16[128,128]{1,0:T(8,128)(2,1)S(1)}, bf16[128,128]{1,0:T(8,128)(2,1)S(1)}, u32[]{:S(2)}, u32[]{:S(2)}) collective-permute-start(bf16[128,128]{1,0:T(8,128)(2,1)S(1)} %shard_map.78.refs_0_), channel_id=1, source_target_pairs={{0,1},{1,0},{2,3},{3,2},{4,5},{5,4},{6,7},{7,6},{8,9},{9,8},{10,11... | collective-permute-start | bytes 98312 | tf_op jit(solution)/shard_map/ppermute | solution.py:711
  59.6 1.4 %collective-permute-start.20 = (bf16[128,128]{1,0:T(8,128)(2,1)S(1)}, bf16[128,128]{1,0:T(8,128)(2,1)S(1)}, u32[]{:S(2)}, u32[]{:S(2)}) collective-permute-start(bf16[128,128]{1,0:T(8,128)(2,1)S(1)} %collective-permute-done.16.refs_1_), channel_id=1, source_target_pairs={{0,1},{1,0},{2,3},{3,2},{4,5},{5,4},{6,7},{7,6},{8,9},{9,8},{10,11... | collective-permute-start | bytes 98312 | tf_op jit(solution)/shard_map/ppermute | solution.py:711
  60.1 1.2 %collective-permute-start.21 = (bf16[128,128]{1,0:T(8,128)(2,1)S(1)}, bf16[128,128]{1,0:T(8,128)(2,1)S(1)}, u32[]{:S(2)}, u32[]{:S(2)}) collective-permute-start(bf16[128,128]{1,0:T(8,128)(2,1)S(1)} %collective-permute-done.17.refs_2_), channel_id=1, source_target_pairs={{0,1},{1,0},{2,3},{3,2},{4,5},{5,4},{6,7},{7,6},{8,9},{9,8},{10,11... | collective-permute-start | bytes 98312 | tf_op jit(solution)/shard_map/ppermute | solution.py:711
  60.1 1.4 %collective-permute-start.22 = (bf16[128,128]{1,0:T(8,128)(2,1)S(1)}, bf16[128,128]{1,0:T(8,128)(2,1)S(1)}, u32[]{:S(2)}, u32[]{:S(2)}) collective-permute-start(bf16[128,128]{1,0:T(8,128)(2,1)S(1)} %collective-permute-done.18.refs_3_), channel_id=1, source_target_pairs={{0,1},{1,0},{2,3},{3,2},{4,5},{5,4},{6,7},{7,6},{8,9},{9,8},{10,11... | collective-permute-start | bytes 98312 | tf_op jit(solution)/shard_map/ppermute | solution.py:711

commit v5 on v4

--- a/solution.py
+++ b/solution.py
@@ -680,8 +680,10 @@
             ],
         )(kb, kb_other, hidden, h0)
     )
+    late = n // 2
     for d in range(1, n):
-        pieces[d] = along_mp(pieces[d], d)
+        if d != late:
+            pieces[d] = along_mp(pieces[d], d)
 
     size = chan_b * taps + 16 * chunks
     sums = list(
@@ -693,10 +695,12 @@
             [pltpu.VMEM((n, size, 128), BF)],
         )(*sums)
     )
+    *sums, last_piece = lax.optimization_barrier((*sums, pieces[late]))
     for d in range(1, n):
         sums[d] = along_mp(sums[d], d)
-    both = lax.optimization_barrier((*sums, *pieces))
-    sums, pieces = both[:n], both[n:]
+    both = lax.optimization_barrier((*sums, *pieces[:late], *pieces[late + 1 :]))
+    sums, pieces = both[:n], list(both[n:])
+    pieces.insert(late, along_mp(last_piece, late))
 
     samples = volume.shape[0] * dp
     scale_a = 1 / math.sqrt(samples * (GRID // 2) ** 3)

time: 62.6 us -> 59.8 us (0.955)
  waiting for transfers between devices: 7.95 us -> 4.32 us
  starting transfers between devices: 29.4 us -> 30.3 us
    ppermute x6, waiting for transfers between devices: 4.26 us -> 1.51 us  [along_mp(): return lax.ppermute(x, 'mp', [(i, (i + d) % n) for i in range(n)])]
    ppermute x6, starting transfers between devices: 9.8 us -> 10.7 us  [along_mp(): return lax.ppermute(x, 'mp', [(i, (i + d) % n) for i in range(n)])]
    ppermute x6, waiting for transfers between devices: 1.62 us -> 0.74 us  [along_dp(): return lax.ppermute(x, 'dp', [(i, i ^ 2 * m) for i in range(dp)])]
  transfers between devices with their start and end apart: 23 -> 23, of which waited for: 10 -> 9; matrix products, arithmetic and copies ran while one was open for 0% -> 0% of each run, Pallas kernels for 35% -> 37%
where the time goes in v5:
time: 59.8 us; the launch traced here: 59.6 us
  starting transfers between devices  30.3 us (51%)
  Pallas kernels  24 us (40%)
  waiting for transfers between devices  4.32 us (7%)
  between operations  0.82 us (1%)
    ppermute x6, starting transfers between devices, along_mp(): return lax.ppermute(x, 'mp', [(i, (i + d) % n) for i in range(n)])  10.7 us
    pallas_call x1, Pallas kernels, shards(): pl.pallas_call(first_kernel, out_shape=(pltpu.HBM((planes, 5, 144, 256),...  8.46 us
    ppermute x6, starting transfers between devices, along_dp(): return lax.ppermute(x, 'dp', [(i, i ^ 2 * m) for i in range(dp)])  7.11 us
    ppermute x3, starting transfers between devices, shards(): lax.ppermute(parts[d], 'mp', [(i, (i + d) % n) for i in range(n)])  5.55 us
    ppermute x1, starting transfers between devices, shards(): halo = lax.ppermute(halo, 'mp', up)  5.08 us
    pallas_call x1, Pallas kernels, shards(): call(functools.partial(grad_a_kernel, n), (pltpu.VMEM((columns * chunks,...  4.87 us
    pallas_call x1, Pallas kernels, shards(): pl.pallas_call(functools.partial(pack_kernel, n), grid=(1,), out_shape=[p...  2.05 us
    pallas_call x1, Pallas kernels, shards(): call(functools.partial(features_kernel, n), [pltpu.VMEM(((slab + 1) * row...  1.92 us
  transfers between devices with their start and end apart: 23, of which 9 were waited for; matrix products, arithmetic and copies ran while one was open for 0% of the time, Pallas kernels for 37%

profile of v5, /device:TPU:0, one launch (start us, length us, event | category | flops | bytes accessed | tf_op | source)
XLA Modules:
  0.0 59.6 jit_solution(12201915536324332660)
XLA Ops:
  0.6 1.0 %shard_map.68.after_ref = bf16[64,2048]{1,0:T(8,128)(2,1)S(1)} custom-call(bf16[1,16,64,2048]{3,2,1,0:T(8,128)(2,1)} %vol_ref.3), custom_call_target="tpu_custom_call" | custom-call | flops 1000000000 | bytes 3000000 | tf_op jit(solution)/shard_map/pallas_call | solution.py:574
  1.6 0.0 copy-start
  1.6 5.1 %collective-permute-start = (bf16[64,2048]{1,0:T(8,128)(2,1)S(1)}, bf16[64,2048]{1,0:T(8,128)(2,1)S(1)}, u32[]{:S(2)}, u32[]{:S(2)}) collective-permute-start(bf16[64,2048]{1,0:T(8,128)(2,1)S(1)} %shard_map.68.after_ref), channel_id=1, source_target_pairs={{0,8},{8,16},{16,24},{1,9},{9,17},{17,25},{2,10},{10,18},{18,26},{... | collective-permute-start | bytes 786440 | tf_op jit(solution)/shard_map/ppermute | solution.py:599
  6.7 2.0 %shard_map.70 = (bf16[544,128]{1,0:T(8,128)(2,1)S(1)}, bf16[544,128]{1,0:T(8,128)(2,1)S(1)}, bf16[544,128]{1,0:T(8,128)(2,1)S(1)}, bf16[544,128]{1,0:T(8,128)(2,1)S(1)}) custom-call(bf16[1,16,16,16,32]{4,3,2,1,0:T(8,128)(2,1)} %cot_ref.1, bf16[27,16,128]{2,1,0:T(8,128)(2,1)} %bitcast.4, bf16[64,2048]{1,0:T(8,128)(2,1)S(1)} %shard_map.68.after_ref), custom_call_target="tpu_custom_call" | custom-call | flops 2000000000 | bytes 6000000 | tf_op jit(solution)/shard_map/pallas_call | solution.py:584
  8.7 1.6 %collective-permute-start.1 = (bf16[544,128]{1,0:T(8,128)(2,1)S(1)}, bf16[544,128]{1,0:T(8,128)(2,1)S(1)}, u32[]{:S(2)}, u32[]{:S(2)}) collective-permute-start(bf16[544,128]{1,0:T(8,128)(2,1)S(1)} %get-tuple-element.58), channel_id=1, source_target_pairs={{0,8},{8,16},{16,24},{24,0},{1,9},{9,17},{17,25},{25,1},{2,10},{10... | collective-permute-start | bytes 417800 | tf_op jit(solution)/shard_map/ppermute | solution.py:601
  10.4 1.1 %collective-permute-start.2 = (bf16[544,128]{1,0:T(8,128)(2,1)S(1)}, bf16[544,128]{1,0:T(8,128)(2,1)S(1)}, u32[]{:S(2)}, u32[]{:S(2)}) collective-permute-start(bf16[544,128]{1,0:T(8,128)(2,1)S(1)} %get-tuple-element.59), channel_id=1, source_target_pairs={{0,16},{8,24},{16,0},{24,8},{1,17},{9,25},{17,1},{25,9},{2,18},{10... | collective-permute-start | bytes 417800 | tf_op jit(solution)/shard_map/ppermute | solution.py:601
  11.5 2.8 %collective-permute-start.3 = (bf16[544,128]{1,0:T(8,128)(2,1)S(1)}, bf16[544,128]{1,0:T(8,128)(2,1)S(1)}, u32[]{:S(2)}, u32[]{:S(2)}) collective-permute-start(bf16[544,128]{1,0:T(8,128)(2,1)S(1)} %get-tuple-element.60), channel_id=1, source_target_pairs={{0,24},{8,0},{16,8},{24,16},{1,25},{9,1},{17,9},{25,17},{2,26},{10... | collective-permute-start | bytes 417800 | tf_op jit(solution)/shard_map/ppermute | solution.py:601
  14.3 8.5 %shard_map.67 = (bf16[16,5,144,256]{3,2,1,0:T(8,128)(2,1)}, bf16[8,3,144,256]{3,2,1,0:T(8,128)(2,1)S(1)}, f32[256,256]{1,0:T(8,128)S(1)}) custom-call(bf16[1,16,64,2048]{3,2,1,0:T(8,128)(2,1)} %vol_ref.3, bf16[3,3,3,32,64]{4,3,2,1,0:T(8,128)(2,1)S(1)} %copy-done), custom_call_target="tpu_custom_call" | custom-call | flops 99999997952 | bytes 300000000 | tf_op jit(solution)/shard_map/pallas_call | solution.py:603
  22.8 0.0 collective-permute-done.halo_ref
  22.8 1.1 %shard_map.69 = (bf16[5,144,256]{2,1,0:T(8,128)(2,1)}, bf16[3,144,256]{2,1,0:T(8,128)(2,1)S(1)}) custom-call(bf16[64,2048]{1,0:T(8,128)(2,1)S(1)} %collective-permute-done.halo_ref, bf16[3,3,3,32,64]{4,3,2,1,0:T(8,128)(2,1)S(1)} %copy-done, f32[256,256]{1,0:T(8,128)S(1)} %get-tuple-element.55.pre_ref), custom_call_target="tpu_custom_call" | custom-call | flops 10000000000 | bytes 30000000 | tf_op jit(solution)/shard_map/pallas_call | solution.py:623
  23.8 0.0 collective-permute-done.1.refs_1_
  23.9 0.0 collective-permute-done.2.refs_2_
  23.9 0.0 collective-permute-done.3.refs_3_
  23.9 0.0 slice-start
  23.9 0.1 shard_map.71
  23.9 0.1 collective-permute-start.5
  24.0 0.0 slice-start.1
  24.0 0.0 copy-start.1
  24.0 1.8 %shard_map.72 = (bf16[5,2,144,256]{3,2,1,0:T(8,128)(2,1)S(1)}, f32[2,16,64,128]{3,2,1,0:T(8,128)S(1)}) custom-call(bf16[8,3,144,256]{3,2,1,0:T(8,128)(2,1)S(1)} %get-tuple-element.54.h_ref, bf16[3,144,256]{2,1,0:T(8,128)(2,1)S(1)} %get-tuple-element.61.h0_ref, bf16[4,320,128]{2,1,0:T(8,128)(2,1)S(1)} %get-tuple-element.66.cot_ref), custom_call_target="tpu_custom_call" | custom-call | flops 3000000000 | bytes 9000000 | tf_op jit(solution)/shard_map/pallas_call | solution.py:645
  25.9 0.5 collective-permute-start.4
  26.4 0.0 collective-permute-done.5.other_ref
  26.4 0.2 slice-done.1
  26.6 0.0 copy-done.1
  26.6 4.9 %shard_map.73 = (f32[16,16,128]{2,1,0:T(8,128)S(1)}, f32[16,16,128]{2,1,0:T(8,128)S(1)}) custom-call(bf16[4,224,128]{2,1,0:T(8,128)(2,1)S(1)} %get-tuple-element.68.kb_ref, bf16[4,224,128]{2,1,0:T(8,128)(2,1)S(1)} %collective-permute-done.5.other_ref, bf16[8,3,144,256]{3,2,1,0:T(8,128)(2,1)S(1)} %get-tuple-element.54.h_ref, ...), custom_call_target="tpu_custom_call" | custom-call | flops 8000000000 | bytes 24000000 | tf_op jit(solution)/shard_map/pallas_call | solution.py:653
  31.5 0.2 collective-permute-start.6
  31.7 1.2 %collective-permute-done.6.got_a = f32[16,16,128]{2,1,0:T(8,128)S(1)} collective-permute-done((f32[16,16,128]{2,1,0:T(8,128)S(1)}, f32[16,16,128]{2,1,0:T(8,128)S(1)}, u32[]{:S(2)}, u32[]{:S(2)}) %collective-permute-start.6) | collective-permute-done | bytes 131104 | tf_op jit(solution)/shard_map/ppermute | solution.py:661
  32.9 0.0 collective-permute-done.4.got_b
  32.9 0.1 shard_map.74
  33.0 1.5 %collective-permute-start.7 = (bf16[320,128]{1,0:T(8,128)(2,1)S(1)}, bf16[320,128]{1,0:T(8,128)(2,1)S(1)}, u32[]{:S(2)}, u32[]{:S(2)}) collective-permute-start(bf16[320,128]{1,0:T(8,128)(2,1)S(1)} %get-tuple-element.75), channel_id=1, source_target_pairs={{0,2},{1,3},{2,0},{3,1},{4,6},{5,7},{6,4},{7,5},{8,10},{9,11},{10,... | collective-permute-start | bytes 245768 | tf_op jit(solution)/shard_map/ppermute | solution.py:568
  34.5 1.5 %collective-permute-start.8 = (bf16[320,128]{1,0:T(8,128)(2,1)S(1)}, bf16[320,128]{1,0:T(8,128)(2,1)S(1)}, u32[]{:S(2)}, u32[]{:S(2)}) collective-permute-start(bf16[320,128]{1,0:T(8,128)(2,1)S(1)} %get-tuple-element.76), channel_id=1, source_target_pairs={{0,4},{1,5},{2,6},{3,7},{4,0},{5,1},{6,2},{7,3},{8,12},{9,13},{10,... | collective-permute-start | bytes 245768 | tf_op jit(solution)/shard_map/ppermute | solution.py:568
  36.1 0.5 collective-permute-start.9
  36.5 1.9 %shard_map.76 = (bf16[320,128]{1,0:T(8,128)(2,1)S(1)}, bf16[320,128]{1,0:T(8,128)(2,1)S(1)}, bf16[320,128]{1,0:T(8,128)(2,1)S(1)}, bf16[320,128]{1,0:T(8,128)(2,1)S(1)}) custom-call(bf16[4,224,128]{2,1,0:T(8,128)(2,1)S(1)} %get-tuple-element.68.kb_ref, bf16[4,224,128]{2,1,0:T(8,128)(2,1)S(1)} %collective-permute-done.5.other_ref, ...), custom_call_target="tpu_custom_call" | custom-call | flops 4000000000 | bytes 12000000 | tf_op jit(solution)/shard_map/pallas_call | solution.py:672
  38.5 1.9 %collective-permute-start.13 = (bf16[320,128]{1,0:T(8,128)(2,1)S(1)}, bf16[320,128]{1,0:T(8,128)(2,1)S(1)}, u32[]{:S(2)}, u32[]{:S(2)}) collective-permute-start(bf16[320,128]{1,0:T(8,128)(2,1)S(1)} %get-tuple-element.88), channel_id=1, source_target_pairs={{0,8},{8,16},{16,24},{24,0},{1,9},{9,17},{17,25},{25,1},{2,10},{10... | collective-permute-start | bytes 245768 | tf_op jit(solution)/shard_map/ppermute | solution.py:565
  40.4 2.9 %collective-permute-start.14 = (bf16[320,128]{1,0:T(8,128)(2,1)S(1)}, bf16[320,128]{1,0:T(8,128)(2,1)S(1)}, u32[]{:S(2)}, u32[]{:S(2)}) collective-permute-start(bf16[320,128]{1,0:T(8,128)(2,1)S(1)} %get-tuple-element.89), channel_id=1, source_target_pairs={{0,24},{8,0},{16,8},{24,16},{1,25},{9,1},{17,9},{25,17},{2,26},{10... | collective-permute-start | bytes 245768 | tf_op jit(solution)/shard_map/ppermute | solution.py:565
  43.3 0.0 collective-permute-done.7.refs_1_
  43.3 0.0 collective-permute-done.8.refs_2_
  43.3 0.0 collective-permute-done.9.refs_3_
  43.3 0.1 shard_map.75
  43.4 0.1 collective-permute-start.10
  43.4 3.4 %collective-permute-start.11 = (bf16[128,128]{1,0:T(8,128)(2,1)S(1)}, bf16[128,128]{1,0:T(8,128)(2,1)S(1)}, u32[]{:S(2)}, u32[]{:S(2)}) collective-permute-start(bf16[128,128]{1,0:T(8,128)(2,1)S(1)} %get-tuple-element.85), channel_id=1, source_target_pairs={{0,16},{8,24},{16,0},{24,8},{1,17},{9,25},{17,1},{25,9},{2,18},{10... | collective-permute-start | bytes 98312 | tf_op jit(solution)/shard_map/ppermute | solution.py:565
  46.8 0.5 collective-permute-start.12
  47.2 0.0 collective-permute-done.13.refs_1_
  47.2 2.0 %collective-permute-start.15 = (bf16[320,128]{1,0:T(8,128)(2,1)S(1)}, bf16[320,128]{1,0:T(8,128)(2,1)S(1)}, u32[]{:S(2)}, u32[]{:S(2)}) collective-permute-start(bf16[320,128]{1,0:T(8,128)(2,1)S(1)} %get-tuple-element.92), channel_id=1, source_target_pairs={{0,16},{8,24},{16,0},{24,8},{1,17},{9,25},{17,1},{25,9},{2,18},{10... | collective-permute-start | bytes 245768 | tf_op jit(solution)/shard_map/ppermute | solution.py:565
  49.3 0.0 collective-permute-done.14.refs_3_
  49.3 0.0 collective-permute-done.10.refs_1_
  49.3 0.9 %collective-permute-done.11.refs_2_ = bf16[128,128]{1,0:T(8,128)(2,1)S(1)} collective-permute-done((bf16[128,128]{1,0:T(8,128)(2,1)S(1)}, bf16[128,128]{1,0:T(8,128)(2,1)S(1)}, u32[]{:S(2)}, u32[]{:S(2)}) %collective-permute-start.11) | collective-permute-done | bytes 32800 | tf_op jit(solution)/shard_map/ppermute | solution.py:565
  50.2 0.6 %collective-permute-done.12.refs_3_ = bf16[128,128]{1,0:T(8,128)(2,1)S(1)} collective-permute-done((bf16[128,128]{1,0:T(8,128)(2,1)S(1)}, bf16[128,128]{1,0:T(8,128)(2,1)S(1)}, u32[]{:S(2)}, u32[]{:S(2)}) %collective-permute-start.12) | collective-permute-done | bytes 32800 | tf_op jit(solution)/shard_map/ppermute | solution.py:565
  50.8 1.6 %collective-permute-start.18 = (bf16[128,128]{1,0:T(8,128)(2,1)S(1)}, bf16[128,128]{1,0:T(8,128)(2,1)S(1)}, u32[]{:S(2)}, u32[]{:S(2)}) collective-permute-start(bf16[128,128]{1,0:T(8,128)(2,1)S(1)} %shard_map.78.refs_0_), channel_id=1, source_target_pairs={{0,6},{1,7},{2,4},{3,5},{4,2},{5,3},{6,0},{7,1},{8,14},{9,15},{10,... | collective-permute-start | bytes 98312 | tf_op jit(solution)/shard_map/ppermute | solution.py:568
  52.4 0.5 collective-permute-start.17
  52.9 1.4 %collective-permute-start.16 = (bf16[128,128]{1,0:T(8,128)(2,1)S(1)}, bf16[128,128]{1,0:T(8,128)(2,1)S(1)}, u32[]{:S(2)}, u32[]{:S(2)}) collective-permute-start(bf16[128,128]{1,0:T(8,128)(2,1)S(1)} %shard_map.78.refs_0_), channel_id=1, source_target_pairs={{0,2},{1,3},{2,0},{3,1},{4,6},{5,7},{6,4},{7,5},{8,10},{9,11},{10,... | collective-permute-start | bytes 98312 | tf_op jit(solution)/shard_map/ppermute | solution.py:568
  54.4 0.0 collective-permute-done.15.refs_2_
  54.4 1.8 %shard_map.77 = bf16[1,16,16,16,32]{4,3,2,1,0:T(8,128)(2,1)} custom-call(bf16[320,128]{1,0:T(8,128)(2,1)S(1)} %get-tuple-element.90.refs_0_, bf16[320,128]{1,0:T(8,128)(2,1)S(1)} %collective-permute-done.13.refs_1_, bf16[320,128]{1,0:T(8,128)(2,1)S(1)} %collective-permute-done.15.refs_2_, bf16[320,128]{1,0:T(8,128)(2,1)S(1)} %collective-permute-done.14.refs_3_), custom_call_target="tpu_custom_call" | custom-call | flops 2000000000 | bytes 6000000 | tf_op jit(solution)/shard_map/pallas_call | solution.py:712
  56.1 0.0 collective-permute-done.18.refs_3_
  56.1 0.2 collective-permute-done.17.refs_2_
  56.3 0.5 collective-permute-done.16.refs_1_
  56.9 0.0 collective-permute-start.19
  56.9 0.5 collective-permute-start.20
  57.4 0.0 collective-permute-start.21
  57.4 0.5 collective-permute-start.22
  57.9 0.2 collective-permute-done.19.refs_4_
  58.1 0.2 collective-permute-done.20.refs_5_
  58.2 0.3 collective-permute-done.21.refs_6_
  58.6 0.2 collective-permute-done.22.refs_7_
  58.7 0.9 %shard_map.79 = (f32[3,3,3,32,64]{4,3,2,1,0:T(8,128)}, f32[27,16,128]{2,1,0:T(8,128)}) custom-call(bf16[128,128]{1,0:T(8,128)(2,1)S(1)} %shard_map.78.refs_0_, bf16[128,128]{1,0:T(8,128)(2,1)S(1)} %collective-permute-done.16.refs_1_, bf16[128,128]{1,0:T(8,128)(2,1)S(1)} %collective-permute-done.17.refs_2_, ...), custom_call_target="tpu_custom_call" | custom-call | flops 1000000000 | bytes 3000000 | tf_op jit(solution)/shard_map/pallas_call | solution.py:716
  (4 shorter events, 0.0 us)
Async XLA Ops:
  1.6 12.7 %copy-start = (bf16[3,3,3,32,64]{4,3,2,1,0:T(8,128)(2,1)S(1)}, bf16[3,3,3,32,64]{4,3,2,1,0:T(8,128)(2,1)}, u32[]{:S(2)}) copy-start(bf16[3,3,3,32,64]{4,3,2,1,0:T(8,128)(2,1)} %ka_ref.3) | copy-start | bytes 331780
  1.6 21.2 %collective-permute-start = (bf16[64,2048]{1,0:T(8,128)(2,1)S(1)}, bf16[64,2048]{1,0:T(8,128)(2,1)S(1)}, u32[]{:S(2)}, u32[]{:S(2)}) collective-permute-start(bf16[64,2048]{1,0:T(8,128)(2,1)S(1)} %shard_map.68.after_ref), channel_id=1, source_target_pairs={{0,8},{8,16},{16,24},{1,9},{9,17},{17,25},{2,10},{10,18},{18,26},{... | collective-permute-start | bytes 786440 | tf_op jit(solution)/shard_map/ppermute | solution.py:599
  8.7 15.1 %collective-permute-start.1 = (bf16[544,128]{1,0:T(8,128)(2,1)S(1)}, bf16[544,128]{1,0:T(8,128)(2,1)S(1)}, u32[]{:S(2)}, u32[]{:S(2)}) collective-permute-start(bf16[544,128]{1,0:T(8,128)(2,1)S(1)} %get-tuple-element.58), channel_id=1, source_target_pairs={{0,8},{8,16},{16,24},{24,0},{1,9},{9,17},{17,25},{25,1},{2,10},{10... | collective-permute-start | bytes 417800 | tf_op jit(solution)/shard_map/ppermute | solution.py:601
  10.4 13.5 %collective-permute-start.2 = (bf16[544,128]{1,0:T(8,128)(2,1)S(1)}, bf16[544,128]{1,0:T(8,128)(2,1)S(1)}, u32[]{:S(2)}, u32[]{:S(2)}) collective-permute-start(bf16[544,128]{1,0:T(8,128)(2,1)S(1)} %get-tuple-element.59), channel_id=1, source_target_pairs={{0,16},{8,24},{16,0},{24,8},{1,17},{9,25},{17,1},{25,9},{2,18},{10... | collective-permute-start | bytes 417800 | tf_op jit(solution)/shard_map/ppermute | solution.py:601
  11.5 12.4 %collective-permute-start.3 = (bf16[544,128]{1,0:T(8,128)(2,1)S(1)}, bf16[544,128]{1,0:T(8,128)(2,1)S(1)}, u32[]{:S(2)}, u32[]{:S(2)}) collective-permute-start(bf16[544,128]{1,0:T(8,128)(2,1)S(1)} %get-tuple-element.60), channel_id=1, source_target_pairs={{0,24},{8,0},{16,8},{24,16},{1,25},{9,1},{17,9},{25,17},{2,26},{10... | collective-permute-start | bytes 417800 | tf_op jit(solution)/shard_map/ppermute | solution.py:601
  23.9 2.5 %slice-start = ((s8[5898240]{0:T(1024)(128)(4,1)}), s8[1703936]{0:T(1024)(128)(4,1)S(1)}, s32[]{:S(2)}) async-start(s8[5898240]{0:T(1024)(128)(4,1)} %bitcast.2), calls=%async_computation | async-start | bytes 3407872
  23.9 2.5 %collective-permute-start.5 = (bf16[4,224,128]{2,1,0:T(8,128)(2,1)S(1)}, bf16[4,224,128]{2,1,0:T(8,128)(2,1)S(1)}, u32[]{:S(2)}, u32[]{:S(2)}) collective-permute-start(bf16[4,224,128]{2,1,0:T(8,128)(2,1)S(1)} %get-tuple-element.68.kb_ref), channel_id=1, source_target_pairs={{0,1},{1,0},{2,3},{3,2},{4,5},{5,4},{6,7},{7,6},{8,9},{9,8},{10,11... | collective-permute-start | bytes 688136 | tf_op jit(solution)/shard_map/ppermute | solution.py:643
  24.0 2.6 %slice-start.1 = ((s8[5898240]{0:T(1024)(128)(4,1)}), s8[4194304]{0:T(1024)(128)(4,1)S(1)}, s32[]{:S(2)}) async-start(s8[5898240]{0:T(1024)(128)(4,1)} %bitcast.2), calls=%async_computation.1 | async-start | bytes 8388608
  24.0 2.6 %copy-start.1 = (bf16[5,144,256]{2,1,0:T(8,128)(2,1)S(1)}, bf16[5,144,256]{2,1,0:T(8,128)(2,1)}, u32[]{:S(2)}) copy-start(bf16[5,144,256]{2,1,0:T(8,128)(2,1)} %get-tuple-element.71.vdh_ref) | copy-start | bytes 1105924
  25.9 7.1 %collective-permute-start.4 = (f32[2,16,64,128]{3,2,1,0:T(8,128)S(1)}, f32[2,16,64,128]{3,2,1,0:T(8,128)S(1)}, u32[]{:S(2)}, u32[]{:S(2)}) collective-permute-start(f32[2,16,64,128]{3,2,1,0:T(8,128)S(1)} %get-tuple-element.67.mine_b), channel_id=1, source_target_pairs={{0,1},{1,0},{2,3},{3,2},{4,5},{5,4},{6,7},{7,6},{8,9},{9,8},{10,11... | collective-permute-start | bytes 3145736 | tf_op jit(solution)/shard_map/ppermute | solution.py:651
  31.5 1.4 %collective-permute-start.6 = (f32[16,16,128]{2,1,0:T(8,128)S(1)}, f32[16,16,128]{2,1,0:T(8,128)S(1)}, u32[]{:S(2)}, u32[]{:S(2)}) collective-permute-start(f32[16,16,128]{2,1,0:T(8,128)S(1)} %get-tuple-element.73), channel_id=1, source_target_pairs={{0,1},{1,0},{2,3},{3,2},{4,5},{5,4},{6,7},{7,6},{8,9},{9,8},{10,11... | collective-permute-start | bytes 393224 | tf_op jit(solution)/shard_map/ppermute | solution.py:661
  33.0 10.3 %collective-permute-start.7 = (bf16[320,128]{1,0:T(8,128)(2,1)S(1)}, bf16[320,128]{1,0:T(8,128)(2,1)S(1)}, u32[]{:S(2)}, u32[]{:S(2)}) collective-permute-start(bf16[320,128]{1,0:T(8,128)(2,1)S(1)} %get-tuple-element.75), channel_id=1, source_target_pairs={{0,2},{1,3},{2,0},{3,1},{4,6},{5,7},{6,4},{7,5},{8,10},{9,11},{10,... | collective-permute-start | bytes 245768 | tf_op jit(solution)/shard_map/ppermute | solution.py:568
  34.5 8.7 %collective-permute-start.8 = (bf16[320,128]{1,0:T(8,128)(2,1)S(1)}, bf16[320,128]{1,0:T(8,128)(2,1)S(1)}, u32[]{:S(2)}, u32[]{:S(2)}) collective-permute-start(bf16[320,128]{1,0:T(8,128)(2,1)S(1)} %get-tuple-element.76), channel_id=1, source_target_pairs={{0,4},{1,5},{2,6},{3,7},{4,0},{5,1},{6,2},{7,3},{8,12},{9,13},{10,... | collective-permute-start | bytes 245768 | tf_op jit(solution)/shard_map/ppermute | solution.py:568
  36.1 7.2 %collective-permute-start.9 = (bf16[320,128]{1,0:T(8,128)(2,1)S(1)}, bf16[320,128]{1,0:T(8,128)(2,1)S(1)}, u32[]{:S(2)}, u32[]{:S(2)}) collective-permute-start(bf16[320,128]{1,0:T(8,128)(2,1)S(1)} %get-tuple-element.77), channel_id=1, source_target_pairs={{0,6},{1,7},{2,4},{3,5},{4,2},{5,3},{6,0},{7,1},{8,14},{9,15},{10,... | collective-permute-start | bytes 245768 | tf_op jit(solution)/shard_map/ppermute | solution.py:568
  38.5 8.8 %collective-permute-start.13 = (bf16[320,128]{1,0:T(8,128)(2,1)S(1)}, bf16[320,128]{1,0:T(8,128)(2,1)S(1)}, u32[]{:S(2)}, u32[]{:S(2)}) collective-permute-start(bf16[320,128]{1,0:T(8,128)(2,1)S(1)} %get-tuple-element.88), channel_id=1, source_target_pairs={{0,8},{8,16},{16,24},{24,0},{1,9},{9,17},{17,25},{25,1},{2,10},{10... | collective-permute-start | bytes 245768 | tf_op jit(solution)/shard_map/ppermute | solution.py:565
  40.4 8.9 %collective-permute-start.14 = (bf16[320,128]{1,0:T(8,128)(2,1)S(1)}, bf16[320,128]{1,0:T(8,128)(2,1)S(1)}, u32[]{:S(2)}, u32[]{:S(2)}) collective-permute-start(bf16[320,128]{1,0:T(8,128)(2,1)S(1)} %get-tuple-element.89), channel_id=1, source_target_pairs={{0,24},{8,0},{16,8},{24,16},{1,25},{9,1},{17,9},{25,17},{2,26},{10... | collective-permute-start | bytes 245768 | tf_op jit(solution)/shard_map/ppermute | solution.py:565
  43.4 5.9 %collective-permute-start.10 = (bf16[128,128]{1,0:T(8,128)(2,1)S(1)}, bf16[128,128]{1,0:T(8,128)(2,1)S(1)}, u32[]{:S(2)}, u32[]{:S(2)}) collective-permute-start(bf16[128,128]{1,0:T(8,128)(2,1)S(1)} %get-tuple-element.84), channel_id=1, source_target_pairs={{0,8},{8,16},{16,24},{24,0},{1,9},{9,17},{17,25},{25,1},{2,10},{10... | collective-permute-start | bytes 98312 | tf_op jit(solution)/shard_map/ppermute | solution.py:565
  43.4 6.7 %collective-permute-start.11 = (bf16[128,128]{1,0:T(8,128)(2,1)S(1)}, bf16[128,128]{1,0:T(8,128)(2,1)S(1)}, u32[]{:S(2)}, u32[]{:S(2)}) collective-permute-start(bf16[128,128]{1,0:T(8,128)(2,1)S(1)} %get-tuple-element.85), channel_id=1, source_target_pairs={{0,16},{8,24},{16,0},{24,8},{1,17},{9,25},{17,1},{25,9},{2,18},{10... | collective-permute-start | bytes 98312 | tf_op jit(solution)/shard_map/ppermute | solution.py:565
  46.8 4.0 %collective-permute-start.12 = (bf16[128,128]{1,0:T(8,128)(2,1)S(1)}, bf16[128,128]{1,0:T(8,128)(2,1)S(1)}, u32[]{:S(2)}, u32[]{:S(2)}) collective-permute-start(bf16[128,128]{1,0:T(8,128)(2,1)S(1)} %get-tuple-element.86), channel_id=1, source_target_pairs={{0,24},{8,0},{16,8},{24,16},{1,25},{9,1},{17,9},{25,17},{2,26},{10... | collective-permute-start | bytes 98312 | tf_op jit(solution)/shard_map/ppermute | solution.py:565
  47.2 7.1 %collective-permute-start.15 = (bf16[320,128]{1,0:T(8,128)(2,1)S(1)}, bf16[320,128]{1,0:T(8,128)(2,1)S(1)}, u32[]{:S(2)}, u32[]{:S(2)}) collective-permute-start(bf16[320,128]{1,0:T(8,128)(2,1)S(1)} %get-tuple-element.92), channel_id=1, source_target_pairs={{0,16},{8,24},{16,0},{24,8},{1,17},{9,25},{17,1},{25,9},{2,18},{10... | collective-permute-start | bytes 245768 | tf_op jit(solution)/shard_map/ppermute | solution.py:565
  50.8 5.3 %collective-permute-start.18 = (bf16[128,128]{1,0:T(8,128)(2,1)S(1)}, bf16[128,128]{1,0:T(8,128)(2,1)S(1)}, u32[]{:S(2)}, u32[]{:S(2)}) collective-permute-start(bf16[128,128]{1,0:T(8,128)(2,1)S(1)} %shard_map.78.refs_0_), channel_id=1, source_target_pairs={{0,6},{1,7},{2,4},{3,5},{4,2},{5,3},{6,0},{7,1},{8,14},{9,15},{10,... | collective-permute-start | bytes 98312 | tf_op jit(solution)/shard_map/ppermute | solution.py:568
  52.4 3.9 %collective-permute-start.17 = (bf16[128,128]{1,0:T(8,128)(2,1)S(1)}, bf16[128,128]{1,0:T(8,128)(2,1)S(1)}, u32[]{:S(2)}, u32[]{:S(2)}) collective-permute-start(bf16[128,128]{1,0:T(8,128)(2,1)S(1)} %shard_map.78.refs_0_), channel_id=1, source_target_pairs={{0,4},{1,5},{2,6},{3,7},{4,0},{5,1},{6,2},{7,3},{8,12},{9,13},{10,... | collective-permute-start | bytes 98312 | tf_op jit(solution)/shard_map/ppermute | solution.py:568
  52.9 3.9 %collective-permute-start.16 = (bf16[128,128]{1,0:T(8,128)(2,1)S(1)}, bf16[128,128]{1,0:T(8,128)(2,1)S(1)}, u32[]{:S(2)}, u32[]{:S(2)}) collective-permute-start(bf16[128,128]{1,0:T(8,128)(2,1)S(1)} %shard_map.78.refs_0_), channel_id=1, source_target_pairs={{0,2},{1,3},{2,0},{3,1},{4,6},{5,7},{6,4},{7,5},{8,10},{9,11},{10,... | collective-permute-start | bytes 98312 | tf_op jit(solution)/shard_map/ppermute | solution.py:568
  56.9 1.2 %collective-permute-start.19 = (bf16[128,128]{1,0:T(8,128)(2,1)S(1)}, bf16[128,128]{1,0:T(8,128)(2,1)S(1)}, u32[]{:S(2)}, u32[]{:S(2)}) collective-permute-start(bf16[128,128]{1,0:T(8,128)(2,1)S(1)} %shard_map.78.refs_0_), channel_id=1, source_target_pairs={{0,1},{1,0},{2,3},{3,2},{4,5},{5,4},{6,7},{7,6},{8,9},{9,8},{10,11... | collective-permute-start | bytes 98312 | tf_op jit(solution)/shard_map/ppermute | solution.py:715
  56.9 1.4 %collective-permute-start.20 = (bf16[128,128]{1,0:T(8,128)(2,1)S(1)}, bf16[128,128]{1,0:T(8,128)(2,1)S(1)}, u32[]{:S(2)}, u32[]{:S(2)}) collective-permute-start(bf16[128,128]{1,0:T(8,128)(2,1)S(1)} %collective-permute-done.16.refs_1_), channel_id=1, source_target_pairs={{0,1},{1,0},{2,3},{3,2},{4,5},{5,4},{6,7},{7,6},{8,9},{9,8},{10,11... | collective-permute-start | bytes 98312 | tf_op jit(solution)/shard_map/ppermute | solution.py:715
  57.4 1.2 %collective-permute-start.21 = (bf16[128,128]{1,0:T(8,128)(2,1)S(1)}, bf16[128,128]{1,0:T(8,128)(2,1)S(1)}, u32[]{:S(2)}, u32[]{:S(2)}) collective-permute-start(bf16[128,128]{1,0:T(8,128)(2,1)S(1)} %collective-permute-done.17.refs_2_), channel_id=1, source_target_pairs={{0,1},{1,0},{2,3},{3,2},{4,5},{5,4},{6,7},{7,6},{8,9},{9,8},{10,11... | collective-permute-start | bytes 98312 | tf_op jit(solution)/shard_map/ppermute | solution.py:715
  57.4 1.4 %collective-permute-start.22 = (bf16[128,128]{1,0:T(8,128)(2,1)S(1)}, bf16[128,128]{1,0:T(8,128)(2,1)S(1)}, u32[]{:S(2)}, u32[]{:S(2)}) collective-permute-start(bf16[128,128]{1,0:T(8,128)(2,1)S(1)} %collective-permute-done.18.refs_3_), channel_id=1, source_target_pairs={{0,1},{1,0},{2,3},{3,2},{4,5},{5,4},{6,7},{7,6},{8,9},{9,8},{10,11... | collective-permute-start | bytes 98312 | tf_op jit(solution)/shard_map/ppermute | solution.py:715

commit v6 on v4

--- a/solution.py
+++ b/solution.py
@@ -680,8 +680,7 @@
             ],
         )(kb, kb_other, hidden, h0)
     )
-    for d in range(1, n):
-        pieces[d] = along_mp(pieces[d], d)
+    pieces[1] = along_mp(pieces[1], 1)
 
     size = chan_b * taps + 16 * chunks
     sums = list(
@@ -693,10 +692,12 @@
             [pltpu.VMEM((n, size, 128), BF)],
         )(*sums)
     )
+    both = lax.optimization_barrier((*sums, *pieces[2:]))
+    sums, later = list(both[:n]), both[n:]
     for d in range(1, n):
         sums[d] = along_mp(sums[d], d)
-    both = lax.optimization_barrier((*sums, *pieces))
-    sums, pieces = both[:n], both[n:]
+    *sums, own, after = lax.optimization_barrier((*sums, *pieces[:2]))
+    pieces = [own, after] + [along_mp(x, d) for d, x in enumerate(later, 2)]
 
     samples = volume.shape[0] * dp
     scale_a = 1 / math.sqrt(samples * (GRID // 2) ** 3)

time: 62.6 us -> 60.2 us (0.962)
  waiting for transfers between devices: 7.95 us -> 3.74 us
  starting transfers between devices: 29.4 us -> 31.2 us
    ppermute x6, waiting for transfers between devices: 4.26 us -> 0.02 us  [along_mp(): return lax.ppermute(x, 'mp', [(i, (i + d) % n) for i in range(n)])]
    ppermute x6, starting transfers between devices: 9.8 us -> 11.6 us  [along_mp(): return lax.ppermute(x, 'mp', [(i, (i + d) % n) for i in range(n)])]
  transfers between devices with their start and end apart: 23 -> 23, of which waited for: 10 -> 7; matrix products, arithmetic and copies ran while one was open for 0% -> 0% of each run, Pallas kernels for 35% -> 37%
where the time goes in v6:
time: 60.2 us; the launch traced here: 60 us
  starting transfers between devices  31.2 us (52%)
  Pallas kernels  24 us (40%)
  waiting for transfers between devices  3.74 us (6%)
  between operations  0.81 us (1%)
    ppermute x6, starting transfers between devices, along_mp(): return lax.ppermute(x, 'mp', [(i, (i + d) % n) for i in range(n)])  11.6 us
    pallas_call x1, Pallas kernels, shards(): pl.pallas_call(first_kernel, out_shape=(pltpu.HBM((planes, 5, 144, 256),...  8.46 us
    ppermute x6, starting transfers between devices, along_dp(): return lax.ppermute(x, 'dp', [(i, i ^ 2 * m) for i in range(dp)])  7.11 us
    ppermute x3, starting transfers between devices, shards(): lax.ppermute(parts[d], 'mp', [(i, (i + d) % n) for i in range(n)])  5.55 us
    ppermute x1, starting transfers between devices, shards(): halo = lax.ppermute(halo, 'mp', up)  5.08 us
    pallas_call x1, Pallas kernels, shards(): call(functools.partial(grad_a_kernel, n), (pltpu.VMEM((columns * chunks,...  4.87 us
    pallas_call x1, Pallas kernels, shards(): pl.pallas_call(functools.partial(pack_kernel, n), grid=(1,), out_shape=[p...  2.05 us
    pallas_call x1, Pallas kernels, shards(): call(functools.partial(features_kernel, n), [pltpu.VMEM(((slab + 1) * row...  1.92 us
  transfers between devices with their start and end apart: 23, of which 7 were waited for; matrix products, arithmetic and copies ran while one was open for 0% of the time, Pallas kernels for 37%

profile of v6, /device:TPU:0, one launch (start us, length us, event | category | flops | bytes accessed | tf_op | source)
XLA Modules:
  0.0 60.0 jit_solution(2802739451798993886)
XLA Ops:
  0.6 1.0 %shard_map.68.after_ref = bf16[64,2048]{1,0:T(8,128)(2,1)S(1)} custom-call(bf16[1,16,64,2048]{3,2,1,0:T(8,128)(2,1)} %vol_ref.3), custom_call_target="tpu_custom_call" | custom-call | flops 1000000000 | bytes 3000000 | tf_op jit(solution)/shard_map/pallas_call | solution.py:574
  1.6 0.0 copy-start
  1.6 5.1 %collective-permute-start = (bf16[64,2048]{1,0:T(8,128)(2,1)S(1)}, bf16[64,2048]{1,0:T(8,128)(2,1)S(1)}, u32[]{:S(2)}, u32[]{:S(2)}) collective-permute-start(bf16[64,2048]{1,0:T(8,128)(2,1)S(1)} %shard_map.68.after_ref), channel_id=1, source_target_pairs={{0,8},{8,16},{16,24},{1,9},{9,17},{17,25},{2,10},{10,18},{18,26},{... | collective-permute-start | bytes 786440 | tf_op jit(solution)/shard_map/ppermute | solution.py:599
  6.7 2.0 %shard_map.70 = (bf16[544,128]{1,0:T(8,128)(2,1)S(1)}, bf16[544,128]{1,0:T(8,128)(2,1)S(1)}, bf16[544,128]{1,0:T(8,128)(2,1)S(1)}, bf16[544,128]{1,0:T(8,128)(2,1)S(1)}) custom-call(bf16[1,16,16,16,32]{4,3,2,1,0:T(8,128)(2,1)} %cot_ref.1, bf16[27,16,128]{2,1,0:T(8,128)(2,1)} %bitcast.4, bf16[64,2048]{1,0:T(8,128)(2,1)S(1)} %shard_map.68.after_ref), custom_call_target="tpu_custom_call" | custom-call | flops 2000000000 | bytes 6000000 | tf_op jit(solution)/shard_map/pallas_call | solution.py:584
  8.7 1.6 %collective-permute-start.1 = (bf16[544,128]{1,0:T(8,128)(2,1)S(1)}, bf16[544,128]{1,0:T(8,128)(2,1)S(1)}, u32[]{:S(2)}, u32[]{:S(2)}) collective-permute-start(bf16[544,128]{1,0:T(8,128)(2,1)S(1)} %get-tuple-element.58), channel_id=1, source_target_pairs={{0,8},{8,16},{16,24},{24,0},{1,9},{9,17},{17,25},{25,1},{2,10},{10... | collective-permute-start | bytes 417800 | tf_op jit(solution)/shard_map/ppermute | solution.py:601
  10.4 1.1 %collective-permute-start.2 = (bf16[544,128]{1,0:T(8,128)(2,1)S(1)}, bf16[544,128]{1,0:T(8,128)(2,1)S(1)}, u32[]{:S(2)}, u32[]{:S(2)}) collective-permute-start(bf16[544,128]{1,0:T(8,128)(2,1)S(1)} %get-tuple-element.59), channel_id=1, source_target_pairs={{0,16},{8,24},{16,0},{24,8},{1,17},{9,25},{17,1},{25,9},{2,18},{10... | collective-permute-start | bytes 417800 | tf_op jit(solution)/shard_map/ppermute | solution.py:601
  11.5 2.8 %collective-permute-start.3 = (bf16[544,128]{1,0:T(8,128)(2,1)S(1)}, bf16[544,128]{1,0:T(8,128)(2,1)S(1)}, u32[]{:S(2)}, u32[]{:S(2)}) collective-permute-start(bf16[544,128]{1,0:T(8,128)(2,1)S(1)} %get-tuple-element.60), channel_id=1, source_target_pairs={{0,24},{8,0},{16,8},{24,16},{1,25},{9,1},{17,9},{25,17},{2,26},{10... | collective-permute-start | bytes 417800 | tf_op jit(solution)/shard_map/ppermute | solution.py:601
  14.3 8.5 %shard_map.67 = (bf16[16,5,144,256]{3,2,1,0:T(8,128)(2,1)}, bf16[8,3,144,256]{3,2,1,0:T(8,128)(2,1)S(1)}, f32[256,256]{1,0:T(8,128)S(1)}) custom-call(bf16[1,16,64,2048]{3,2,1,0:T(8,128)(2,1)} %vol_ref.3, bf16[3,3,3,32,64]{4,3,2,1,0:T(8,128)(2,1)S(1)} %copy-done), custom_call_target="tpu_custom_call" | custom-call | flops 99999997952 | bytes 300000000 | tf_op jit(solution)/shard_map/pallas_call | solution.py:603
  22.8 0.0 collective-permute-done.halo_ref
  22.8 1.1 %shard_map.69 = (bf16[5,144,256]{2,1,0:T(8,128)(2,1)}, bf16[3,144,256]{2,1,0:T(8,128)(2,1)S(1)}) custom-call(bf16[64,2048]{1,0:T(8,128)(2,1)S(1)} %collective-permute-done.halo_ref, bf16[3,3,3,32,64]{4,3,2,1,0:T(8,128)(2,1)S(1)} %copy-done, f32[256,256]{1,0:T(8,128)S(1)} %get-tuple-element.55.pre_ref), custom_call_target="tpu_custom_call" | custom-call | flops 10000000000 | bytes 30000000 | tf_op jit(solution)/shard_map/pallas_call | solution.py:623
  23.8 0.0 collective-permute-done.1.refs_1_
  23.9 0.0 collective-permute-done.2.refs_2_
  23.9 0.0 collective-permute-done.3.refs_3_
  23.9 0.0 slice-start
  23.9 0.1 shard_map.71
  23.9 0.1 collective-permute-start.5
  24.0 0.0 slice-start.1
  24.0 0.0 copy-start.1
  24.0 1.8 %shard_map.72 = (bf16[5,2,144,256]{3,2,1,0:T(8,128)(2,1)S(1)}, f32[2,16,64,128]{3,2,1,0:T(8,128)S(1)}) custom-call(bf16[8,3,144,256]{3,2,1,0:T(8,128)(2,1)S(1)} %get-tuple-element.54.h_ref, bf16[3,144,256]{2,1,0:T(8,128)(2,1)S(1)} %get-tuple-element.61.h0_ref, bf16[4,320,128]{2,1,0:T(8,128)(2,1)S(1)} %get-tuple-element.66.cot_ref), custom_call_target="tpu_custom_call" | custom-call | flops 3000000000 | bytes 9000000 | tf_op jit(solution)/shard_map/pallas_call | solution.py:645
  25.9 0.5 collective-permute-start.4
  26.4 0.0 collective-permute-done.5.other_ref
  26.4 0.2 slice-done.1
  26.6 0.0 copy-done.1
  26.6 4.9 %shard_map.73 = (f32[16,16,128]{2,1,0:T(8,128)S(1)}, f32[16,16,128]{2,1,0:T(8,128)S(1)}) custom-call(bf16[4,224,128]{2,1,0:T(8,128)(2,1)S(1)} %get-tuple-element.68.kb_ref, bf16[4,224,128]{2,1,0:T(8,128)(2,1)S(1)} %collective-permute-done.5.other_ref, bf16[8,3,144,256]{3,2,1,0:T(8,128)(2,1)S(1)} %get-tuple-element.54.h_ref, ...), custom_call_target="tpu_custom_call" | custom-call | flops 8000000000 | bytes 24000000 | tf_op jit(solution)/shard_map/pallas_call | solution.py:653
  31.5 0.2 collective-permute-start.6
  31.7 1.2 %collective-permute-done.6.got_a = f32[16,16,128]{2,1,0:T(8,128)S(1)} collective-permute-done((f32[16,16,128]{2,1,0:T(8,128)S(1)}, f32[16,16,128]{2,1,0:T(8,128)S(1)}, u32[]{:S(2)}, u32[]{:S(2)}) %collective-permute-start.6) | collective-permute-done | bytes 131104 | tf_op jit(solution)/shard_map/ppermute | solution.py:661
  32.9 0.0 collective-permute-done.4.got_b
  32.9 0.1 shard_map.74
  33.0 1.5 %collective-permute-start.7 = (bf16[320,128]{1,0:T(8,128)(2,1)S(1)}, bf16[320,128]{1,0:T(8,128)(2,1)S(1)}, u32[]{:S(2)}, u32[]{:S(2)}) collective-permute-start(bf16[320,128]{1,0:T(8,128)(2,1)S(1)} %get-tuple-element.75), channel_id=1, source_target_pairs={{0,2},{1,3},{2,0},{3,1},{4,6},{5,7},{6,4},{7,5},{8,10},{9,11},{10,... | collective-permute-start | bytes 245768 | tf_op jit(solution)/shard_map/ppermute | solution.py:568
  34.5 1.5 %collective-permute-start.8 = (bf16[320,128]{1,0:T(8,128)(2,1)S(1)}, bf16[320,128]{1,0:T(8,128)(2,1)S(1)}, u32[]{:S(2)}, u32[]{:S(2)}) collective-permute-start(bf16[320,128]{1,0:T(8,128)(2,1)S(1)} %get-tuple-element.76), channel_id=1, source_target_pairs={{0,4},{1,5},{2,6},{3,7},{4,0},{5,1},{6,2},{7,3},{8,12},{9,13},{10,... | collective-permute-start | bytes 245768 | tf_op jit(solution)/shard_map/ppermute | solution.py:568
  36.1 0.5 collective-permute-start.9
  36.5 1.9 %shard_map.76 = (bf16[320,128]{1,0:T(8,128)(2,1)S(1)}, bf16[320,128]{1,0:T(8,128)(2,1)S(1)}, bf16[320,128]{1,0:T(8,128)(2,1)S(1)}, bf16[320,128]{1,0:T(8,128)(2,1)S(1)}) custom-call(bf16[4,224,128]{2,1,0:T(8,128)(2,1)S(1)} %get-tuple-element.68.kb_ref, bf16[4,224,128]{2,1,0:T(8,128)(2,1)S(1)} %collective-permute-done.5.other_ref, ...), custom_call_target="tpu_custom_call" | custom-call | flops 4000000000 | bytes 12000000 | tf_op jit(solution)/shard_map/pallas_call | solution.py:672
  38.5 1.9 %collective-permute-start.13 = (bf16[320,128]{1,0:T(8,128)(2,1)S(1)}, bf16[320,128]{1,0:T(8,128)(2,1)S(1)}, u32[]{:S(2)}, u32[]{:S(2)}) collective-permute-start(bf16[320,128]{1,0:T(8,128)(2,1)S(1)} %get-tuple-element.89), channel_id=1, source_target_pairs={{0,8},{8,16},{16,24},{24,0},{1,9},{9,17},{17,25},{25,1},{2,10},{10... | collective-permute-start | bytes 245768 | tf_op jit(solution)/shard_map/ppermute | solution.py:565
  40.4 0.0 collective-permute-done.7.refs_1_
  40.4 0.0 collective-permute-done.8.refs_2_
  40.4 1.0 %collective-permute-done.9.refs_3_ = bf16[320,128]{1,0:T(8,128)(2,1)S(1)} collective-permute-done((bf16[320,128]{1,0:T(8,128)(2,1)S(1)}, bf16[320,128]{1,0:T(8,128)(2,1)S(1)}, u32[]{:S(2)}, u32[]{:S(2)}) %collective-permute-start.9) | collective-permute-done | bytes 81952 | tf_op jit(solution)/shard_map/ppermute | solution.py:568
  41.4 0.1 shard_map.75
  41.5 1.9 %collective-permute-start.10 = (bf16[128,128]{1,0:T(8,128)(2,1)S(1)}, bf16[128,128]{1,0:T(8,128)(2,1)S(1)}, u32[]{:S(2)}, u32[]{:S(2)}) collective-permute-start(bf16[128,128]{1,0:T(8,128)(2,1)S(1)} %get-tuple-element.85), channel_id=1, source_target_pairs={{0,8},{8,16},{16,24},{24,0},{1,9},{9,17},{17,25},{25,1},{2,10},{10... | collective-permute-start | bytes 98312 | tf_op jit(solution)/shard_map/ppermute | solution.py:565
  43.4 3.4 %collective-permute-start.11 = (bf16[128,128]{1,0:T(8,128)(2,1)S(1)}, bf16[128,128]{1,0:T(8,128)(2,1)S(1)}, u32[]{:S(2)}, u32[]{:S(2)}) collective-permute-start(bf16[128,128]{1,0:T(8,128)(2,1)S(1)} %get-tuple-element.86), channel_id=1, source_target_pairs={{0,16},{8,24},{16,0},{24,8},{1,17},{9,25},{17,1},{25,9},{2,18},{10... | collective-permute-start | bytes 98312 | tf_op jit(solution)/shard_map/ppermute | solution.py:565
  46.8 0.1 collective-permute-start.12
  46.8 1.5 %collective-permute-start.14 = (bf16[320,128]{1,0:T(8,128)(2,1)S(1)}, bf16[320,128]{1,0:T(8,128)(2,1)S(1)}, u32[]{:S(2)}, u32[]{:S(2)}) collective-permute-start(bf16[320,128]{1,0:T(8,128)(2,1)S(1)} %get-tuple-element.92), channel_id=1, source_target_pairs={{0,16},{8,24},{16,0},{24,8},{1,17},{9,25},{17,1},{25,9},{2,18},{10... | collective-permute-start | bytes 245768 | tf_op jit(solution)/shard_map/ppermute | solution.py:565
  48.3 0.0 collective-permute-done.13.refs_1_
  48.3 2.8 %collective-permute-start.15 = (bf16[320,128]{1,0:T(8,128)(2,1)S(1)}, bf16[320,128]{1,0:T(8,128)(2,1)S(1)}, u32[]{:S(2)}, u32[]{:S(2)}) collective-permute-start(bf16[320,128]{1,0:T(8,128)(2,1)S(1)} %get-tuple-element.93), channel_id=1, source_target_pairs={{0,24},{8,0},{16,8},{24,16},{1,25},{9,1},{17,9},{25,17},{2,26},{10... | collective-permute-start | bytes 245768 | tf_op jit(solution)/shard_map/ppermute | solution.py:565
  51.2 0.0 collective-permute-done.10.refs_1_
  51.2 0.0 collective-permute-done.11.refs_2_
  51.2 0.0 collective-permute-done.12.refs_3_
  51.2 0.9 %collective-permute-start.18 = (bf16[128,128]{1,0:T(8,128)(2,1)S(1)}, bf16[128,128]{1,0:T(8,128)(2,1)S(1)}, u32[]{:S(2)}, u32[]{:S(2)}) collective-permute-start(bf16[128,128]{1,0:T(8,128)(2,1)S(1)} %shard_map.78.refs_0_), channel_id=1, source_target_pairs={{0,6},{1,7},{2,4},{3,5},{4,2},{5,3},{6,0},{7,1},{8,14},{9,15},{10,... | collective-permute-start | bytes 98312 | tf_op jit(solution)/shard_map/ppermute | solution.py:568
  52.1 1.2 %collective-permute-start.17 = (bf16[128,128]{1,0:T(8,128)(2,1)S(1)}, bf16[128,128]{1,0:T(8,128)(2,1)S(1)}, u32[]{:S(2)}, u32[]{:S(2)}) collective-permute-start(bf16[128,128]{1,0:T(8,128)(2,1)S(1)} %shard_map.78.refs_0_), channel_id=1, source_target_pairs={{0,4},{1,5},{2,6},{3,7},{4,0},{5,1},{6,2},{7,3},{8,12},{9,13},{10,... | collective-permute-start | bytes 98312 | tf_op jit(solution)/shard_map/ppermute | solution.py:568
  53.3 1.5 %collective-permute-start.16 = (bf16[128,128]{1,0:T(8,128)(2,1)S(1)}, bf16[128,128]{1,0:T(8,128)(2,1)S(1)}, u32[]{:S(2)}, u32[]{:S(2)}) collective-permute-start(bf16[128,128]{1,0:T(8,128)(2,1)S(1)} %shard_map.78.refs_0_), channel_id=1, source_target_pairs={{0,2},{1,3},{2,0},{3,1},{4,6},{5,7},{6,4},{7,5},{8,10},{9,11},{10,... | collective-permute-start | bytes 98312 | tf_op jit(solution)/shard_map/ppermute | solution.py:568
  54.8 0.0 collective-permute-done.14.refs_2_
  54.8 0.0 collective-permute-done.15.refs_3_
  54.8 1.8 %shard_map.77 = bf16[1,16,16,16,32]{4,3,2,1,0:T(8,128)(2,1)} custom-call(bf16[320,128]{1,0:T(8,128)(2,1)S(1)} %get-tuple-element.90.refs_0_, bf16[320,128]{1,0:T(8,128)(2,1)S(1)} %collective-permute-done.13.refs_1_, bf16[320,128]{1,0:T(8,128)(2,1)S(1)} %collective-permute-done.14.refs_2_, bf16[320,128]{1,0:T(8,128)(2,1)S(1)} %collective-permute-done.15.refs_3_), custom_call_target="tpu_custom_call" | custom-call | flops 2000000000 | bytes 6000000 | tf_op jit(solution)/shard_map/pallas_call | solution.py:709
  56.5 0.0 collective-permute-done.18.refs_3_
  56.5 0.0 collective-permute-done.17.refs_2_
  56.5 0.6 %collective-permute-done.16.refs_1_ = bf16[128,128]{1,0:T(8,128)(2,1)S(1)} collective-permute-done((bf16[128,128]{1,0:T(8,128)(2,1)S(1)}, bf16[128,128]{1,0:T(8,128)(2,1)S(1)}, u32[]{:S(2)}, u32[]{:S(2)}) %collective-permute-start.16) | collective-permute-done | bytes 32800 | tf_op jit(solution)/shard_map/ppermute | solution.py:568
  57.2 0.0 collective-permute-start.19
  57.2 0.5 collective-permute-start.20
  57.7 0.0 collective-permute-start.21
  57.7 0.5 collective-permute-start.22
  58.2 0.2 collective-permute-done.19.refs_4_
  58.4 0.2 collective-permute-done.20.refs_5_
  58.6 0.3 collective-permute-done.21.refs_6_
  58.9 0.2 collective-permute-done.22.refs_7_
  59.1 0.9 %shard_map.79 = (f32[3,3,3,32,64]{4,3,2,1,0:T(8,128)}, f32[27,16,128]{2,1,0:T(8,128)}) custom-call(bf16[128,128]{1,0:T(8,128)(2,1)S(1)} %shard_map.78.refs_0_, bf16[128,128]{1,0:T(8,128)(2,1)S(1)} %collective-permute-done.16.refs_1_, bf16[128,128]{1,0:T(8,128)(2,1)S(1)} %collective-permute-done.17.refs_2_, ...), custom_call_target="tpu_custom_call" | custom-call | flops 1000000000 | bytes 3000000 | tf_op jit(solution)/shard_map/pallas_call | solution.py:713
  (4 shorter events, 0.0 us)
Async XLA Ops:
  1.6 12.7 %copy-start = (bf16[3,3,3,32,64]{4,3,2,1,0:T(8,128)(2,1)S(1)}, bf16[3,3,3,32,64]{4,3,2,1,0:T(8,128)(2,1)}, u32[]{:S(2)}) copy-start(bf16[3,3,3,32,64]{4,3,2,1,0:T(8,128)(2,1)} %ka_ref.3) | copy-start | bytes 331780
  1.6 21.2 %collective-permute-start = (bf16[64,2048]{1,0:T(8,128)(2,1)S(1)}, bf16[64,2048]{1,0:T(8,128)(2,1)S(1)}, u32[]{:S(2)}, u32[]{:S(2)}) collective-permute-start(bf16[64,2048]{1,0:T(8,128)(2,1)S(1)} %shard_map.68.after_ref), channel_id=1, source_target_pairs={{0,8},{8,16},{16,24},{1,9},{9,17},{17,25},{2,10},{10,18},{18,26},{... | collective-permute-start | bytes 786440 | tf_op jit(solution)/shard_map/ppermute | solution.py:599
  8.7 15.1 %collective-permute-start.1 = (bf16[544,128]{1,0:T(8,128)(2,1)S(1)}, bf16[544,128]{1,0:T(8,128)(2,1)S(1)}, u32[]{:S(2)}, u32[]{:S(2)}) collective-permute-start(bf16[544,128]{1,0:T(8,128)(2,1)S(1)} %get-tuple-element.58), channel_id=1, source_target_pairs={{0,8},{8,16},{16,24},{24,0},{1,9},{9,17},{17,25},{25,1},{2,10},{10... | collective-permute-start | bytes 417800 | tf_op jit(solution)/shard_map/ppermute | solution.py:601
  10.4 13.5 %collective-permute-start.2 = (bf16[544,128]{1,0:T(8,128)(2,1)S(1)}, bf16[544,128]{1,0:T(8,128)(2,1)S(1)}, u32[]{:S(2)}, u32[]{:S(2)}) collective-permute-start(bf16[544,128]{1,0:T(8,128)(2,1)S(1)} %get-tuple-element.59), channel_id=1, source_target_pairs={{0,16},{8,24},{16,0},{24,8},{1,17},{9,25},{17,1},{25,9},{2,18},{10... | collective-permute-start | bytes 417800 | tf_op jit(solution)/shard_map/ppermute | solution.py:601
  11.5 12.4 %collective-permute-start.3 = (bf16[544,128]{1,0:T(8,128)(2,1)S(1)}, bf16[544,128]{1,0:T(8,128)(2,1)S(1)}, u32[]{:S(2)}, u32[]{:S(2)}) collective-permute-start(bf16[544,128]{1,0:T(8,128)(2,1)S(1)} %get-tuple-element.60), channel_id=1, source_target_pairs={{0,24},{8,0},{16,8},{24,16},{1,25},{9,1},{17,9},{25,17},{2,26},{10... | collective-permute-start | bytes 417800 | tf_op jit(solution)/shard_map/ppermute | solution.py:601
  23.9 2.5 %slice-start = ((s8[5898240]{0:T(1024)(128)(4,1)}), s8[1703936]{0:T(1024)(128)(4,1)S(1)}, s32[]{:S(2)}) async-start(s8[5898240]{0:T(1024)(128)(4,1)} %bitcast.2), calls=%async_computation | async-start | bytes 3407872
  23.9 2.5 %collective-permute-start.5 = (bf16[4,224,128]{2,1,0:T(8,128)(2,1)S(1)}, bf16[4,224,128]{2,1,0:T(8,128)(2,1)S(1)}, u32[]{:S(2)}, u32[]{:S(2)}) collective-permute-start(bf16[4,224,128]{2,1,0:T(8,128)(2,1)S(1)} %get-tuple-element.68.kb_ref), channel_id=1, source_target_pairs={{0,1},{1,0},{2,3},{3,2},{4,5},{5,4},{6,7},{7,6},{8,9},{9,8},{10,11... | collective-permute-start | bytes 688136 | tf_op jit(solution)/shard_map/ppermute | solution.py:643
  24.0 2.6 %slice-start.1 = ((s8[5898240]{0:T(1024)(128)(4,1)}), s8[4194304]{0:T(1024)(128)(4,1)S(1)}, s32[]{:S(2)}) async-start(s8[5898240]{0:T(1024)(128)(4,1)} %bitcast.2), calls=%async_computation.1 | async-start | bytes 8388608
  24.0 2.6 %copy-start.1 = (bf16[5,144,256]{2,1,0:T(8,128)(2,1)S(1)}, bf16[5,144,256]{2,1,0:T(8,128)(2,1)}, u32[]{:S(2)}) copy-start(bf16[5,144,256]{2,1,0:T(8,128)(2,1)} %get-tuple-element.71.vdh_ref) | copy-start | bytes 1105924
  25.9 7.1 %collective-permute-start.4 = (f32[2,16,64,128]{3,2,1,0:T(8,128)S(1)}, f32[2,16,64,128]{3,2,1,0:T(8,128)S(1)}, u32[]{:S(2)}, u32[]{:S(2)}) collective-permute-start(f32[2,16,64,128]{3,2,1,0:T(8,128)S(1)} %get-tuple-element.67.mine_b), channel_id=1, source_target_pairs={{0,1},{1,0},{2,3},{3,2},{4,5},{5,4},{6,7},{7,6},{8,9},{9,8},{10,11... | collective-permute-start | bytes 3145736 | tf_op jit(solution)/shard_map/ppermute | solution.py:651
  31.5 1.4 %collective-permute-start.6 = (f32[16,16,128]{2,1,0:T(8,128)S(1)}, f32[16,16,128]{2,1,0:T(8,128)S(1)}, u32[]{:S(2)}, u32[]{:S(2)}) collective-permute-start(f32[16,16,128]{2,1,0:T(8,128)S(1)} %get-tuple-element.73), channel_id=1, source_target_pairs={{0,1},{1,0},{2,3},{3,2},{4,5},{5,4},{6,7},{7,6},{8,9},{9,8},{10,11... | collective-permute-start | bytes 393224 | tf_op jit(solution)/shard_map/ppermute | solution.py:661
  33.0 7.4 %collective-permute-start.7 = (bf16[320,128]{1,0:T(8,128)(2,1)S(1)}, bf16[320,128]{1,0:T(8,128)(2,1)S(1)}, u32[]{:S(2)}, u32[]{:S(2)}) collective-permute-start(bf16[320,128]{1,0:T(8,128)(2,1)S(1)} %get-tuple-element.75), channel_id=1, source_target_pairs={{0,2},{1,3},{2,0},{3,1},{4,6},{5,7},{6,4},{7,5},{8,10},{9,11},{10,... | collective-permute-start | bytes 245768 | tf_op jit(solution)/shard_map/ppermute | solution.py:568
  34.5 5.9 %collective-permute-start.8 = (bf16[320,128]{1,0:T(8,128)(2,1)S(1)}, bf16[320,128]{1,0:T(8,128)(2,1)S(1)}, u32[]{:S(2)}, u32[]{:S(2)}) collective-permute-start(bf16[320,128]{1,0:T(8,128)(2,1)S(1)} %get-tuple-element.76), channel_id=1, source_target_pairs={{0,4},{1,5},{2,6},{3,7},{4,0},{5,1},{6,2},{7,3},{8,12},{9,13},{10,... | collective-permute-start | bytes 245768 | tf_op jit(solution)/shard_map/ppermute | solution.py:568
  36.1 5.3 %collective-permute-start.9 = (bf16[320,128]{1,0:T(8,128)(2,1)S(1)}, bf16[320,128]{1,0:T(8,128)(2,1)S(1)}, u32[]{:S(2)}, u32[]{:S(2)}) collective-permute-start(bf16[320,128]{1,0:T(8,128)(2,1)S(1)} %get-tuple-element.77), channel_id=1, source_target_pairs={{0,6},{1,7},{2,4},{3,5},{4,2},{5,3},{6,0},{7,1},{8,14},{9,15},{10,... | collective-permute-start | bytes 245768 | tf_op jit(solution)/shard_map/ppermute | solution.py:568
  38.5 9.8 %collective-permute-start.13 = (bf16[320,128]{1,0:T(8,128)(2,1)S(1)}, bf16[320,128]{1,0:T(8,128)(2,1)S(1)}, u32[]{:S(2)}, u32[]{:S(2)}) collective-permute-start(bf16[320,128]{1,0:T(8,128)(2,1)S(1)} %get-tuple-element.89), channel_id=1, source_target_pairs={{0,8},{8,16},{16,24},{24,0},{1,9},{9,17},{17,25},{25,1},{2,10},{10... | collective-permute-start | bytes 245768 | tf_op jit(solution)/shard_map/ppermute | solution.py:565
  41.5 9.7 %collective-permute-start.10 = (bf16[128,128]{1,0:T(8,128)(2,1)S(1)}, bf16[128,128]{1,0:T(8,128)(2,1)S(1)}, u32[]{:S(2)}, u32[]{:S(2)}) collective-permute-start(bf16[128,128]{1,0:T(8,128)(2,1)S(1)} %get-tuple-element.85), channel_id=1, source_target_pairs={{0,8},{8,16},{16,24},{24,0},{1,9},{9,17},{17,25},{25,1},{2,10},{10... | collective-permute-start | bytes 98312 | tf_op jit(solution)/shard_map/ppermute | solution.py:565
  43.4 7.8 %collective-permute-start.11 = (bf16[128,128]{1,0:T(8,128)(2,1)S(1)}, bf16[128,128]{1,0:T(8,128)(2,1)S(1)}, u32[]{:S(2)}, u32[]{:S(2)}) collective-permute-start(bf16[128,128]{1,0:T(8,128)(2,1)S(1)} %get-tuple-element.86), channel_id=1, source_target_pairs={{0,16},{8,24},{16,0},{24,8},{1,17},{9,25},{17,1},{25,9},{2,18},{10... | collective-permute-start | bytes 98312 | tf_op jit(solution)/shard_map/ppermute | solution.py:565
  46.8 4.4 %collective-permute-start.12 = (bf16[128,128]{1,0:T(8,128)(2,1)S(1)}, bf16[128,128]{1,0:T(8,128)(2,1)S(1)}, u32[]{:S(2)}, u32[]{:S(2)}) collective-permute-start(bf16[128,128]{1,0:T(8,128)(2,1)S(1)} %get-tuple-element.87), channel_id=1, source_target_pairs={{0,24},{8,0},{16,8},{24,16},{1,25},{9,1},{17,9},{25,17},{2,26},{10... | collective-permute-start | bytes 98312 | tf_op jit(solution)/shard_map/ppermute | solution.py:565
  46.8 7.9 %collective-permute-start.14 = (bf16[320,128]{1,0:T(8,128)(2,1)S(1)}, bf16[320,128]{1,0:T(8,128)(2,1)S(1)}, u32[]{:S(2)}, u32[]{:S(2)}) collective-permute-start(bf16[320,128]{1,0:T(8,128)(2,1)S(1)} %get-tuple-element.92), channel_id=1, source_target_pairs={{0,16},{8,24},{16,0},{24,8},{1,17},{9,25},{17,1},{25,9},{2,18},{10... | collective-permute-start | bytes 245768 | tf_op jit(solution)/shard_map/ppermute | solution.py:565
  48.3 6.5 %collective-permute-start.15 = (bf16[320,128]{1,0:T(8,128)(2,1)S(1)}, bf16[320,128]{1,0:T(8,128)(2,1)S(1)}, u32[]{:S(2)}, u32[]{:S(2)}) collective-permute-start(bf16[320,128]{1,0:T(8,128)(2,1)S(1)} %get-tuple-element.93), channel_id=1, source_target_pairs={{0,24},{8,0},{16,8},{24,16},{1,25},{9,1},{17,9},{25,17},{2,26},{10... | collective-permute-start | bytes 245768 | tf_op jit(solution)/shard_map/ppermute | solution.py:565
  51.2 5.3 %collective-permute-start.18 = (bf16[128,128]{1,0:T(8,128)(2,1)S(1)}, bf16[128,128]{1,0:T(8,128)(2,1)S(1)}, u32[]{:S(2)}, u32[]{:S(2)}) collective-permute-start(bf16[128,128]{1,0:T(8,128)(2,1)S(1)} %shard_map.78.refs_0_), channel_id=1, source_target_pairs={{0,6},{1,7},{2,4},{3,5},{4,2},{5,3},{6,0},{7,1},{8,14},{9,15},{10,... | collective-permute-start | bytes 98312 | tf_op jit(solution)/shard_map/ppermute | solution.py:568
  52.1 4.4 %collective-permute-start.17 = (bf16[128,128]{1,0:T(8,128)(2,1)S(1)}, bf16[128,128]{1,0:T(8,128)(2,1)S(1)}, u32[]{:S(2)}, u32[]{:S(2)}) collective-permute-start(bf16[128,128]{1,0:T(8,128)(2,1)S(1)} %shard_map.78.refs_0_), channel_id=1, source_target_pairs={{0,4},{1,5},{2,6},{3,7},{4,0},{5,1},{6,2},{7,3},{8,12},{9,13},{10,... | collective-permute-start | bytes 98312 | tf_op jit(solution)/shard_map/ppermute | solution.py:568
  53.3 3.9 %collective-permute-start.16 = (bf16[128,128]{1,0:T(8,128)(2,1)S(1)}, bf16[128,128]{1,0:T(8,128)(2,1)S(1)}, u32[]{:S(2)}, u32[]{:S(2)}) collective-permute-start(bf16[128,128]{1,0:T(8,128)(2,1)S(1)} %shard_map.78.refs_0_), channel_id=1, source_target_pairs={{0,2},{1,3},{2,0},{3,1},{4,6},{5,7},{6,4},{7,5},{8,10},{9,11},{10,... | collective-permute-start | bytes 98312 | tf_op jit(solution)/shard_map/ppermute | solution.py:568
  57.2 1.2 %collective-permute-start.19 = (bf16[128,128]{1,0:T(8,128)(2,1)S(1)}, bf16[128,128]{1,0:T(8,128)(2,1)S(1)}, u32[]{:S(2)}, u32[]{:S(2)}) collective-permute-start(bf16[128,128]{1,0:T(8,128)(2,1)S(1)} %shard_map.78.refs_0_), channel_id=1, source_target_pairs={{0,1},{1,0},{2,3},{3,2},{4,5},{5,4},{6,7},{7,6},{8,9},{9,8},{10,11... | collective-permute-start | bytes 98312 | tf_op jit(solution)/shard_map/ppermute | solution.py:712
  57.2 1.4 %collective-permute-start.20 = (bf16[128,128]{1,0:T(8,128)(2,1)S(1)}, bf16[128,128]{1,0:T(8,128)(2,1)S(1)}, u32[]{:S(2)}, u32[]{:S(2)}) collective-permute-start(bf16[128,128]{1,0:T(8,128)(2,1)S(1)} %collective-permute-done.16.refs_1_), channel_id=1, source_target_pairs={{0,1},{1,0},{2,3},{3,2},{4,5},{5,4},{6,7},{7,6},{8,9},{9,8},{10,11... | collective-permute-start | bytes 98312 | tf_op jit(solution)/shard_map/ppermute | solution.py:712
  57.7 1.2 %collective-permute-start.21 = (bf16[128,128]{1,0:T(8,128)(2,1)S(1)}, bf16[128,128]{1,0:T(8,128)(2,1)S(1)}, u32[]{:S(2)}, u32[]{:S(2)}) collective-permute-start(bf16[128,128]{1,0:T(8,128)(2,1)S(1)} %collective-permute-done.17.refs_2_), channel_id=1, source_target_pairs={{0,1},{1,0},{2,3},{3,2},{4,5},{5,4},{6,7},{7,6},{8,9},{9,8},{10,11... | collective-permute-start | bytes 98312 | tf_op jit(solution)/shard_map/ppermute | solution.py:712
  57.7 1.4 %collective-permute-start.22 = (bf16[128,128]{1,0:T(8,128)(2,1)S(1)}, bf16[128,128]{1,0:T(8,128)(2,1)S(1)}, u32[]{:S(2)}, u32[]{:S(2)}) collective-permute-start(bf16[128,128]{1,0:T(8,128)(2,1)S(1)} %collective-permute-done.18.refs_3_), channel_id=1, source_target_pairs={{0,1},{1,0},{2,3},{3,2},{4,5},{5,4},{6,7},{7,6},{8,9},{9,8},{10,11... | collective-permute-start | bytes 98312 | tf_op jit(solution)/shard_map/ppermute | solution.py:712
